TPU v7x, 256 devices: a whole 4x4x8 slice. The times are simulated.
256 devices in a mesh: section: 16 (over x_hi, y, core), dp: 16 (over z, x_lo).
Axes of the slice: x: 4 (x_hi: 2, x_lo: 2; x = x_hi * 2 + x_lo), y: 4, z: 8, core: 2. Of those that a mesh axis runs over, the one named last changes fastest.
Arguments:
- entering: bfloat16 [2, 4, 256, 8192], P(None, None, 'dp'), may hold values from -6 to 6
- cotangent: bfloat16 [2, 4, 256, 8192], P(None, None, 'dp'), may hold values from -6 to 6
- down_proj: bfloat16 [16, 8192, 256], P('section', 'dp'), may hold values from -0.0625 to 0.0625
- up_proj: bfloat16 [16, 256, 8192], P('section', None, 'dp'), may hold values from -0.375 to 0.375
Outputs:
- grad_down: float32 [16, 8192, 256], P('section', 'dp')
- grad_up: float32 [16, 256, 8192], P('section', None, 'dp')
All inputs are finite; a program needn't handle non-finite values.
Results may differ from a plain program's by a relative error of at most 0.035.
Values may be sent and summed in bfloat16 or wider, within the bound.
No kernel may reach another device: no remote copies, remote signals or barrier semaphores. Data moves between devices by JAX's collectives and lax.ppermute only.
A program may use at most 128 MiB of HBM per device.

v0:
```python
import math

import jax
import jax.numpy as jnp
from jax import lax
from jax.sharding import PartitionSpec as P

epsilon = 1e-05
root_half = 0.7071067811865476
inv_root_tau = 0.3989422804014327


def from_partner(value, axis, distance):
    mask = 2**distance
    pairs = [(source, source ^ mask) for source in range(lax.axis_size(axis))]
    return lax.ppermute(value, axis, pairs)


def passed_along(block, axis, distance):
    devices = range(lax.axis_size(axis))
    route = [(i - distance, i) for i in devices if i - distance in devices]
    return lax.ppermute(block, axis, route)


def gelu_value(values):
    return 0.5 * values * (1.0 + lax.erf(values * root_half))


def gelu_slope(values):
    return 0.5 * (1.0 + lax.erf(values * root_half)) + values * inv_root_tau * jnp.exp(
        -0.5 * values * values
    )


def unit_scale(hidden):
    widened = hidden.astype(jnp.float32)
    scaling = lax.rsqrt(jnp.mean(widened * widened, axis=-1, keepdims=True) + epsilon)
    return (widened, scaling)


def layer_forward(hidden, down_weight, up_weight):
    widened, scaling = unit_scale(hidden)
    normed = (widened * scaling).astype(jnp.bfloat16)
    latent = jnp.dot(normed, down_weight, preferred_element_type=jnp.float32)
    active = gelu_value(latent).astype(jnp.bfloat16)
    return (widened + jnp.dot(active, up_weight, preferred_element_type=jnp.float32)).astype(
        jnp.bfloat16
    )


def layer_backward(hidden, incoming, down_weight, up_weight):
    widened, scaling = unit_scale(hidden)
    unit_rows = widened * scaling
    normed = unit_rows.astype(jnp.bfloat16)
    latent = jnp.dot(normed, down_weight, preferred_element_type=jnp.float32)
    active = gelu_value(latent).astype(jnp.bfloat16)
    dactive = jnp.dot(incoming, up_weight.T, preferred_element_type=jnp.float32)
    dlatent = (dactive * gelu_slope(latent)).astype(jnp.bfloat16)
    unit_grad = jnp.dot(dlatent, down_weight.T, preferred_element_type=jnp.float32)
    inner = jnp.mean(unit_grad * unit_rows, axis=-1, keepdims=True)
    passed = (incoming.astype(jnp.float32) + scaling * (unit_grad - unit_rows * inner)).astype(
        jnp.bfloat16
    )
    return (dlatent, active, passed)


def packed_pair(first, second):
    return jnp.concatenate([first.reshape(-1), second.reshape(-1)])


def split_pair(packed, first_shape, second_shape):
    first_size = math.prod(first_shape)
    return (packed[:first_size].reshape(first_shape), packed[first_size:].reshape(second_shape))


def reverse_section(packed, section_count):
    shifted_copy = packed
    for bit_number in range(section_count.bit_length() - 1):
        shifted_copy = from_partner(
            shifted_copy.astype(jnp.bfloat16), "section", bit_number
        ).astype(shifted_copy.dtype)
    return shifted_copy


def body(entering, cotangent, down_proj, up_proj):
    section_count = lax.axis_size("section")
    position = lax.axis_index("section")
    mirror_position = section_count - 1 - position
    micro_count = entering.shape[1]
    row_count = entering.shape[2]
    feature_count = entering.shape[3]
    bottleneck = down_proj.shape[2]
    mirrored = reverse_section(packed_pair(down_proj, up_proj).astype(jnp.float32), section_count)
    mirror_down, mirror_up = split_pair(
        mirrored.astype(jnp.bfloat16), down_proj.shape, up_proj.shape
    )
    gathered = (
        lax.all_gather(down_proj, "dp", axis=1, tiled=True),
        lax.all_gather(up_proj, "dp", axis=2, tiled=True),
        lax.all_gather(mirror_down, "dp", axis=1, tiled=True),
        lax.all_gather(mirror_up, "dp", axis=2, tiled=True),
    )
    down_weight = gathered[0][0]
    up_weight = gathered[1][0]
    mirror_dw = gathered[2][0]
    mirror_uw = gathered[3][0]
    tick_count = micro_count + section_count - 1

    def select_slot(stack, index):
        return lax.dynamic_index_in_dim(
            stack, jnp.clip(index, 0, micro_count - 1).astype(jnp.int32), 0, keepdims=False
        )

    def inside(index):
        return (index >= 0) & (index < micro_count)

    def store_slot(stack, index, value):
        updated = lax.dynamic_update_index_in_dim(
            stack, value, jnp.clip(index, 0, micro_count - 1), 0
        )
        return jnp.where(inside(index), updated, stack)

    empty_rows = jnp.zeros((row_count, feature_count), jnp.bfloat16)
    empty_narrow = jnp.zeros((row_count, bottleneck), jnp.bfloat16)
    empty_store = jnp.zeros((micro_count, row_count, feature_count), jnp.bfloat16)
    empty_small = jnp.zeros((micro_count, row_count, bottleneck), jnp.bfloat16)

    def forward_tick(tick_index, loop_state):
        recv_down, recv_up, saved_down, saved_up = loop_state
        slot_down = tick_index - position
        slot_up = tick_index - mirror_position
        source_down = jnp.where(position == 0, select_slot(entering[0], tick_index), recv_down)
        source_up = jnp.where(
            position == section_count - 1, select_slot(entering[1], tick_index), recv_up
        )
        saved_down = store_slot(saved_down, slot_down, source_down)
        saved_up = store_slot(saved_up, slot_up, source_up)
        output_down = lax.cond(
            inside(slot_down),
            lambda: layer_forward(source_down, down_weight, up_weight),
            lambda: empty_rows,
        )
        output_up = lax.cond(
            inside(slot_up),
            lambda: layer_forward(source_up, mirror_dw, mirror_uw),
            lambda: empty_rows,
        )
        recv_down = passed_along(output_down, "section", 1)
        recv_up = passed_along(output_up, "section", -1)
        return (recv_down, recv_up, saved_down, saved_up)

    _, _, saved_down, saved_up = lax.fori_loop(
        0, tick_count, forward_tick, (empty_rows, empty_rows, empty_store, empty_store)
    )

    def backward_tick(tick_index, loop_state):
        recv_down, recv_up, inc_down, inc_up, lat_down, lat_up, act_down, act_up = loop_state
        slot_down = tick_index - mirror_position
        slot_up = tick_index - position
        incoming_down = jnp.where(
            position == section_count - 1, select_slot(cotangent[0], tick_index), recv_down
        )
        incoming_up = jnp.where(position == 0, select_slot(cotangent[1], tick_index), recv_up)
        hidden_down = select_slot(saved_down, slot_down)
        hidden_up = select_slot(saved_up, slot_up)
        dlat_down, active_down, passed_down = lax.cond(
            inside(slot_down),
            lambda: layer_backward(hidden_down, incoming_down, down_weight, up_weight),
            lambda: (empty_narrow, empty_narrow, empty_rows),
        )
        dlat_up, active_up, passed_up = lax.cond(
            inside(slot_up),
            lambda: layer_backward(hidden_up, incoming_up, mirror_dw, mirror_uw),
            lambda: (empty_narrow, empty_narrow, empty_rows),
        )
        inc_down = store_slot(inc_down, slot_down, incoming_down)
        inc_up = store_slot(inc_up, slot_up, incoming_up)
        lat_down = store_slot(lat_down, slot_down, dlat_down)
        lat_up = store_slot(lat_up, slot_up, dlat_up)
        act_down = store_slot(act_down, slot_down, active_down)
        act_up = store_slot(act_up, slot_up, active_up)
        recv_down = passed_along(passed_down, "section", -1)
        recv_up = passed_along(passed_up, "section", 1)
        return (recv_down, recv_up, inc_down, inc_up, lat_down, lat_up, act_down, act_up)

    final_state = lax.fori_loop(
        0,
        tick_count,
        backward_tick,
        (
            empty_rows,
            empty_rows,
            empty_store,
            empty_store,
            empty_small,
            empty_small,
            empty_small,
            empty_small,
        ),
    )
    _, _, inc_down, inc_up, lat_down, lat_up, act_down, act_up = final_state
    flat_rows = micro_count * row_count

    def normed_rows(saved):
        widened, scaling = unit_scale(saved.reshape(flat_rows, feature_count))
        return (widened * scaling).astype(jnp.bfloat16)

    groups = (
        (
            normed_rows(saved_down),
            inc_down.reshape(flat_rows, feature_count),
            lat_down.reshape(flat_rows, bottleneck),
            act_down.reshape(flat_rows, bottleneck),
        ),
        (
            normed_rows(saved_up),
            inc_up.reshape(flat_rows, feature_count),
            lat_up.reshape(flat_rows, bottleneck),
            act_up.reshape(flat_rows, bottleneck),
        ),
    )
    contract_rows = (((0,), (0,)), ((), ()))
    pieces = []
    for normed_all, incoming_all, latent_all, active_all in groups:
        pieces.append(
            lax.dot_general(
                normed_all, latent_all, contract_rows, preferred_element_type=jnp.float32
            )
        )
        pieces.append(
            lax.dot_general(
                incoming_all, active_all, contract_rows, preferred_element_type=jnp.float32
            )
        )
    summed = lax.psum_scatter(
        jnp.concatenate(pieces, axis=1).astype(jnp.bfloat16), "dp", scatter_dimension=0, tiled=True
    ).astype(jnp.float32)
    partner = reverse_section(summed[:, 2 * bottleneck :], section_count)
    totals = summed[:, : 2 * bottleneck] + partner
    total_down = totals[:, :bottleneck]
    total_up = totals[:, bottleneck:].T
    return (total_down[None], total_up[None])


def solution(mesh):
    return jax.shard_map(
        body,
        mesh=mesh,
        in_specs=(
            P(None, None, "dp", None),
            P(None, None, "dp", None),
            P("section", "dp", None),
            P("section", None, "dp"),
        ),
        out_specs=(P("section", "dp", None), P("section", None, "dp")),
        check_vma=False,
    )
```

profile of v0, /device:TPU:1, one launch (start us, length us, event | category | flops | bytes accessed | tf_op | source)
XLA Modules:
  0.0 1766.9 jit_solution(3362450965716382387)
XLA Ops:
  15.8 13.2 collective-permute-done.5
  30.1 12.9 collective-permute-done.6
  43.9 36.5 %collective-permute-done.7 = bf16[262144]{0:T(1024)(128)(2,1)S(1)} collective-permute-done((bf16[262144]{0:T(1024)(128)(2,1)S(1)}, bf16[262144]{0:T(1024)(128)(2,1)S(1)}, u32[]{:S(2)}, u32[]{:S(2)}) %collective-permute-start.7) | collective-permute-done | bytes 524320 | tf_op jit(solution)/shard_map/ppermute | solution.py:16
  82.4 41.0 %all-gather.5.cloned.1.call-done = bf16[1,8192,256]{2,1,0:T(8,128)(2,1)} async-done(((bf16[1,512,256]{2,1,0:T(8,128)(2,1)}), bf16[1,8192,256]{2,1,0:T(8,128)(2,1)}) %all-gather.5.cloned.1.call-update) | async-done | bytes 4194320 | tf_op jit(solution)/shard_map/all_gather | solution.py:98
  123.4 99.5 %all-gather.7.cloned.1.call-done = bf16[1,256,8192]{2,1,0:T(8,128)(2,1)} async-done(((bf16[1,256,512]{2,1,0:T(8,128)(2,1)}), bf16[1,256,8192]{2,1,0:T(8,128)(2,1)}) %all-gather.7.cloned.1.call-update) | async-done | bytes 4194320 | tf_op jit(solution)/shard_map/all_gather | solution.py:99
  222.9 101.6 %all-gather.11.cloned.1.call-done = bf16[1,256,8192]{2,1,0:T(8,128)(2,1)} async-done(((bf16[1,256,512]{2,1,0:T(8,128)(2,1)}), bf16[1,256,8192]{2,1,0:T(8,128)(2,1)}) %all-gather.11.cloned.1.call-update) | async-done | bytes 4194320 | tf_op jit(solution)/shard_map/all_gather | solution.py:101
  324.5 101.4 %all-gather.9.cloned.1.call-done = bf16[1,8192,256]{2,1,0:T(8,128)(2,1)} async-done(((bf16[1,512,256]{2,1,0:T(8,128)(2,1)}), bf16[1,8192,256]{2,1,0:T(8,128)(2,1)}) %all-gather.9.cloned.1.call-update) | async-done | bytes 4194320 | tf_op jit(solution)/shard_map/all_gather | solution.py:100
  427.5 394.9 %while.48 = (s32[]{:T(128)}, bf16[16,8192]{1,0:T(8,128)(2,1)}, bf16[16,8192]{1,0:T(8,128)(2,1)}, bf16[4,16,8192]{2,1,0:T(8,128)(2,1)S(1)}, bf16[4,16,8192]{2,1,0...) while((s32[]{:T(128)}, bf16[16,8192]{1,0:T(8,128)(2,1)}, ...), condition=%wide.region_7.8_spmd, body=%wide.region_0.7_spmd.sunk | while | flops 271360064 | bytes 28312568 | solution.py:152
  431.1 4.5 collective-permute-start.1
  450.9 6.1 conditional.8
  451.1 5.9 fusion
  469.4 6.1 conditional.8
  469.6 5.9 fusion
  490.3 6.1 conditional.8
  490.6 5.9 fusion
  511.3 6.1 conditional.8
  511.5 5.9 fusion
  532.4 10.4 collective-permute-start
  568.3 6.3 collective-permute-start
  600.0 8.0 collective-permute-start
  633.5 6.3 collective-permute-start
  665.3 38.3 %collective-permute-start = (bf16[16,8192]{1,0:T(8,128)(2,1)S(1)}, bf16[16,8192]{1,0:T(8,128)(2,1)S(1)}, u32[]{:S(2)}, u32[]{:S(2)}) collective-permute-start(bf16[16,8192]{1,0:T(8,128)(2,1)S(1)} %get-tuple-element.1224), channel_id=1, source_target_pairs={{0,16},{16,32},{32,48},{48,64},{64,80},{80,96},{96,112},{112,128},... | collective-permute-start | bytes 786440 | tf_op jit(solution)/shard_map/while/body/eval_jaxpr/ppermute | solution.py:22
  710.4 6.8 conditional.9
  710.6 6.6 fusion.16
  720.2 7.5 collective-permute-start
  734.5 6.8 conditional.9
  734.7 6.6 fusion.16
  744.3 14.0 collective-permute-start
  765.1 6.8 conditional.9
  765.3 6.6 fusion.16
  775.0 8.0 collective-permute-start
  789.7 6.8 conditional.9
  790.0 6.6 fusion.16
  810.7 4.6 collective-permute-start.1
  826.5 527.9 %while.49 = (s32[]{:T(128)}, bf16[16,8192]{1,0:T(8,128)(2,1)}, bf16[16,8192]{1,0:T(8,128)(2,1)}, bf16[4,16,8192]{2,1,0:T(8,128)(2,1)}, bf16[4,16,8192]{2,1,0:T(8...) while((s32[]{:T(128)}, bf16[16,8192]{1,0:T(8,128)(2,1)}, ...), condition=%wide.region_18.19_spmd, body=%wide.region_9.18_spmd.sunk | while | flops 408035392 | bytes 108254080 | solution.py:186
  850.6 6.9 conditional.11
  874.1 6.9 conditional.11
  889.3 4.9 collective-permute-done.2
  898.7 6.9 conditional.11
  913.9 13.5 collective-permute-done.2
  931.9 6.9 conditional.11
  956.7 7.4 collective-permute-start.3
  968.6 5.9 collective-permute-done.2
  987.8 10.1 collective-permute-done.2
  1011.3 4.5 collective-permute-done.2
  1030.4 12.5 collective-permute-done.2
  1056.2 24.3 %collective-permute-done.2 = bf16[16,8192]{1,0:T(8,128)(2,1)S(1)} collective-permute-done((bf16[16,8192]{1,0:T(8,128)(2,1)S(1)}, bf16[16,8192]{1,0:T(8,128)(2,1)S(1)}, u32[]{:S(2)}, u32[]{:S(2)}) %collective-permute-start.2) | collective-permute-done | bytes 262176 | tf_op jit(solution)/shard_map/while/body/eval_jaxpr/ppermute | solution.py:22
  1093.9 12.7 collective-permute-done.2
  1112.3 5.3 collective-permute-start.3
  1122.1 25.3 %collective-permute-done.2 = bf16[16,8192]{1,0:T(8,128)(2,1)S(1)} collective-permute-done((bf16[16,8192]{1,0:T(8,128)(2,1)S(1)}, bf16[16,8192]{1,0:T(8,128)(2,1)S(1)}, u32[]{:S(2)}, u32[]{:S(2)}) %collective-permute-start.2) | collective-permute-done | bytes 262176 | tf_op jit(solution)/shard_map/while/body/eval_jaxpr/ppermute | solution.py:22
  1160.7 27.5 %collective-permute-done.2 = bf16[16,8192]{1,0:T(8,128)(2,1)S(1)} collective-permute-done((bf16[16,8192]{1,0:T(8,128)(2,1)S(1)}, bf16[16,8192]{1,0:T(8,128)(2,1)S(1)}, u32[]{:S(2)}, u32[]{:S(2)}) %collective-permute-start.2) | collective-permute-done | bytes 262176 | tf_op jit(solution)/shard_map/while/body/eval_jaxpr/ppermute | solution.py:22
  1194.0 5.8 collective-permute-start.3
  1204.3 19.2 %collective-permute-done.2 = bf16[16,8192]{1,0:T(8,128)(2,1)S(1)} collective-permute-done((bf16[16,8192]{1,0:T(8,128)(2,1)S(1)}, bf16[16,8192]{1,0:T(8,128)(2,1)S(1)}, u32[]{:S(2)}, u32[]{:S(2)}) %collective-permute-start.2) | collective-permute-done | bytes 262176 | tf_op jit(solution)/shard_map/while/body/eval_jaxpr/ppermute | solution.py:22
  1233.0 7.5 conditional.10
  1243.2 14.9 collective-permute-done.2
  1267.7 7.5 conditional.10
  1292.4 7.5 conditional.10
  1317.2 7.5 conditional.10
  1342.6 10.0 collective-permute-start.2
  1359.6 7.1 pad_maximum_fusion
  1366.8 347.5 %reduce-scatter.2.cloned.1.call-done = bf16[512,1024]{0,1:T(8,128)(2,1)} async-done(((bf16[8192,1024]{0,1:T(8,128)(2,1)}), bf16[512,1024]{0,1:T(8,128)(2,1)}) %reduce-scatter.2.cloned.1.call-update) | async-done | bytes 1048592 | tf_op jit(solution)/shard_map/reduce_scatter | solution.py:235
  1718.8 11.9 collective-permute-done.9
  1733.5 11.0 collective-permute-done.10
  1746.9 10.4 collective-permute-done.11
  (729 shorter events, 634.9 us)
Async XLA Ops:
  7.2 116.3 %all-gather.5.cloned.1.call-start = ((), (), s32[]{:S(2)}) async-start(), calls=%async_computation.1 | async-start | bytes 4456448 | tf_op jit(solution)/shard_map/all_gather | solution.py:98
  7.9 215.0 %all-gather.7.cloned.1.call-start = ((), (), s32[]{:S(2)}) async-start(), calls=%async_computation.2 | async-start | bytes 4456448 | tf_op jit(solution)/shard_map/all_gather | solution.py:99
  8.6 315.9 %all-gather.11.cloned.1.call-start = ((), (), s32[]{:S(2)}) async-start(), calls=%async_computation.4 | async-start | bytes 4456448 | tf_op jit(solution)/shard_map/all_gather | solution.py:101
  15.8 13.2 collective-permute-start.5
  29.1 13.9 collective-permute-start.6
  43.0 37.4 %collective-permute-start.7 = (bf16[262144]{0:T(1024)(128)(2,1)S(1)}, bf16[262144]{0:T(1024)(128)(2,1)S(1)}, u32[]{:S(2)}, u32[]{:S(2)}) collective-permute-start(bf16[262144]{0:T(1024)(128)(2,1)S(1)} %collective-permute-done.6), channel_id=1, source_target_pairs={{0,128},{16,144},{32,160},{48,176},{64,192},{80,208},{96,224},{112... | collective-permute-start | bytes 1572872 | tf_op jit(solution)/shard_map/ppermute | solution.py:16
  81.3 344.6 %all-gather.9.cloned.1.call-start = ((), (), s32[]{:S(2)}) async-start(), calls=%async_computation.3 | async-start | bytes 4456448 | tf_op jit(solution)/shard_map/all_gather | solution.py:100
  82.2 1632.2 %reduce-scatter.2.cloned.1.call-start = ((), (), s32[]{:S(2)}) async-start(), calls=%async_computation.5 | async-start | bytes 17825792 | tf_op jit(solution)/shard_map/reduce_scatter | solution.py:235
  431.1 9.7 collective-permute-start.1
  447.7 11.2 collective-permute-start.1
  466.4 13.5 collective-permute-start.1
  487.3 13.5 collective-permute-start.1
  508.3 13.5 collective-permute-start.1
  529.3 13.5 collective-permute-start.1
  532.4 13.7 collective-permute-start
  550.3 8.7 collective-permute-start.1
  565.2 10.7 collective-permute-start.1
  568.3 9.6 collective-permute-start
  582.1 8.7 collective-permute-start.1
  597.0 12.3 collective-permute-start.1
  600.0 11.3 collective-permute-start
  615.5 8.7 collective-permute-start.1
  630.4 10.7 collective-permute-start.1
  633.5 9.6 collective-permute-start
  647.3 8.7 collective-permute-start.1
  662.2 42.7 %collective-permute-start.1 = (bf16[16,8192]{1,0:T(8,128)(2,1)}, bf16[16,8192]{1,0:T(8,128)(2,1)}, u32[]{:S(2)}, u32[]{:S(2)}) collective-permute-start(bf16[16,8192]{1,0:T(8,128)(2,1)} %get-tuple-element.1225), channel_id=1, source_target_pairs={{16,0},{32,16},{48,32},{64,48},{80,64},{96,80},{112,96},{128,112},... | collective-permute-start | bytes 786440 | tf_op jit(solution)/shard_map/while/body/eval_jaxpr/ppermute | solution.py:22
  665.3 41.6 %collective-permute-start = (bf16[16,8192]{1,0:T(8,128)(2,1)S(1)}, bf16[16,8192]{1,0:T(8,128)(2,1)S(1)}, u32[]{:S(2)}, u32[]{:S(2)}) collective-permute-start(bf16[16,8192]{1,0:T(8,128)(2,1)S(1)} %get-tuple-element.1224), channel_id=1, source_target_pairs={{0,16},{16,32},{32,48},{48,64},{64,80},{80,96},{96,112},{112,128},... | collective-permute-start | bytes 786440 | tf_op jit(solution)/shard_map/while/body/eval_jaxpr/ppermute | solution.py:22
  717.2 11.8 collective-permute-start.1
  720.2 10.8 collective-permute-start
  741.3 18.4 %collective-permute-start.1 = (bf16[16,8192]{1,0:T(8,128)(2,1)}, bf16[16,8192]{1,0:T(8,128)(2,1)}, u32[]{:S(2)}, u32[]{:S(2)}) collective-permute-start(bf16[16,8192]{1,0:T(8,128)(2,1)} %get-tuple-element.1225), channel_id=1, source_target_pairs={{16,0},{32,16},{48,32},{64,48},{80,64},{96,80},{112,96},{128,112},... | collective-permute-start | bytes 786440 | tf_op jit(solution)/shard_map/while/body/eval_jaxpr/ppermute | solution.py:22
  744.3 17.4 collective-permute-start
  771.9 12.4 collective-permute-start.1
  775.0 11.3 collective-permute-start
  796.5 8.0 collective-permute-start.1
  810.7 8.7 collective-permute-start.1
  831.6 10.4 collective-permute-start.3
  857.5 8.3 collective-permute-start.3
  881.0 8.3 collective-permute-start.3
  885.5 8.8 collective-permute-start.2
  905.6 8.3 collective-permute-start.3
  910.1 17.4 collective-permute-start.2
  938.8 8.3 collective-permute-start.3
  956.7 11.9 collective-permute-start.3
  966.6 7.9 collective-permute-start.2
  984.6 13.3 collective-permute-start.2
  1021.6 8.8 collective-permute-start.3
  1028.4 14.5 collective-permute-start.2
  1053.0 27.5 %collective-permute-start.2 = (bf16[16,8192]{1,0:T(8,128)(2,1)S(1)}, bf16[16,8192]{1,0:T(8,128)(2,1)S(1)}, u32[]{:S(2)}, u32[]{:S(2)}) collective-permute-start(bf16[16,8192]{1,0:T(8,128)(2,1)S(1)} %get-tuple-element.1072), channel_id=1, source_target_pairs={{16,0},{32,16},{48,32},{64,48},{80,64},{96,80},{112,96},{128,112},... | collective-permute-start | bytes 786440 | tf_op jit(solution)/shard_map/while/body/eval_jaxpr/ppermute | solution.py:22
  1090.7 15.8 collective-permute-start.2
  1112.3 9.8 collective-permute-start.3
  1120.1 27.3 %collective-permute-start.2 = (bf16[16,8192]{1,0:T(8,128)(2,1)S(1)}, bf16[16,8192]{1,0:T(8,128)(2,1)S(1)}, u32[]{:S(2)}, u32[]{:S(2)}) collective-permute-start(bf16[16,8192]{1,0:T(8,128)(2,1)S(1)} %get-tuple-element.1072), channel_id=1, source_target_pairs={{16,0},{32,16},{48,32},{64,48},{80,64},{96,80},{112,96},{128,112},... | collective-permute-start | bytes 786440 | tf_op jit(solution)/shard_map/while/body/eval_jaxpr/ppermute | solution.py:22
  1158.4 29.9 %collective-permute-start.2 = (bf16[16,8192]{1,0:T(8,128)(2,1)S(1)}, bf16[16,8192]{1,0:T(8,128)(2,1)S(1)}, u32[]{:S(2)}, u32[]{:S(2)}) collective-permute-start(bf16[16,8192]{1,0:T(8,128)(2,1)S(1)} %get-tuple-element.1072), channel_id=1, source_target_pairs={{16,0},{32,16},{48,32},{64,48},{80,64},{96,80},{112,96},{128,112},... | collective-permute-start | bytes 786440 | tf_op jit(solution)/shard_map/while/body/eval_jaxpr/ppermute | solution.py:22
  1194.0 10.3 collective-permute-start.3
  1202.3 21.2 %collective-permute-start.2 = (bf16[16,8192]{1,0:T(8,128)(2,1)S(1)}, bf16[16,8192]{1,0:T(8,128)(2,1)S(1)}, u32[]{:S(2)}, u32[]{:S(2)}) collective-permute-start(bf16[16,8192]{1,0:T(8,128)(2,1)S(1)} %get-tuple-element.1072), channel_id=1, source_target_pairs={{16,0},{32,16},{48,32},{64,48},{80,64},{96,80},{112,96},{128,112},... | collective-permute-start | bytes 786440 | tf_op jit(solution)/shard_map/while/body/eval_jaxpr/ppermute | solution.py:22
  1229.2 14.0 collective-permute-start.3
  1240.5 17.6 collective-permute-start.2
  1263.9 15.1 collective-permute-start.3
  1288.6 15.1 collective-permute-start.3
  1313.4 15.1 collective-permute-start.3
  1338.1 14.5 collective-permute-start.3
  1342.6 11.1 collective-permute-start.2
  1717.6 13.1 collective-permute-start.9
  1730.8 13.7 collective-permute-start.10
  1744.5 12.8 collective-permute-start.11
  (96 other events, 319.9 us)
Sparse Core Ops, SparseCore 0:
  9.8 113.6 all-gather.4
  125.2 97.6 all-gather.6
  225.3 99.1 all-gather.10
  326.8 99.1 all-gather.8
  1366.9 347.3 reduce-scatter.1
where the time goes:
time: 1770 us
  waiting for transfers between devices  1050 us (59%)
  starting transfers between devices  308 us (17%)
  local copies, waits for them, and re-layouts  152 us (9%)
  other arithmetic  135 us (8%)
  matrix products  100 us (6%)
    reduce_scatter x1, waiting for transfers between devices, body(): lax.psum_scatter(jnp.concatenate(pieces, axis=1).astype(jnp.bfloat16), 'd...  348 us
    ppermute x76, starting transfers between devices, passed_along(): return lax.ppermute(block, axis, route)  295 us
    ppermute x76, waiting for transfers between devices, passed_along(): return lax.ppermute(block, axis, route)  263 us
    select_n x114, other arithmetic, store_slot(): return jnp.where(inside(index), updated, stack)  118 us
    all_gather x1, waiting for transfers between devices, body(): lax.all_gather(mirror_up, 'dp', axis=2, tiled=True)  102 us
    all_gather x1, waiting for transfers between devices, body(): lax.all_gather(mirror_down, 'dp', axis=1, tiled=True)  101 us
    all_gather x1, waiting for transfers between devices, body(): lax.all_gather(up_proj, 'dp', axis=2, tiled=True)  99.5 us
    ppermute x8, waiting for transfers between devices, from_partner(): return lax.ppermute(value, axis, pairs)  99 us
  transfers between devices with their start and end apart: 89, of which 65 were waited for; matrix products, arithmetic and copies ran while one was open for 7% of the time, Pallas kernels for 0%

commit v1 on v0

v1 whole, which is shorter than its diff:
```python
import functools

import jax
import jax.numpy as jnp
from jax import lax
from jax.experimental import pallas as pl
from jax.experimental.pallas import tpu as pltpu
from jax.sharding import PartitionSpec as P

epsilon = 1e-05
root_half = 0.7071067811865476
inv_root_tau = 0.3989422804014327

BF = jnp.bfloat16
F32 = jnp.float32
BOTH = ("section", "dp")
WIDTH = 8192
RANK = 256
BLOCK = 512
BLOCKS = WIDTH // BLOCK
ROWS = 32
LAYERS = 4
EXTRA = WIDTH + RANK
VMEM_LIMIT = 50 * 2**20

GROUPS = ((0,), (1, -1), (2, -2), (3, -3), (4,))
SINGLES = (0, 1, -1, 2, -2, 3, -3, 4)


def unpack(section, dp):
    return section // 8, (section // 2) % 4, section % 2, dp // 2, dp % 2


def pack(x_hi, y, core, z, x_lo):
    return (x_hi * 8 + y * 2 + core) * 16 + z * 2 + x_lo


def pairs_of(target, keep=lambda *place: True):
    routes = []
    for section in range(16):
        for dp in range(16):
            place = unpack(section, dp)
            if keep(*place):
                routes.append((pack(*place), pack(*target(*place))))
    return routes


def send(value, target, keep=lambda *place: True):
    return lax.ppermute(value, BOTH, pairs_of(target, keep))


def along_z(value, step):
    return send(value, lambda xh, y, c, z, x: (xh, y, c, (z + step) % 8, x))


def to_core(value):
    return send(value, lambda xh, y, c, z, x: (xh, y, 1 - c, z, x))


def to_y(value):
    return send(value, lambda xh, y, c, z, x: (xh, y ^ 1, c, z, x))


def to_x(value):
    return send(value, lambda xh, y, c, z, x: (xh, y, c, z, 1 - x))


def to_first(value):
    return send(
        value,
        lambda xh, y, c, z, x: (xh, y, c, z, 1 - x) if c == 0 else (xh, y ^ 1, c, z, x),
    )


def to_second(value):
    return send(
        value,
        lambda xh, y, c, z, x: (xh, y ^ 1, c, z, x) if c == 0 else (xh, y, c, z, 1 - x),
    )


def ring(block):
    held = {0: block}
    for step in range(1, 5):
        held[step] = along_z(held[step - 1], 1)
        if step < 4:
            held[-step] = along_z(held[1 - step], -1)
    return held


def neighbourhood(block):
    first = to_first(block)
    second = to_second(block)
    third = to_second(first)
    return jnp.stack([block, first, second, third])


def hop_forward(value, stage):
    if stage == 1:
        return send(
            value,
            lambda xh, y, c, z, x: (1, 3 - y, c, z, 1 - x),
            lambda xh, y, c, z, x: xh == 0 and y >= 2,
        )
    return send(
        value,
        lambda xh, y, c, z, x: (xh, 3 - y, c, z, x),
        lambda xh, y, c, z, x: xh * 2 + y // 2 == stage,
    )


def hop_backward(value, stage):
    if stage == 2:
        return send(
            value,
            lambda xh, y, c, z, x: (0, 3 - y, c, z, 1 - x),
            lambda xh, y, c, z, x: xh == 1 and y < 2,
        )
    return send(
        value,
        lambda xh, y, c, z, x: (xh, 3 - y, c, z, x),
        lambda xh, y, c, z, x: xh * 2 + y // 2 == stage,
    )


def gelu_value(values):
    return 0.5 * values * (1.0 + lax.erf(values * root_half))


def gelu_slope(values):
    return 0.5 * (1.0 + lax.erf(values * root_half)) + values * inv_root_tau * jnp.exp(
        -0.5 * values * values
    )


def where_am_i():
    section = lax.axis_index("section")
    dp = lax.axis_index("dp")
    stage = section // 4
    return stage, (section // 2) % 2, section % 2, dp // 2, dp % 2


def fetch_weights(weight_refs, down, up, down_sem, up_sem, backward):
    _, y_lo, core, z, x_lo = where_am_i()
    down_refs = weight_refs[: 2 * len(GROUPS)]
    up_refs = weight_refs[2 * len(GROUPS) :]

    def one_layer(step, carry):
        layer = LAYERS - 1 - step if backward else step
        parity = layer % 2
        y_far = (layer // 2 + y_lo) % 2

        def start_down(offset):
            for index, distances in enumerate(GROUPS):
                source = down_refs[2 * index + offset]
                for member, distance in enumerate(distances):
                    for x_far in range(2):
                        entry = lax.select(parity == 0, x_far + 2 * y_far, y_far + 2 * x_far)
                        block = ((x_lo + x_far) % 2) * 8 + (z - distance + 8) % 8
                        pltpu.make_async_copy(
                            source.at[entry, member], down.at[layer, block], down_sem.at[layer]
                        ).start()

        def start_up(offset):
            for index, distance in enumerate(SINGLES):
                source = up_refs[2 * index + offset]
                for x_far in range(2):
                    entry = lax.select(parity == 0, x_far + 2 * y_far, y_far + 2 * x_far)
                    block = ((x_lo + x_far) % 2) * 8 + (z - distance + 8) % 8
                    pltpu.make_async_copy(
                        source.at[entry], up.at[layer, block], up_sem.at[layer]
                    ).start()

        @pl.when(parity == core)
        def _():
            if backward:
                start_up(0)
                start_down(0)
            else:
                start_down(0)
                start_up(0)

        @pl.when(parity != core)
        def _():
            if backward:
                start_up(1)
                start_down(1)
            else:
                start_down(1)
                start_up(1)

        return carry

    lax.fori_loop(0, LAYERS, one_layer, 0)


def span(block):
    return slice(block * BLOCK, (block + 1) * BLOCK)


def forward_kernel(stage, aliased, *refs):
    count = 2 * len(GROUPS) + 2 * len(SINGLES)
    h_in = refs[0]
    weight_refs = refs[1 : 1 + count]
    rest = refs[1 + count + (3 if aliased else 0) :]
    h_out, h_save, ua_save, zs_save = rest[:4]
    down, up, hidden, ua, zs, down_sem, up_sem, in_sem, h_sem, ua_sem, zs_sem = rest[4:]

    @pl.when(where_am_i()[0] == stage)
    def _():
        load = pltpu.make_async_copy(h_in, hidden.at[0], in_sem)
        load.start()
        fetch_weights(weight_refs, down, up, down_sem, up_sem, False)
        load.wait()

        def one_layer(layer, carry):
            total = jnp.zeros((ROWS, BLOCK), F32)
            for block in range(BLOCKS):
                part = hidden[layer, :, span(block)].astype(F32)
                total += part * part
            mean = jnp.sum(total, axis=-1, keepdims=True) * (1.0 / WIDTH)
            scaling = lax.rsqrt(mean + epsilon)
            pltpu.make_async_copy(down.at[layer], down.at[layer], down_sem.at[layer]).wait()
            latent = jnp.zeros((ROWS, RANK), F32)
            for block in range(BLOCKS):
                part = hidden[layer, :, span(block)].astype(F32)
                normed = (part * scaling).astype(BF)
                ua[layer, :, span(block)] = normed
                latent += jnp.dot(normed, down[layer, block], preferred_element_type=F32)
            active = gelu_value(latent).astype(BF)
            ua[layer, :, WIDTH:] = active
            zs[layer, :, :RANK] = latent
            zs[layer, :, RANK:] = jnp.broadcast_to(scaling, (ROWS, 128))
            pltpu.make_async_copy(hidden.at[layer], h_save.at[layer], h_sem.at[layer]).start()
            pltpu.make_async_copy(ua.at[layer], ua_save.at[layer], ua_sem.at[layer]).start()
            pltpu.make_async_copy(zs.at[layer], zs_save.at[layer], zs_sem.at[layer]).start()
            pltpu.make_async_copy(up.at[layer], up.at[layer], up_sem.at[layer]).wait()
            for block in range(BLOCKS):
                part = hidden[layer, :, span(block)].astype(F32)
                added = jnp.dot(active, up[layer, block], preferred_element_type=F32)
                hidden[layer + 1, :, span(block)] = (part + added).astype(BF)
            return carry

        lax.fori_loop(0, LAYERS, one_layer, 0)
        last = pltpu.make_async_copy(hidden.at[LAYERS], h_out, in_sem)
        last.start()
        for layer in range(LAYERS):
            pltpu.make_async_copy(hidden.at[layer], h_save.at[layer], h_sem.at[layer]).wait()
            pltpu.make_async_copy(ua.at[layer], ua_save.at[layer], ua_sem.at[layer]).wait()
            pltpu.make_async_copy(zs.at[layer], zs_save.at[layer], zs_sem.at[layer]).wait()
        last.wait()


def backward_kernel(stage, aliased, *refs):
    count = 2 * len(GROUPS) + 2 * len(SINGLES)
    c_in, h_save, zs_save = refs[:3]
    weight_refs = refs[3 : 3 + count]
    rest = refs[3 + count + (1 if aliased else 0) :]
    c_out, cz_save = rest[:2]
    down, up, hidden, cz, zs, down_sem, up_sem, in_sem, cz_sem = rest[2:]
    contract_last = (((1,), (1,)), ((), ()))

    @pl.when(where_am_i()[0] == stage)
    def _():
        loads = [
            pltpu.make_async_copy(c_in, cz.at[LAYERS, :, :WIDTH], in_sem.at[0]),
            pltpu.make_async_copy(zs_save, zs, in_sem.at[1]),
            pltpu.make_async_copy(h_save, hidden, in_sem.at[2]),
        ]
        for load in loads:
            load.start()
        fetch_weights(weight_refs, down, up, down_sem, up_sem, True)
        for load in loads:
            load.wait()

        def one_layer(step, carry):
            layer = LAYERS - 1 - step
            pltpu.make_async_copy(up.at[layer], up.at[layer], up_sem.at[layer]).wait()
            dactive = jnp.zeros((ROWS, RANK), F32)
            for block in range(BLOCKS):
                dactive += lax.dot_general(
                    cz[layer + 1, :, span(block)],
                    up[layer, block],
                    contract_last,
                    preferred_element_type=F32,
                )
            latent = zs[layer, :, :RANK]
            scaling = zs[layer, :, RANK:][:, :1]
            dlatent = (dactive * gelu_slope(latent)).astype(BF)
            cz[layer + 1, :, WIDTH:] = dlatent
            inner = jnp.sum(dlatent.astype(F32) * latent, axis=-1, keepdims=True) * (1.0 / WIDTH)
            pltpu.make_async_copy(cz.at[layer + 1], cz_save.at[layer], cz_sem.at[layer]).start()
            pltpu.make_async_copy(down.at[layer], down.at[layer], down_sem.at[layer]).wait()
            for block in range(BLOCKS):
                unit_grad = lax.dot_general(
                    dlatent, down[layer, block], contract_last, preferred_element_type=F32
                )
                unit_rows = hidden[layer, :, span(block)].astype(F32) * scaling
                passed = cz[layer + 1, :, span(block)].astype(F32) + scaling * (
                    unit_grad - unit_rows * inner
                )
                cz[layer, :, span(block)] = passed.astype(BF)
            return carry

        lax.fori_loop(0, LAYERS, one_layer, 0)
        last = pltpu.make_async_copy(cz.at[0, :, :WIDTH], c_out, in_sem.at[0])
        last.start()
        for layer in range(LAYERS):
            pltpu.make_async_copy(cz.at[layer + 1], cz_save.at[layer], cz_sem.at[layer]).wait()
        last.wait()


def any_specs(number):
    return [pl.BlockSpec(memory_space=pl.ANY)] * number


def weight_scratch():
    return [
        pltpu.VMEM((LAYERS, BLOCKS, BLOCK, RANK), BF),
        pltpu.VMEM((LAYERS, BLOCKS, RANK, BLOCK), BF),
    ]


row_shape = jax.ShapeDtypeStruct((ROWS, WIDTH), BF)
h_shape = jax.ShapeDtypeStruct((LAYERS, ROWS, WIDTH), BF)
pack_shape = jax.ShapeDtypeStruct((LAYERS, ROWS, EXTRA), BF)
zs_shape = jax.ShapeDtypeStruct((LAYERS, ROWS, RANK + 128), F32)
cost = pl.CostEstimate(flops=2 * 10**9, bytes_accessed=40 * 2**20, transcendentals=10**5)


def run_forward(stage, h_in, weights, saved):
    operands = [h_in, *weights, *(saved or ())]
    first = 1 + len(weights)
    return pl.pallas_call(
        functools.partial(forward_kernel, stage, saved is not None),
        out_shape=(row_shape, h_shape, pack_shape, zs_shape),
        in_specs=any_specs(len(operands)),
        out_specs=tuple(any_specs(4)),
        scratch_shapes=[
            *weight_scratch(),
            pltpu.VMEM((LAYERS + 1, ROWS, WIDTH), BF),
            pltpu.VMEM((LAYERS, ROWS, EXTRA), BF),
            pltpu.VMEM((LAYERS, ROWS, RANK + 128), F32),
            pltpu.SemaphoreType.DMA((LAYERS,)),
            pltpu.SemaphoreType.DMA((LAYERS,)),
            pltpu.SemaphoreType.DMA,
            pltpu.SemaphoreType.DMA((LAYERS,)),
            pltpu.SemaphoreType.DMA((LAYERS,)),
            pltpu.SemaphoreType.DMA((LAYERS,)),
        ],
        input_output_aliases={first + i: 1 + i for i in range(3)} if saved else {},
        compiler_params=pltpu.CompilerParams(vmem_limit_bytes=VMEM_LIMIT),
        cost_estimate=cost,
    )(*operands)


def run_backward(stage, c_in, h_save, zs_save, weights, saved):
    operands = [c_in, h_save, zs_save, *weights, *([] if saved is None else [saved])]
    first = 3 + len(weights)
    return pl.pallas_call(
        functools.partial(backward_kernel, stage, saved is not None),
        out_shape=(row_shape, pack_shape),
        in_specs=any_specs(len(operands)),
        out_specs=tuple(any_specs(2)),
        scratch_shapes=[
            *weight_scratch(),
            pltpu.VMEM((LAYERS, ROWS, WIDTH), BF),
            pltpu.VMEM((LAYERS + 1, ROWS, EXTRA), BF),
            pltpu.VMEM((LAYERS, ROWS, RANK + 128), F32),
            pltpu.SemaphoreType.DMA((LAYERS,)),
            pltpu.SemaphoreType.DMA((LAYERS,)),
            pltpu.SemaphoreType.DMA((3,)),
            pltpu.SemaphoreType.DMA((LAYERS,)),
        ],
        input_output_aliases={first: 1} if saved is not None else {},
        compiler_params=pltpu.CompilerParams(vmem_limit_bytes=VMEM_LIMIT),
        cost_estimate=cost,
    )(*operands)


def gather_weights(down_shard, up_shard):
    up_ring = ring(neighbourhood(up_shard))
    down_ring = ring(down_shard)
    weights = []
    for distances in GROUPS:
        full = neighbourhood(jnp.stack([down_ring[k] for k in distances]))
        weights += [full, to_core(full)]
    for distance in SINGLES:
        weights += [up_ring[distance], to_core(up_ring[distance])]
    return weights


def pick(value, index):
    return lax.dynamic_index_in_dim(value, index, 0, keepdims=False)


def exchange(saved, y_lo, core, x_lo):
    by_core = saved.reshape(2, 2, ROWS, EXTRA).swapaxes(0, 1)
    rows = jnp.concatenate(
        [pick(by_core, core), to_core(pick(by_core, 1 - core))], axis=1
    )
    rows = jnp.concatenate([pick(rows, y_lo), to_y(pick(rows, 1 - y_lo))], axis=0)
    wide = rows[:, :WIDTH].reshape(4 * ROWS, 2, WIDTH // 2).swapaxes(0, 1)
    narrow = rows[:, WIDTH:]
    own = jnp.concatenate([pick(wide, x_lo), narrow], axis=1)
    other = jnp.concatenate([pick(wide, 1 - x_lo), narrow], axis=1)
    rows = jnp.concatenate([own, to_x(other)], axis=0)
    return rows[:, : WIDTH // 2], rows[:, WIDTH // 2 :]


def body(entering, cotangent, down_proj, up_proj):
    section = lax.axis_index("section")
    dp = lax.axis_index("dp")
    y_lo, core, x_lo = (section // 2) % 2, section % 2, dp % 2

    def own_rows(array, half):
        chosen = pick(array, core).reshape(2, ROWS, 8, 2, BLOCK)
        return pick(chosen, half).swapaxes(1, 2).reshape(ROWS, WIDTH)

    hidden = own_rows(entering, y_lo)
    incoming = send(
        own_rows(cotangent, 1 - y_lo),
        lambda xh, y, c, z, x: (xh, y, c, z, 1 - x),
        lambda xh, y, c, z, x: xh == 1 and y >= 2,
    )
    weights = gather_weights(down_proj[0], up_proj[0])

    saved = None
    for stage in range(4):
        hidden, *saved = run_forward(stage, hidden, weights, saved)
        if stage < 3:
            hidden = hop_forward(hidden, stage)
    h_save, ua_save, zs_save = saved

    cz_save = None
    for stage in (3, 2, 1, 0):
        incoming, cz_save = run_backward(stage, incoming, h_save, zs_save, weights, cz_save)
        if stage > 0:
            incoming = hop_backward(incoming, stage)

    normed, active = exchange(ua_save, y_lo, core, x_lo)
    cotangents, dlatent = exchange(cz_save, y_lo, core, x_lo)
    contract_rows = (((0,), (0,)), ((), ()))
    pieces = jnp.concatenate(
        [
            lax.dot_general(normed, dlatent, contract_rows, preferred_element_type=F32),
            lax.dot_general(cotangents, active, contract_rows, preferred_element_type=F32),
        ],
        axis=1,
    ).astype(BF)
    groups = [[x + 2 * z for z in range(8)] for x in range(2)]
    totals = lax.psum_scatter(
        pieces, "dp", scatter_dimension=0, axis_index_groups=groups, tiled=True
    ).astype(F32)
    return (totals[:, :RANK][None], totals[:, RANK:].T[None])


def solution(mesh):
    return jax.shard_map(
        body,
        mesh=mesh,
        in_specs=(
            P(None, None, "dp", None),
            P(None, None, "dp", None),
            P("section", "dp", None),
            P("section", None, "dp"),
        ),
        out_specs=(P("section", "dp", None), P("section", None, "dp")),
        check_vma=False,
    )
```

time: 1770 us -> 603 us (0.34)
  waiting for transfers between devices: 1050 us -> 408 us
  starting transfers between devices: 308 us -> 72.7 us
  other arithmetic: 135 us -> 16.5 us
  local copies, waits for them, and re-layouts: 152 us -> 41.1 us
  matrix products: 100 us -> 1.5 us
  Pallas kernels: 0 us -> 38.2 us
    all_gather x4 -> x0, waiting for transfers between devices: 344 us -> none  [the longest x1 102 us: body(): lax.all_gather(mirror_up, 'dp', axis=2, tiled=True)]
    reduce_scatter x1, waiting for transfers between devices: 348 us -> 50.7 us  [body(): lax.psum_scatter(pieces, 'dp', scatter_dimension=0, axis_index_groups=gro...]
    ppermute x84 -> x58, starting transfers between devices: 308 us -> 72.6 us  [send(): return lax.ppermute(value, BOTH, pairs_of(target, keep))]
    select_n x114 -> x0, other arithmetic: 118 us -> none  [store_slot(): return jnp.where(inside(index), updated, stack)]
    dot_general x36 -> x2, matrix products: 100 us -> 1.5 us  [the longest x1 0.76 us: body(): lax.dot_general(normed, dlatent, contract_rows, preferred_element_type=F32)]
    slice x42 -> x0, local copies, waits for them, and re-layouts: 69.3 us -> none  [the longest x19 34.7 us: backward_tick(): cotangent[1]]
    broadcast_in_dim x133 -> x1, local copies, waits for them, and re-layouts: 46.3 us -> 1.05 us  [body(): return (totals[:, :RANK][None], totals[:, RANK:].T[None])]
    pallas_call x0 -> x8, Pallas kernels: none -> 38.2 us  [the longest x4 23.4 us: run_backward(): pl.pallas_call(functools.partial(backward_kernel, stage, saved is not Non...]
  transfers between devices with their start and end apart: 89 -> 59, of which waited for: 65 -> 25; matrix products, arithmetic and copies ran while one was open for 7% -> 5% of each run, Pallas kernels for 0% -> 4%
where the time goes in v1:
time: 603 us; the launch traced here: 593 us
  waiting for transfers between devices  408 us (68%)
  starting transfers between devices  72.7 us (12%)
  local copies, waits for them, and re-layouts  41.1 us (7%)
  Pallas kernels  38.2 us (6%)
  other arithmetic  16.5 us (3%)
  between operations  15.1 us (3%)
    ppermute x58, waiting for transfers between devices, send(): return lax.ppermute(value, BOTH, pairs_of(target, keep))  358 us
    ppermute x58, starting transfers between devices, send(): return lax.ppermute(value, BOTH, pairs_of(target, keep))  72.6 us
    reduce_scatter x1, waiting for transfers between devices, body(): lax.psum_scatter(pieces, 'dp', scatter_dimension=0, axis_index_groups=gro...  50.7 us
    pallas_call x4, Pallas kernels, run_backward(): pl.pallas_call(functools.partial(backward_kernel, stage, saved is not Non...  23.4 us
    pallas_call x4, Pallas kernels, run_forward(): pl.pallas_call(functools.partial(forward_kernel, stage, saved is not None...  14.8 us
  transfers between devices with their start and end apart: 59, of which 25 were waited for; matrix products, arithmetic and copies ran while one was open for 5% of the time, Pallas kernels for 4%

profile of v1, /device:TPU:1, one launch (start us, length us, event | category | flops | bytes accessed | tf_op | source)
XLA Modules:
  0.0 593.5 jit_solution(11495880054922440089)
XLA Ops:
  7.2 2.5 collective-permute-start.4
  9.8 4.0 collective-permute-start.5
  13.8 1.3 collective-permute-start.27
  15.1 1.2 collective-permute-start.28
  16.3 3.6 collective-permute-done.4
  20.0 1.3 collective-permute-start
  21.3 2.7 collective-permute-start.11
  23.9 1.2 collective-permute-start.1
  25.4 2.3 collective-permute-done.10
  27.8 1.4 collective-permute-start.6
  29.2 2.7 collective-permute-start.17
  32.0 1.6 collective-permute-start.7
  35.8 1.5 collective-permute-start.13
  37.4 14.4 %collective-permute-done.2 = bf16[1,512,256]{2,1,0:T(8,128)(2,1)S(1)} collective-permute-done((bf16[1,512,256]{2,1,0:T(8,128)(2,1)S(1)}, bf16[1,512,256]{2,1,0:T(8,128)(2,1)S(1)}, u32[]{:S(2)}, u32[]{:S(2)}) %collective-permute-start.2) | collective-permute-done | bytes 262176 | tf_op jit(solution)/shard_map/ppermute | solution.py:49
  51.8 1.5 collective-permute-start.19
  53.7 5.0 collective-permute-done.13
  58.8 1.2 collective-permute-done.22
  60.0 1.9 collective-permute-start.33
  61.9 3.9 collective-permute-done.18
  65.8 3.8 collective-permute-done.19
  69.7 5.0 collective-permute-start.30
  74.6 2.6 collective-permute-done.8
  77.3 2.1 collective-permute-start.24
  79.6 3.9 collective-permute-done.24
  83.4 3.2 collective-permute-start.3
  88.3 2.6 collective-permute-start.37
  90.9 4.1 collective-permute-done.14
  95.1 3.6 collective-permute-start.9
  99.0 1.6 pad_maximum_fusion.7.refs_5_.refs_7_
  100.6 6.6 %collective-permute-done.20 = bf16[2,512,256]{2,1,0:T(8,128)(2,1)S(1)} collective-permute-done((bf16[2,512,256]{2,1,0:T(8,128)(2,1)S(1)}, bf16[2,512,256]{2,1,0:T(8,128)(2,1)S(1)}, u32[]{:S(2)}, u32[]{:S(2)}) %collective-permute-start.20) | collective-permute-done | bytes 524320 | tf_op jit(solution)/shard_map/ppermute | solution.py:49
  108.3 2.6 collective-permute-done.35.refs_17_.refs_19_
  110.9 4.2 collective-permute-start.32
  116.4 1.6 pad_maximum_fusion.8.refs_7_.refs_9_
  118.9 1.8 collective-permute-start.41
  120.7 1.4 copy-done.5
  122.5 18.6 %collective-permute-done.39.refs_21_.refs_23_ = bf16[4,256,512]{2,1,0:T(8,128)(2,1)} collective-permute-done((bf16[4,256,512]{2,1,0:T(8,128)(2,1)}, bf16[4,256,512]{2,1,0:T(8,128)(2,1)}, u32[]{:S(2)}, u32[]{:S(2)}) %collective-permute-start.39) | collective-permute-done | bytes 1048608 | tf_op jit(solution)/shard_map/ppermute | solution.py:49
  144.8 21.2 %collective-permute-done.43.refs_25_.refs_27_ = bf16[4,256,512]{2,1,0:T(8,128)(2,1)} collective-permute-done((bf16[4,256,512]{2,1,0:T(8,128)(2,1)}, bf16[4,256,512]{2,1,0:T(8,128)(2,1)}, u32[]{:S(2)}, u32[]{:S(2)}) %collective-permute-start.43) | collective-permute-done | bytes 1048608 | tf_op jit(solution)/shard_map/ppermute | solution.py:49
  166.0 2.2 collective-permute-start.44
  169.3 1.8 reshape.46
  172.3 13.9 %shard_map.59 = (bf16[32,8192]{1,0:T(8,128)(2,1)S(1)}, bf16[4,32,8192]{2,1,0:T(8,128)(2,1)}, bf16[4,32,8448]{2,1,0:T(8,128)(2,1)}, f32[4,32,384]{2,1,0:T(8,128)S(1)}) custom-call(bf16[32,8192]{1,0:T(8,128)(2,1)S(1)} %bitcast.87, bf16[4,1,512,256]{3,2,1,0:T(8,128)(2,1)S(1)} %pad_maximum_fusion.11.refs_1_.refs_3_, bf16[4,1,512,256]{3,2,1,0:T(8,128)(2,1)S(1)} %copy-done.3, ...), custom_call_target="tpu_custom_call" | custom-call | flops 2000000000 | bytes 41943040 | tf_op jit(solution)/shard_map/pallas_call | solution.py:334
  186.3 1.3 collective-permute-start.45
  187.6 11.5 %collective-permute-done.45.refs_0_ = bf16[32,8192]{1,0:T(8,128)(2,1)S(1)} collective-permute-done((bf16[32,8192]{1,0:T(8,128)(2,1)S(1)}, bf16[32,8192]{1,0:T(8,128)(2,1)S(1)}, u32[]{:S(2)}, u32[]{:S(2)}) %collective-permute-start.45) | collective-permute-done | bytes 524320 | tf_op jit(solution)/shard_map/ppermute | solution.py:49
  202.7 2.6 reshape.50
  205.3 1.5 constant_dynamic-slice_fusion.2
  210.4 1.4 collective-permute-start.54
  212.7 167.2 %collective-permute-done.54.refs_0_ = bf16[32,8192]{1,0:T(8,128)(2,1)S(1)} collective-permute-done((bf16[32,8192]{1,0:T(8,128)(2,1)S(1)}, bf16[32,8192]{1,0:T(8,128)(2,1)S(1)}, u32[]{:S(2)}, u32[]{:S(2)}) %collective-permute-start.54) | collective-permute-done | bytes 524320 | tf_op jit(solution)/shard_map/ppermute | solution.py:49
  379.9 22.6 %shard_map.66 = (bf16[32,8192]{1,0:T(8,128)(2,1)}, bf16[4,32,8448]{2,1,0:T(8,128)(2,1)}) custom-call(bf16[32,8192]{1,0:T(8,128)(2,1)S(1)} %collective-permute-done.54.refs_0_, bf16[4,32,8192]{2,1,0:T(8,128)(2,1)} %get-tuple-element.37.refs_1_, f32[4,32,384]{2,1,0:T(8,128)S(1)} %get-tuple-element.38.refs_2_, ...), custom_call_target="tpu_custom_call", output_to_operand_aliasing={{1}: (29, {})} | custom-call | flops 2000000000 | bytes 41943040 | tf_op jit(solution)/shard_map/pallas_call | solution.py:360
  402.5 1.7 dynamic-slice_bitcast_fusion
  404.2 3.7 collective-permute-start.55
  409.0 1.2 collective-permute-done.55
  410.3 1.5 fusion.7
  412.0 22.7 %collective-permute-done.49 = bf16[64,8448]{1,0:T(8,128)(2,1)S(1)} collective-permute-done((bf16[64,8448]{1,0:T(8,128)(2,1)}, bf16[64,8448]{1,0:T(8,128)(2,1)S(1)}, u32[]{:S(2)}, u32[]{:S(2)}) %collective-permute-start.49) | collective-permute-done | bytes 1081376 | tf_op jit(solution)/shard_map/ppermute | solution.py:49
  435.7 1.5 fusion.1
  437.2 3.3 reshape.49
  441.4 16.6 %collective-permute-done.56 = bf16[64,8448]{1,0:T(8,128)(2,1)} collective-permute-done((bf16[64,8448]{1,0:T(8,128)(2,1)}, bf16[64,8448]{1,0:T(8,128)(2,1)}, u32[]{:S(2)}, u32[]{:S(2)}) %collective-permute-start.56) | collective-permute-done | bytes 1081376 | tf_op jit(solution)/shard_map/ppermute | solution.py:49
  458.0 2.8 fusion
  460.7 4.5 reshape.53
  465.2 11.5 %constant_dynamic-slice_fusion.1 = (bf16[128,1,4096]{2,1,0:T(2,128)(2,1)S(1)}, bf16[128,1,4096]{2,1,0:T(2,128)(2,1)S(1)}, bf16[128,1,4096]{2,1,0:T(2,128)(2,1)S(1)}, bf16[128,1,4096]{2,1,0:T(2,128)(2,1)S(1)}) fusion(bf16[128,2,4096]{2,1,0:T(2,128)(2,1)} %reshape.53, s32[]{:T(128)S(6)} %select_n.60, s32[]{:T(128)S(6)} %select_n.61, ...), kind=kLoop, calls=%fused_computation.64 | loop fusion | bytes 8388616 | tf_op jit(solution)/shard_map/dynamic-slice.6
  480.1 1.8 collective-permute-start.57
  484.2 19.2 %collective-permute-done.50 = bf16[128,4352]{1,0:T(8,128)(2,1)S(1)} collective-permute-done((bf16[128,4352]{1,0:T(8,128)(2,1)S(1)}, bf16[128,4352]{1,0:T(8,128)(2,1)S(1)}, u32[]{:S(2)}, u32[]{:S(2)}) %collective-permute-start.50) | collective-permute-done | bytes 1114144 | tf_op jit(solution)/shard_map/ppermute | solution.py:49
  503.5 23.7 %collective-permute-done.57 = bf16[128,4352]{1,0:T(8,128)(2,1)S(1)} collective-permute-done((bf16[128,4352]{1,0:T(8,128)(2,1)S(1)}, bf16[128,4352]{1,0:T(8,128)(2,1)S(1)}, u32[]{:S(2)}, u32[]{:S(2)}) %collective-permute-start.57) | collective-permute-done | bytes 1114144 | tf_op jit(solution)/shard_map/ppermute | solution.py:49
  528.7 2.5 pad_maximum_fusion
  531.3 50.7 %reduce-scatter.2.cloned.1.call-done = bf16[512,512]{0,1:T(8,128)(2,1)} async-done(((bf16[4096,512]{0,1:T(8,128)(2,1)}), bf16[512,512]{0,1:T(8,128)(2,1)}) %reduce-scatter.2.cloned.1.call-update) | async-done | bytes 524304 | tf_op jit(solution)/shard_map/reduce_scatter | solution.py:452
  584.2 2.0 copy.30
  (150 shorter events, 35.5 us)
Async XLA Ops:
  7.2 161.1 %copy-start = (bf16[2,4,16,8192]{3,2,1,0:T(8,128)(2,1)S(1)}, bf16[2,4,16,8192]{3,2,1,0:T(8,128)(2,1)}, u32[]{:S(2)}) copy-start(bf16[2,4,16,8192]{3,2,1,0:T(8,128)(2,1)} %param.4) | copy-start | bytes 6291460
  7.2 574.8 %reduce-scatter.2.cloned.1.call-start = ((), (), s32[]{:S(2)}) async-start(), calls=%async_computation.1 | async-start | bytes 4718592 | tf_op jit(solution)/shard_map/reduce_scatter | solution.py:452
  7.2 12.7 %collective-permute-start.4 = (bf16[512,256]{1,0:T(8,128)(2,1)}, bf16[512,256]{1,0:T(8,128)(2,1)S(1)}, u32[]{:S(2)}, u32[]{:S(2)}) collective-permute-start(bf16[512,256]{1,0:T(8,128)(2,1)} %bitcast.116), channel_id=1, source_target_pairs={{0,2},{1,3},{2,4},{3,5},{4,6},{5,7},{6,8},{7,9},{8,10},{9,11},{10,... | collective-permute-start | bytes 786440 | tf_op jit(solution)/shard_map/ppermute | solution.py:49
  9.8 11.5 %collective-permute-start.5 = (bf16[512,256]{1,0:T(8,128)(2,1)}, bf16[512,256]{1,0:T(8,128)(2,1)S(1)}, u32[]{:S(2)}, u32[]{:S(2)}) collective-permute-start(bf16[512,256]{1,0:T(8,128)(2,1)} %bitcast.117), channel_id=1, source_target_pairs={{0,14},{1,15},{2,0},{3,1},{4,2},{5,3},{6,4},{7,5},{8,6},{9,7},{10,... | collective-permute-start | bytes 786440 | tf_op jit(solution)/shard_map/ppermute | solution.py:49
  13.8 10.1 %collective-permute-start.27 = (bf16[256,512]{1,0:T(8,128)(2,1)}, bf16[256,512]{1,0:T(8,128)(2,1)S(1)}, u32[]{:S(2)}, u32[]{:S(2)}) collective-permute-start(bf16[256,512]{1,0:T(8,128)(2,1)} %bitcast.114), channel_id=1, source_target_pairs={{0,1},{1,0},{2,3},{3,2},{4,5},{5,4},{6,7},{7,6},{8,9},{9,8},{10,11... | collective-permute-start | bytes 786440 | tf_op jit(solution)/shard_map/ppermute | solution.py:49
  15.1 10.1 %collective-permute-start.28 = (bf16[256,512]{1,0:T(8,128)(2,1)}, bf16[256,512]{1,0:T(8,128)(2,1)S(1)}, u32[]{:S(2)}, u32[]{:S(2)}) collective-permute-start(bf16[256,512]{1,0:T(8,128)(2,1)} %bitcast.115), channel_id=1, source_target_pairs={{0,32},{1,33},{2,34},{3,35},{4,36},{5,37},{6,38},{7,39},{8,40},{9,... | collective-permute-start | bytes 786440 | tf_op jit(solution)/shard_map/ppermute | solution.py:49
  20.0 7.8 %collective-permute-start.10 = (bf16[512,256]{1,0:T(8,128)(2,1)S(1)}, bf16[512,256]{1,0:T(8,128)(2,1)S(1)}, u32[]{:S(2)}, u32[]{:S(2)}) collective-permute-start(bf16[512,256]{1,0:T(8,128)(2,1)S(1)} %collective-permute-done.4), channel_id=1, source_target_pairs={{0,2},{1,3},{2,4},{3,5},{4,6},{5,7},{6,8},{7,9},{8,10},{9,11},{10,... | collective-permute-start | bytes 786440 | tf_op jit(solution)/shard_map/ppermute | solution.py:49
  20.0 7.9 %collective-permute-start = (bf16[1,512,256]{2,1,0:T(8,128)(2,1)}, bf16[1,512,256]{2,1,0:T(8,128)(2,1)S(1)}, u32[]{:S(2)}, u32[]{:S(2)}) collective-permute-start(bf16[1,512,256]{2,1,0:T(8,128)(2,1)} %param.6), channel_id=1, source_target_pairs={{0,1},{1,0},{2,3},{3,2},{4,5},{5,4},{6,7},{7,6},{8,9},{9,8},{10,11... | collective-permute-start | bytes 786440 | tf_op jit(solution)/shard_map/ppermute | solution.py:49
  21.3 8.0 %collective-permute-start.11 = (bf16[512,256]{1,0:T(8,128)(2,1)S(1)}, bf16[512,256]{1,0:T(8,128)(2,1)S(1)}, u32[]{:S(2)}, u32[]{:S(2)}) collective-permute-start(bf16[512,256]{1,0:T(8,128)(2,1)S(1)} %collective-permute-done.5), channel_id=1, source_target_pairs={{0,14},{1,15},{2,0},{3,1},{4,2},{5,3},{6,4},{7,5},{8,6},{9,7},{10,... | collective-permute-start | bytes 786440 | tf_op jit(solution)/shard_map/ppermute | solution.py:49
  23.9 8.0 %collective-permute-start.1 = (bf16[1,512,256]{2,1,0:T(8,128)(2,1)}, bf16[1,512,256]{2,1,0:T(8,128)(2,1)S(1)}, u32[]{:S(2)}, u32[]{:S(2)}) collective-permute-start(bf16[1,512,256]{2,1,0:T(8,128)(2,1)} %param.6), channel_id=1, source_target_pairs={{0,32},{1,33},{2,34},{3,35},{4,36},{5,37},{6,38},{7,39},{8,40},{9,... | collective-permute-start | bytes 786440 | tf_op jit(solution)/shard_map/ppermute | solution.py:49
  25.1 8.5 %collective-permute-start.29 = (bf16[256,512]{1,0:T(8,128)(2,1)S(1)}, bf16[256,512]{1,0:T(8,128)(2,1)S(1)}, u32[]{:S(2)}, u32[]{:S(2)}) collective-permute-start(bf16[256,512]{1,0:T(8,128)(2,1)S(1)} %collective-permute-done.27), channel_id=1, source_target_pairs={{0,32},{1,33},{2,34},{3,35},{4,36},{5,37},{6,38},{7,39},{8,40},{9,... | collective-permute-start | bytes 786440 | tf_op jit(solution)/shard_map/ppermute | solution.py:49
  27.7 6.9 %collective-permute-start.16 = (bf16[512,256]{1,0:T(8,128)(2,1)S(1)}, bf16[512,256]{1,0:T(8,128)(2,1)S(1)}, u32[]{:S(2)}, u32[]{:S(2)}) collective-permute-start(bf16[512,256]{1,0:T(8,128)(2,1)S(1)} %collective-permute-done.10), channel_id=1, source_target_pairs={{0,2},{1,3},{2,4},{3,5},{4,6},{5,7},{6,8},{7,9},{8,10},{9,11},{10,... | collective-permute-start | bytes 786440 | tf_op jit(solution)/shard_map/ppermute | solution.py:49
  27.8 24.0 %collective-permute-start.6 = (bf16[2,512,256]{2,1,0:T(8,128)(2,1)S(1)}, bf16[2,512,256]{2,1,0:T(8,128)(2,1)S(1)}, u32[]{:S(2)}, u32[]{:S(2)}) collective-permute-start(bf16[2,512,256]{2,1,0:T(8,128)(2,1)S(1)} %get-tuple-element.71), channel_id=1, source_target_pairs={{0,1},{1,0},{2,3},{3,2},{4,5},{5,4},{6,7},{7,6},{8,9},{9,8},{10,11... | collective-permute-start | bytes 1572872 | tf_op jit(solution)/shard_map/ppermute | solution.py:49
  29.2 6.6 %collective-permute-start.17 = (bf16[512,256]{1,0:T(8,128)(2,1)S(1)}, bf16[512,256]{1,0:T(8,128)(2,1)S(1)}, u32[]{:S(2)}, u32[]{:S(2)}) collective-permute-start(bf16[512,256]{1,0:T(8,128)(2,1)S(1)} %collective-permute-done.11), channel_id=1, source_target_pairs={{0,14},{1,15},{2,0},{3,1},{4,2},{5,3},{6,4},{7,5},{8,6},{9,7},{10,... | collective-permute-start | bytes 786440 | tf_op jit(solution)/shard_map/ppermute | solution.py:49
  32.0 47.5 %copy-start.21 = (bf16[1,512,256]{2,1,0:T(8,128)(2,1)S(1)}, bf16[1,512,256]{2,1,0:T(8,128)(2,1)}, u32[]{:S(2)}) copy-start(bf16[1,512,256]{2,1,0:T(8,128)(2,1)} %param.6) | copy-start | bytes 786436
  32.0 21.3 %collective-permute-start.7 = (bf16[2,512,256]{2,1,0:T(8,128)(2,1)S(1)}, bf16[2,512,256]{2,1,0:T(8,128)(2,1)S(1)}, u32[]{:S(2)}, u32[]{:S(2)}) collective-permute-start(bf16[2,512,256]{2,1,0:T(8,128)(2,1)S(1)} %get-tuple-element.71), channel_id=1, source_target_pairs={{0,32},{1,33},{2,34},{3,35},{4,36},{5,37},{6,38},{7,39},{8,40},{9,... | collective-permute-start | bytes 1572872 | tf_op jit(solution)/shard_map/ppermute | solution.py:49
  33.6 19.7 %collective-permute-start.12 = (bf16[2,512,256]{2,1,0:T(8,128)(2,1)S(1)}, bf16[2,512,256]{2,1,0:T(8,128)(2,1)S(1)}, u32[]{:S(2)}, u32[]{:S(2)}) collective-permute-start(bf16[2,512,256]{2,1,0:T(8,128)(2,1)S(1)} %get-tuple-element.69), channel_id=1, source_target_pairs={{0,1},{1,0},{2,3},{3,2},{4,5},{5,4},{6,7},{7,6},{8,9},{9,8},{10,11... | collective-permute-start | bytes 1572872 | tf_op jit(solution)/shard_map/ppermute | solution.py:49
  34.6 17.2 %collective-permute-start.2 = (bf16[1,512,256]{2,1,0:T(8,128)(2,1)S(1)}, bf16[1,512,256]{2,1,0:T(8,128)(2,1)S(1)}, u32[]{:S(2)}, u32[]{:S(2)}) collective-permute-start(bf16[1,512,256]{2,1,0:T(8,128)(2,1)S(1)} %collective-permute-done), channel_id=1, source_target_pairs={{0,32},{1,33},{2,34},{3,35},{4,36},{5,37},{6,38},{7,39},{8,40},{9,... | collective-permute-start | bytes 786440 | tf_op jit(solution)/shard_map/ppermute | solution.py:49
  35.8 23.0 %collective-permute-start.13 = (bf16[2,512,256]{2,1,0:T(8,128)(2,1)S(1)}, bf16[2,512,256]{2,1,0:T(8,128)(2,1)S(1)}, u32[]{:S(2)}, u32[]{:S(2)}) collective-permute-start(bf16[2,512,256]{2,1,0:T(8,128)(2,1)S(1)} %get-tuple-element.69), channel_id=1, source_target_pairs={{0,32},{1,33},{2,34},{3,35},{4,36},{5,37},{6,38},{7,39},{8,40},{9,... | collective-permute-start | bytes 1572872 | tf_op jit(solution)/shard_map/ppermute | solution.py:49
  51.8 14.0 %collective-permute-start.18 = (bf16[2,512,256]{2,1,0:T(8,128)(2,1)S(1)}, bf16[2,512,256]{2,1,0:T(8,128)(2,1)S(1)}, u32[]{:S(2)}, u32[]{:S(2)}) collective-permute-start(bf16[2,512,256]{2,1,0:T(8,128)(2,1)S(1)} %get-tuple-element.67), channel_id=1, source_target_pairs={{0,1},{1,0},{2,3},{3,2},{4,5},{5,4},{6,7},{7,6},{8,9},{9,8},{10,11... | collective-permute-start | bytes 1572872 | tf_op jit(solution)/shard_map/ppermute | solution.py:49
  51.8 17.9 %collective-permute-start.19 = (bf16[2,512,256]{2,1,0:T(8,128)(2,1)S(1)}, bf16[2,512,256]{2,1,0:T(8,128)(2,1)S(1)}, u32[]{:S(2)}, u32[]{:S(2)}) collective-permute-start(bf16[2,512,256]{2,1,0:T(8,128)(2,1)S(1)} %get-tuple-element.67), channel_id=1, source_target_pairs={{0,32},{1,33},{2,34},{3,35},{4,36},{5,37},{6,38},{7,39},{8,40},{9,... | collective-permute-start | bytes 1572872 | tf_op jit(solution)/shard_map/ppermute | solution.py:49
  53.3 24.0 %collective-permute-start.8 = (bf16[2,512,256]{2,1,0:T(8,128)(2,1)S(1)}, bf16[2,512,256]{2,1,0:T(8,128)(2,1)S(1)}, u32[]{:S(2)}, u32[]{:S(2)}) collective-permute-start(bf16[2,512,256]{2,1,0:T(8,128)(2,1)S(1)} %collective-permute-done.6), channel_id=1, source_target_pairs={{0,32},{1,33},{2,34},{3,35},{4,36},{5,37},{6,38},{7,39},{8,40},{9,... | collective-permute-start | bytes 1572872 | tf_op jit(solution)/shard_map/ppermute | solution.py:49
  53.4 6.6 %collective-permute-start.22 = (bf16[512,256]{1,0:T(8,128)(2,1)S(1)}, bf16[512,256]{1,0:T(8,128)(2,1)S(1)}, u32[]{:S(2)}, u32[]{:S(2)}) collective-permute-start(bf16[512,256]{1,0:T(8,128)(2,1)S(1)} %collective-permute-done.16), channel_id=1, source_target_pairs={{0,2},{1,3},{2,4},{3,5},{4,6},{5,7},{6,8},{7,9},{8,10},{9,11},{10,... | collective-permute-start | bytes 786440 | tf_op jit(solution)/shard_map/ppermute | solution.py:49
  53.7 34.2 %copy-start.6 = (bf16[4,256,512]{2,1,0:T(8,128)(2,1)}, bf16[4,256,512]{2,1,0:T(8,128)(2,1)S(1)}, u32[]{:S(2)}) copy-start(bf16[4,256,512]{2,1,0:T(8,128)(2,1)S(1)} %pad_maximum_fusion.13.refs_11_.refs_13_) | copy-start | bytes 3145732
  58.8 29.4 %collective-permute-start.31 = (bf16[4,256,512]{2,1,0:T(8,128)(2,1)S(1)}, bf16[4,256,512]{2,1,0:T(8,128)(2,1)S(1)}, u32[]{:S(2)}, u32[]{:S(2)}) collective-permute-start(bf16[4,256,512]{2,1,0:T(8,128)(2,1)S(1)} %pad_maximum_fusion.13.refs_11_.refs_13_), channel_id=1, source_target_pairs={{0,2},{1,3},{2,4},{3,5},{4,6},{5,7},{6,8},{7,9},{8,10},{9,11},{10,... | collective-permute-start | bytes 3145736 | tf_op jit(solution)/shard_map/ppermute | solution.py:49
  60.0 28.3 %collective-permute-start.33 = (bf16[4,256,512]{2,1,0:T(8,128)(2,1)S(1)}, bf16[4,256,512]{2,1,0:T(8,128)(2,1)S(1)}, u32[]{:S(2)}, u32[]{:S(2)}) collective-permute-start(bf16[4,256,512]{2,1,0:T(8,128)(2,1)S(1)} %pad_maximum_fusion.13.refs_11_.refs_13_), channel_id=1, source_target_pairs={{0,14},{1,15},{2,0},{3,1},{4,2},{5,3},{6,4},{7,5},{8,6},{9,7},{10,... | collective-permute-start | bytes 3145736 | tf_op jit(solution)/shard_map/ppermute | solution.py:49
  65.8 13.6 %collective-permute-start.23 = (bf16[1,512,256]{2,1,0:T(8,128)(2,1)S(1)}, bf16[1,512,256]{2,1,0:T(8,128)(2,1)S(1)}, u32[]{:S(2)}, u32[]{:S(2)}) collective-permute-start(bf16[1,512,256]{2,1,0:T(8,128)(2,1)S(1)} %bitcast.125), channel_id=1, source_target_pairs={{0,1},{1,0},{2,3},{3,2},{4,5},{5,4},{6,7},{7,6},{8,9},{9,8},{10,11... | collective-permute-start | bytes 786440 | tf_op jit(solution)/shard_map/ppermute | solution.py:49
  69.7 29.0 %collective-permute-start.30 = (bf16[4,256,512]{2,1,0:T(8,128)(2,1)S(1)}, bf16[4,256,512]{2,1,0:T(8,128)(2,1)S(1)}, u32[]{:S(2)}, u32[]{:S(2)}) collective-permute-start(bf16[4,256,512]{2,1,0:T(8,128)(2,1)S(1)} %pad_maximum_fusion.13.refs_11_.refs_13_), channel_id=1, source_target_pairs={{0,16},{1,17},{2,18},{3,19},{4,20},{5,21},{6,22},{7,23},{8,24},{9,... | collective-permute-start | bytes 3145736 | tf_op jit(solution)/shard_map/ppermute | solution.py:49
  77.3 6.2 %collective-permute-start.24 = (bf16[1,512,256]{2,1,0:T(8,128)(2,1)S(1)}, bf16[1,512,256]{2,1,0:T(8,128)(2,1)S(1)}, u32[]{:S(2)}, u32[]{:S(2)}) collective-permute-start(bf16[1,512,256]{2,1,0:T(8,128)(2,1)S(1)} %bitcast.126), channel_id=1, source_target_pairs={{0,32},{1,33},{2,34},{3,35},{4,36},{5,37},{6,38},{7,39},{8,40},{9,... | collective-permute-start | bytes 786440 | tf_op jit(solution)/shard_map/ppermute | solution.py:49
  79.4 7.2 %collective-permute-start.25 = (bf16[1,512,256]{2,1,0:T(8,128)(2,1)S(1)}, bf16[1,512,256]{2,1,0:T(8,128)(2,1)S(1)}, u32[]{:S(2)}, u32[]{:S(2)}) collective-permute-start(bf16[1,512,256]{2,1,0:T(8,128)(2,1)S(1)} %collective-permute-done.23), channel_id=1, source_target_pairs={{0,32},{1,33},{2,34},{3,35},{4,36},{5,37},{6,38},{7,39},{8,40},{9,... | collective-permute-start | bytes 786440 | tf_op jit(solution)/shard_map/ppermute | solution.py:49
  83.4 15.3 %collective-permute-start.3 = (bf16[4,1,512,256]{3,2,1,0:T(8,128)(2,1)S(1)}, bf16[4,1,512,256]{3,2,1,0:T(8,128)(2,1)S(1)}, u32[]{:S(2)}, u32[]{:S(2)}) collective-permute-start(bf16[4,1,512,256]{3,2,1,0:T(8,128)(2,1)S(1)} %pad_maximum_fusion.11.refs_1_.refs_3_), channel_id=1, source_target_pairs={{0,16},{1,17},{2,18},{3,19},{4,20},{5,21},{6,22},{7,23},{8,24},{9,... | collective-permute-start | bytes 3145736 | tf_op jit(solution)/shard_map/ppermute | solution.py:49
  86.6 8.4 %collective-permute-start.14 = (bf16[2,512,256]{2,1,0:T(8,128)(2,1)S(1)}, bf16[2,512,256]{2,1,0:T(8,128)(2,1)S(1)}, u32[]{:S(2)}, u32[]{:S(2)}) collective-permute-start(bf16[2,512,256]{2,1,0:T(8,128)(2,1)S(1)} %collective-permute-done.12), channel_id=1, source_target_pairs={{0,32},{1,33},{2,34},{3,35},{4,36},{5,37},{6,38},{7,39},{8,40},{9,... | collective-permute-start | bytes 1572872 | tf_op jit(solution)/shard_map/ppermute | solution.py:49
  88.2 22.7 %collective-permute-start.35 = (bf16[4,256,512]{2,1,0:T(8,128)(2,1)S(1)}, bf16[4,256,512]{2,1,0:T(8,128)(2,1)}, u32[]{:S(2)}, u32[]{:S(2)}) collective-permute-start(bf16[4,256,512]{2,1,0:T(8,128)(2,1)S(1)} %collective-permute-done.31.refs_13_.refs_15_), channel_id=1, source_target_pairs={{0,2},{1,3},{2,4},{3,5},{4,6},{5,7},{6,8},{7,9},{8,10},{9,11},{10,... | collective-permute-start | bytes 3145736 | tf_op jit(solution)/shard_map/ppermute | solution.py:49
  88.3 26.9 %copy-start.9 = (bf16[4,256,512]{2,1,0:T(8,128)(2,1)}, bf16[4,256,512]{2,1,0:T(8,128)(2,1)S(1)}, u32[]{:S(2)}) copy-start(bf16[4,256,512]{2,1,0:T(8,128)(2,1)S(1)} %collective-permute-done.33.refs_15_.refs_17_) | copy-start | bytes 3145732
  88.3 26.9 %collective-permute-start.37 = (bf16[4,256,512]{2,1,0:T(8,128)(2,1)S(1)}, bf16[4,256,512]{2,1,0:T(8,128)(2,1)}, u32[]{:S(2)}, u32[]{:S(2)}) collective-permute-start(bf16[4,256,512]{2,1,0:T(8,128)(2,1)S(1)} %collective-permute-done.33.refs_15_.refs_17_), channel_id=1, source_target_pairs={{0,14},{1,15},{2,0},{3,1},{4,2},{5,3},{6,4},{7,5},{8,6},{9,7},{10,... | collective-permute-start | bytes 3145736 | tf_op jit(solution)/shard_map/ppermute | solution.py:49
  95.1 25.7 %collective-permute-start.9 = (bf16[4,2,512,256]{3,2,1,0:T(8,128)(2,1)S(1)}, bf16[4,2,512,256]{3,2,1,0:T(8,128)(2,1)S(1)}, u32[]{:S(2)}, u32[]{:S(2)}) collective-permute-start(bf16[4,2,512,256]{3,2,1,0:T(8,128)(2,1)S(1)} %pad_maximum_fusion.6.refs_3_.refs_5_), channel_id=1, source_target_pairs={{0,16},{1,17},{2,18},{3,19},{4,20},{5,21},{6,22},{7,23},{8,24},{9,... | collective-permute-start | bytes 6291464 | tf_op jit(solution)/shard_map/ppermute | solution.py:49
  98.6 16.6 %collective-permute-start.26 = (bf16[4,1,512,256]{3,2,1,0:T(8,128)(2,1)S(1)}, bf16[4,1,512,256]{3,2,1,0:T(8,128)(2,1)S(1)}, u32[]{:S(2)}, u32[]{:S(2)}) collective-permute-start(bf16[4,1,512,256]{3,2,1,0:T(8,128)(2,1)S(1)} %pad_maximum_fusion.12.refs_9_.refs_11_), channel_id=1, source_target_pairs={{0,16},{1,17},{2,18},{3,19},{4,20},{5,21},{6,22},{7,23},{8,24},{9,... | collective-permute-start | bytes 3145736 | tf_op jit(solution)/shard_map/ppermute | solution.py:49
  98.7 8.4 %collective-permute-start.20 = (bf16[2,512,256]{2,1,0:T(8,128)(2,1)S(1)}, bf16[2,512,256]{2,1,0:T(8,128)(2,1)S(1)}, u32[]{:S(2)}, u32[]{:S(2)}) collective-permute-start(bf16[2,512,256]{2,1,0:T(8,128)(2,1)S(1)} %collective-permute-done.18), channel_id=1, source_target_pairs={{0,32},{1,33},{2,34},{3,35},{4,36},{5,37},{6,38},{7,39},{8,40},{9,... | collective-permute-start | bytes 1572872 | tf_op jit(solution)/shard_map/ppermute | solution.py:49
  107.2 34.3 %collective-permute-start.15 = (bf16[4,2,512,256]{3,2,1,0:T(8,128)(2,1)}, bf16[4,2,512,256]{3,2,1,0:T(8,128)(2,1)}, u32[]{:S(2)}, u32[]{:S(2)}) collective-permute-start(bf16[4,2,512,256]{3,2,1,0:T(8,128)(2,1)} %pad_maximum_fusion.7.refs_5_.refs_7_), channel_id=1, source_target_pairs={{0,16},{1,17},{2,18},{3,19},{4,20},{5,21},{6,22},{7,23},{8,24},{9,... | collective-permute-start | bytes 6291464 | tf_op jit(solution)/shard_map/ppermute | solution.py:49
  110.9 7.1 %collective-permute-start.32 = (bf16[4,256,512]{2,1,0:T(8,128)(2,1)S(1)}, bf16[4,256,512]{2,1,0:T(8,128)(2,1)S(1)}, u32[]{:S(2)}, u32[]{:S(2)}) collective-permute-start(bf16[4,256,512]{2,1,0:T(8,128)(2,1)S(1)} %collective-permute-done.31.refs_13_.refs_15_), channel_id=1, source_target_pairs={{0,16},{1,17},{2,18},{3,19},{4,20},{5,21},{6,22},{7,23},{8,24},{9,... | collective-permute-start | bytes 3145736 | tf_op jit(solution)/shard_map/ppermute | solution.py:49
  115.1 3.8 collective-permute-start.34
  115.3 25.9 %collective-permute-start.39 = (bf16[4,256,512]{2,1,0:T(8,128)(2,1)}, bf16[4,256,512]{2,1,0:T(8,128)(2,1)}, u32[]{:S(2)}, u32[]{:S(2)}) collective-permute-start(bf16[4,256,512]{2,1,0:T(8,128)(2,1)} %collective-permute-done.35.refs_17_.refs_19_), channel_id=1, source_target_pairs={{0,2},{1,3},{2,4},{3,5},{4,6},{5,7},{6,8},{7,9},{8,10},{9,11},{10,... | collective-permute-start | bytes 3145736 | tf_op jit(solution)/shard_map/ppermute | solution.py:49
  118.0 53.9 %collective-permute-start.21 = (bf16[4,2,512,256]{3,2,1,0:T(8,128)(2,1)}, bf16[4,2,512,256]{3,2,1,0:T(8,128)(2,1)}, u32[]{:S(2)}, u32[]{:S(2)}) collective-permute-start(bf16[4,2,512,256]{3,2,1,0:T(8,128)(2,1)} %pad_maximum_fusion.8.refs_7_.refs_9_), channel_id=1, source_target_pairs={{0,16},{1,17},{2,18},{3,19},{4,20},{5,21},{6,22},{7,23},{8,24},{9,... | collective-permute-start | bytes 6291464 | tf_op jit(solution)/shard_map/ppermute | solution.py:49
  118.9 24.7 %collective-permute-start.41 = (bf16[4,256,512]{2,1,0:T(8,128)(2,1)}, bf16[4,256,512]{2,1,0:T(8,128)(2,1)}, u32[]{:S(2)}, u32[]{:S(2)}) collective-permute-start(bf16[4,256,512]{2,1,0:T(8,128)(2,1)} %collective-permute-done.37.refs_19_.refs_21_), channel_id=1, source_target_pairs={{0,14},{1,15},{2,0},{3,1},{4,2},{5,3},{6,4},{7,5},{8,6},{9,7},{10,... | collective-permute-start | bytes 3145736 | tf_op jit(solution)/shard_map/ppermute | solution.py:49
  122.1 22.7 %collective-permute-start.36 = (bf16[4,256,512]{2,1,0:T(8,128)(2,1)}, bf16[4,256,512]{2,1,0:T(8,128)(2,1)}, u32[]{:S(2)}, u32[]{:S(2)}) collective-permute-start(bf16[4,256,512]{2,1,0:T(8,128)(2,1)} %collective-permute-done.35.refs_17_.refs_19_), channel_id=1, source_target_pairs={{0,16},{1,17},{2,18},{3,19},{4,20},{5,21},{6,22},{7,23},{8,24},{9,... | collective-permute-start | bytes 3145736 | tf_op jit(solution)/shard_map/ppermute | solution.py:49
  141.1 24.9 %collective-permute-start.43 = (bf16[4,256,512]{2,1,0:T(8,128)(2,1)}, bf16[4,256,512]{2,1,0:T(8,128)(2,1)}, u32[]{:S(2)}, u32[]{:S(2)}) collective-permute-start(bf16[4,256,512]{2,1,0:T(8,128)(2,1)} %collective-permute-done.39.refs_21_.refs_23_), channel_id=1, source_target_pairs={{0,2},{1,3},{2,4},{3,5},{4,6},{5,7},{6,8},{7,9},{8,10},{9,11},{10,... | collective-permute-start | bytes 3145736 | tf_op jit(solution)/shard_map/ppermute | solution.py:49
  141.5 30.5 %collective-permute-start.38 = (bf16[4,256,512]{2,1,0:T(8,128)(2,1)}, bf16[4,256,512]{2,1,0:T(8,128)(2,1)}, u32[]{:S(2)}, u32[]{:S(2)}) collective-permute-start(bf16[4,256,512]{2,1,0:T(8,128)(2,1)} %collective-permute-done.37.refs_19_.refs_21_), channel_id=1, source_target_pairs={{0,16},{1,17},{2,18},{3,19},{4,20},{5,21},{6,22},{7,23},{8,24},{9,... | collective-permute-start | bytes 3145736 | tf_op jit(solution)/shard_map/ppermute | solution.py:49
  143.6 28.4 %collective-permute-start.40 = (bf16[4,256,512]{2,1,0:T(8,128)(2,1)}, bf16[4,256,512]{2,1,0:T(8,128)(2,1)}, u32[]{:S(2)}, u32[]{:S(2)}) collective-permute-start(bf16[4,256,512]{2,1,0:T(8,128)(2,1)} %collective-permute-done.39.refs_21_.refs_23_), channel_id=1, source_target_pairs={{0,16},{1,17},{2,18},{3,19},{4,20},{5,21},{6,22},{7,23},{8,24},{9,... | collective-permute-start | bytes 3145736 | tf_op jit(solution)/shard_map/ppermute | solution.py:49
  144.8 27.2 %collective-permute-start.42 = (bf16[4,256,512]{2,1,0:T(8,128)(2,1)}, bf16[4,256,512]{2,1,0:T(8,128)(2,1)}, u32[]{:S(2)}, u32[]{:S(2)}) collective-permute-start(bf16[4,256,512]{2,1,0:T(8,128)(2,1)} %collective-permute-done.41.refs_23_.refs_25_), channel_id=1, source_target_pairs={{0,16},{1,17},{2,18},{3,19},{4,20},{5,21},{6,22},{7,23},{8,24},{9,... | collective-permute-start | bytes 3145736 | tf_op jit(solution)/shard_map/ppermute | solution.py:49
  166.0 5.9 %collective-permute-start.44 = (bf16[4,256,512]{2,1,0:T(8,128)(2,1)}, bf16[4,256,512]{2,1,0:T(8,128)(2,1)}, u32[]{:S(2)}, u32[]{:S(2)}) collective-permute-start(bf16[4,256,512]{2,1,0:T(8,128)(2,1)} %collective-permute-done.43.refs_25_.refs_27_), channel_id=1, source_target_pairs={{0,16},{1,17},{2,18},{3,19},{4,20},{5,21},{6,22},{7,23},{8,24},{9,... | collective-permute-start | bytes 3145736 | tf_op jit(solution)/shard_map/ppermute | solution.py:49
  186.3 12.8 %collective-permute-start.45 = (bf16[32,8192]{1,0:T(8,128)(2,1)S(1)}, bf16[32,8192]{1,0:T(8,128)(2,1)S(1)}, u32[]{:S(2)}, u32[]{:S(2)}) collective-permute-start(bf16[32,8192]{1,0:T(8,128)(2,1)S(1)} %get-tuple-element.24), channel_id=1, source_target_pairs={{0,96},{1,97},{2,98},{3,99},{4,100},{5,101},{6,102},{7,103},{8,104... | collective-permute-start | bytes 1572872 | tf_op jit(solution)/shard_map/ppermute | solution.py:49
  199.3 0.7 collective-permute-start.46
  200.5 7.4 %collective-permute-start.47 = (bf16[32,8192]{1,0:T(8,128)(2,1)}, bf16[32,8192]{1,0:T(8,128)(2,1)S(1)}, u32[]{:S(2)}, u32[]{:S(2)}) collective-permute-start(bf16[32,8192]{1,0:T(8,128)(2,1)} %get-tuple-element.32), channel_id=1, source_target_pairs={{128,224},{129,225},{130,226},{131,227},{132,228},{133,229},{134,2... | collective-permute-start | bytes 1572872 | tf_op jit(solution)/shard_map/ppermute | solution.py:49
  207.2 1.0 collective-permute-start.51
  208.4 0.7 collective-permute-start.52
  209.3 0.7 collective-permute-start.53
  210.4 169.5 %collective-permute-start.54 = (bf16[32,8192]{1,0:T(8,128)(2,1)S(1)}, bf16[32,8192]{1,0:T(8,128)(2,1)S(1)}, u32[]{:S(2)}, u32[]{:S(2)}) collective-permute-start(bf16[32,8192]{1,0:T(8,128)(2,1)S(1)} %get-tuple-element.43), channel_id=1, source_target_pairs={{64,32},{65,33},{66,34},{67,35},{68,36},{69,37},{70,38},{71,39},{7... | collective-permute-start | bytes 1572872 | tf_op jit(solution)/shard_map/ppermute | solution.py:49
  212.0 195.9 %collective-permute-start.48 = (bf16[2,32,8448]{2,1,0:T(8,128)(2,1)S(1)}, bf16[2,32,8448]{2,1,0:T(8,128)(2,1)S(1)}, u32[]{:S(2)}, u32[]{:S(2)}) collective-permute-start(bf16[2,32,8448]{2,1,0:T(8,128)(2,1)S(1)} %get-tuple-element.54), channel_id=1, source_target_pairs={{0,16},{1,17},{2,18},{3,19},{4,20},{5,21},{6,22},{7,23},{8,24},{9,... | collective-permute-start | bytes 3244040 | tf_op jit(solution)/shard_map/ppermute | solution.py:49
  404.2 6.0 %collective-permute-start.55 = (bf16[2,32,8448]{2,1,0:T(8,128)(2,1)S(1)}, bf16[2,32,8448]{2,1,0:T(8,128)(2,1)S(1)}, u32[]{:S(2)}, u32[]{:S(2)}) collective-permute-start(bf16[2,32,8448]{2,1,0:T(8,128)(2,1)S(1)} %get-tuple-element.58), channel_id=1, source_target_pairs={{0,16},{1,17},{2,18},{3,19},{4,20},{5,21},{6,22},{7,23},{8,24},{9,... | collective-permute-start | bytes 3244040 | tf_op jit(solution)/shard_map/ppermute | solution.py:49
  409.0 25.7 %collective-permute-start.49 = (bf16[64,8448]{1,0:T(8,128)(2,1)}, bf16[64,8448]{1,0:T(8,128)(2,1)S(1)}, u32[]{:S(2)}, u32[]{:S(2)}) collective-permute-start(bf16[64,8448]{1,0:T(8,128)(2,1)} %get-tuple-element.53), channel_id=1, source_target_pairs={{0,32},{1,33},{2,34},{3,35},{4,36},{5,37},{6,38},{7,39},{8,40},{9,... | collective-permute-start | bytes 3244040 | tf_op jit(solution)/shard_map/ppermute | solution.py:49
  411.7 46.3 %collective-permute-start.56 = (bf16[64,8448]{1,0:T(8,128)(2,1)}, bf16[64,8448]{1,0:T(8,128)(2,1)}, u32[]{:S(2)}, u32[]{:S(2)}) collective-permute-start(bf16[64,8448]{1,0:T(8,128)(2,1)} %get-tuple-element.57), channel_id=1, source_target_pairs={{0,32},{1,33},{2,34},{3,35},{4,36},{5,37},{6,38},{7,39},{8,40},{9,... | collective-permute-start | bytes 3244040 | tf_op jit(solution)/shard_map/ppermute | solution.py:49
  478.0 25.4 %collective-permute-start.50 = (bf16[128,4352]{1,0:T(8,128)(2,1)S(1)}, bf16[128,4352]{1,0:T(8,128)(2,1)S(1)}, u32[]{:S(2)}, u32[]{:S(2)}) collective-permute-start(bf16[128,4352]{1,0:T(8,128)(2,1)S(1)} %pad_maximum_fusion.9), channel_id=1, source_target_pairs={{0,1},{1,0},{2,3},{3,2},{4,5},{5,4},{6,7},{7,6},{8,9},{9,8},{10,11... | collective-permute-start | bytes 3342344 | tf_op jit(solution)/shard_map/ppermute | solution.py:49
  480.1 47.1 %collective-permute-start.57 = (bf16[128,4352]{1,0:T(8,128)(2,1)S(1)}, bf16[128,4352]{1,0:T(8,128)(2,1)S(1)}, u32[]{:S(2)}, u32[]{:S(2)}) collective-permute-start(bf16[128,4352]{1,0:T(8,128)(2,1)S(1)} %pad_maximum_fusion.10), channel_id=1, source_target_pairs={{0,1},{1,0},{2,3},{3,2},{4,5},{5,4},{6,7},{7,6},{8,9},{9,8},{10,11... | collective-permute-start | bytes 3342344 | tf_op jit(solution)/shard_map/ppermute | solution.py:49
  531.3 55.0 %copy-start.1 = (bf16[2,4,16,8192]{3,2,1,0:T(8,128)(2,1)S(1)}, bf16[2,4,16,8192]{3,2,1,0:T(8,128)(2,1)}, u32[]{:S(2)}) copy-start(bf16[2,4,16,8192]{3,2,1,0:T(8,128)(2,1)} %param.4) | copy-start | bytes 6291460
  (17 other events, 199.4 us)
Sparse Core Ops, SparseCore 0:
  531.4 50.5 reduce-scatter.1

commit v2 on v1

v2 whole, which is shorter than its diff:
```python
import functools

import jax
import jax.numpy as jnp
from jax import lax
from jax.experimental import pallas as pl
from jax.experimental.pallas import tpu as pltpu
from jax.sharding import PartitionSpec as P

epsilon = 1e-05
root_half = 0.7071067811865476
inv_root_tau = 0.3989422804014327

BF = jnp.bfloat16
F32 = jnp.float32
BOTH = ("section", "dp")
WIDTH = 8192
RANK = 256
BLOCK = 512
BLOCKS = WIDTH // BLOCK
ROWS = 32
LAYERS = 4
HALF = WIDTH // 2
PACKED = HALF + RANK
MINOR = 48
MAJOR = RANK - MINOR
VMEM_LIMIT = 12 * 2**20
FIRST_LIMIT = 25 * 2**20

def unpack(section, dp):
    return section // 8, (section // 2) % 4, section % 2, dp // 2, dp % 2


def pack(x_hi, y, core, z, x_lo):
    return (x_hi * 8 + y * 2 + core) * 16 + z * 2 + x_lo


def pairs_of(target, keep=lambda *place: True):
    routes = []
    for section in range(16):
        for dp in range(16):
            place = unpack(section, dp)
            if keep(*place):
                routes.append((pack(*place), pack(*target(*place))))
    return routes


def send(value, target, keep=lambda *place: True):
    return lax.ppermute(value, BOTH, pairs_of(target, keep))


def along_z(value, step):
    return send(value, lambda xh, y, c, z, x: (xh, y, c, (z + step) % 8, x))


def to_core(value):
    return send(value, lambda xh, y, c, z, x: (xh, y, 1 - c, z, x))


def to_y(value):
    return send(value, lambda xh, y, c, z, x: (xh, y ^ 1, c, z, x))


def to_x(value):
    return send(value, lambda xh, y, c, z, x: (xh, y, c, z, 1 - x))


def to_first(value):
    return send(
        value,
        lambda xh, y, c, z, x: (xh, y, c, z, 1 - x) if c == 0 else (xh, y ^ 1, c, z, x),
    )


def to_second(value):
    return send(
        value,
        lambda xh, y, c, z, x: (xh, y ^ 1, c, z, x) if c == 0 else (xh, y, c, z, 1 - x),
    )


def exchange_pair(block):
    first = to_first(block)
    second = to_second(block)
    third = to_second(first)
    return jnp.stack([block, first, second, third])


def noop_kernel(*refs):
    pass


def after(value, *needed):
    return pl.pallas_call(
        noop_kernel,
        out_shape=jax.ShapeDtypeStruct(value.shape, value.dtype),
        in_specs=any_specs(1 + len(needed)),
        out_specs=pl.BlockSpec(memory_space=pltpu.HBM),
        input_output_aliases={0: 0},
        compiler_params=pltpu.CompilerParams(vmem_limit_bytes=VMEM_LIMIT),
    )(value, *needed)


def hop_forward(value, stage):
    if stage == 1:
        return send(
            value,
            lambda xh, y, c, z, x: (1, 3 - y, c, z, 1 - x),
            lambda xh, y, c, z, x: xh == 0 and y >= 2,
        )
    return send(
        value,
        lambda xh, y, c, z, x: (xh, 3 - y, c, z, x),
        lambda xh, y, c, z, x: xh * 2 + y // 2 == stage,
    )


def hop_backward(value, stage):
    if stage == 2:
        return send(
            value,
            lambda xh, y, c, z, x: (0, 3 - y, c, z, 1 - x),
            lambda xh, y, c, z, x: xh == 1 and y < 2,
        )
    return send(
        value,
        lambda xh, y, c, z, x: (xh, 3 - y, c, z, x),
        lambda xh, y, c, z, x: xh * 2 + y // 2 == stage,
    )


def gelu_value(values):
    return 0.5 * values * (1.0 + lax.erf(values * root_half))


def gelu_slope(values):
    return 0.5 * (1.0 + lax.erf(values * root_half)) + values * inv_root_tau * jnp.exp(
        -0.5 * values * values
    )


def where_am_i():
    section = lax.axis_index("section")
    dp = lax.axis_index("dp")
    stage = section // 4
    return stage, (section // 2) % 2, section % 2, dp // 2, dp % 2


def span(block):
    return slice(block * BLOCK, (block + 1) * BLOCK)


def fetch(plan, sources, down, up, down_sem, up_sem):
    _, y_lo, core, z, x_lo = where_am_i()

    def copies(layer, offset):
        parity = layer % 2
        y_far = (layer // 2 + y_lo) % 2
        downs, ups = [], []
        for index, (kind, distances) in enumerate(plan):
            source = sources[2 * index + offset]
            for member, distance in enumerate(distances):
                for x_far in range(2):
                    entry = lax.select(parity == 0, x_far + 2 * y_far, y_far + 2 * x_far)
                    block = ((x_lo + x_far) % 2) * 8 + (z - distance + 8) % 8
                    if kind == "both":
                        downs.append(
                            (source.at[entry, member, pl.ds(0, BLOCK)], down.at[layer, block])
                        )
                        for side in range(2):
                            rows = pl.ds(BLOCK + side * MINOR, MINOR)
                            columns = pl.ds(side * RANK, RANK)
                            ups.append(
                                (
                                    source.at[entry, member, rows],
                                    up.at[layer, block, pl.ds(MAJOR, MINOR), columns],
                                )
                            )
                    else:
                        low, high = kind
                        ups.append(
                            (source.at[entry], up.at[layer, block, pl.ds(low, high - low)])
                        )
        return [pltpu.make_async_copy(a, b, down_sem.at[layer]) for a, b in downs] + [
            pltpu.make_async_copy(a, b, up_sem.at[layer]) for a, b in ups
        ]

    def one_layer(layer, carry):
        for offset in range(2):

            @pl.when((layer % 2 == core) == (offset == 0))
            def _():
                for copy in copies(layer, offset):
                    copy.start()

        return carry

    lax.fori_loop(0, LAYERS, one_layer, 0)


def fetched(layer, matrix, sem):
    pltpu.make_async_copy(matrix.at[layer], matrix.at[layer], sem.at[layer]).wait()


down_shape = (LAYERS, BLOCKS, BLOCK, RANK)
up_shape = (LAYERS, BLOCKS, RANK, BLOCK)


def in_vmem(number):
    return [pl.BlockSpec(memory_space=pltpu.VMEM)] * number


def any_specs(number):
    return [pl.BlockSpec(memory_space=pltpu.HBM)] * number


def pack_kernel(parts, *refs):
    sources, (target, sem) = refs[: len(parts)], refs[len(parts) :]
    copies = []
    row = 0
    for index, (source, (place, count)) in enumerate(zip(sources, parts)):
        copies.append(
            pltpu.make_async_copy(
                source.at[place], target.at[pl.ds(row, count)], sem.at[index]
            )
        )
        row += count
    for copy in copies:
        copy.start()
    for copy in copies:
        copy.wait()


def packed_rows(*parts):
    arrays = [array for array, _ in parts]
    takes = [(place, array[place].shape[0]) for array, place in parts]
    shape = (sum(count for _, count in takes), *arrays[0][parts[0][1]].shape[1:])
    return pl.pallas_call(
        functools.partial(pack_kernel, takes),
        out_shape=jax.ShapeDtypeStruct(shape, BF),
        in_specs=any_specs(len(arrays)),
        out_specs=any_specs(1)[0],
        scratch_shapes=[pltpu.SemaphoreType.DMA((len(arrays),))],
        compiler_params=pltpu.CompilerParams(vmem_limit_bytes=4 * 2**20),
    )(*arrays)


def scatter(layer, wide, narrow, kept, sent, sem):
    _, y_lo, core, _, x_lo = where_am_i()
    parity = layer % 2
    y_far = (layer // 2 + y_lo) % 2

    def copies(target):
        made = []
        for half in range(2):
            x_far = (half + x_lo) % 2
            first = lax.select(parity == 0, x_far, y_far)
            second = lax.select(parity == 0, y_far, x_far)
            place = target.at[first, second]
            made.append((wide.at[:, half * HALF : (half + 1) * HALF], place.at[:, :HALF]))
            made.append((narrow, place.at[:, HALF:]))
        return [pltpu.make_async_copy(a, b, sem.at[i]) for i, (a, b) in enumerate(made)]

    def start():
        @pl.when(parity == core)
        def _():
            for copy in copies(kept):
                copy.start()

        @pl.when(parity != core)
        def _():
            for copy in copies(sent):
                copy.start()

    def wait():
        for copy in copies(kept):
            copy.wait()

    return start, wait


def first_kernel(plan, *refs):
    h_in, sources = refs[0], refs[1 : 1 + 2 * len(plan)]
    down, up, *rest = refs[1 + 2 * len(plan) :]
    *rest, down_sem, up_sem = rest
    fetch(plan, sources, down, up, down_sem, up_sem)
    compute_forward(
        0,
        h_in,
        down,
        up,
        *rest,
        ready=lambda layer: fetched(layer, down, down_sem),
        ready_up=lambda layer: fetched(layer, up, up_sem),
    )

    @pl.when(where_am_i()[0] != 0)
    def _():
        for layer in range(LAYERS):
            fetched(layer, down, down_sem)
            fetched(layer, up, up_sem)


def forward_kernel(stage, *refs):
    compute_forward(stage, *refs[:3], *refs[7:])


def compute_forward(
    stage,
    h_in,
    down,
    up,
    h_out,
    hidden,
    zs,
    kept,
    sent,
    normed_rows,
    active_rows,
    sem,
    ready=lambda layer: None,
    ready_up=lambda layer: None,
):
    @pl.when(where_am_i()[0] == stage)
    def _():
        hidden[0] = h_in[...]

        def one_layer(layer, carry):
            total = jnp.zeros((ROWS, BLOCK), F32)
            for block in range(BLOCKS):
                part = hidden[layer, :, span(block)].astype(F32)
                total += part * part
            mean = jnp.sum(total, axis=-1, keepdims=True) * (1.0 / WIDTH)
            scaling = lax.rsqrt(mean + epsilon)
            ready(layer)
            latent = jnp.zeros((ROWS, RANK), F32)
            for block in range(BLOCKS):
                part = hidden[layer, :, span(block)].astype(F32)
                normed = (part * scaling).astype(BF)
                normed_rows[layer, :, span(block)] = normed
                latent += jnp.dot(normed, down[layer, block], preferred_element_type=F32)
            active = gelu_value(latent).astype(BF)
            active_rows[layer] = active
            zs[layer, :, :RANK] = latent
            zs[layer, :, RANK:] = jnp.broadcast_to(scaling, (ROWS, 128))
            start, _ = scatter(
                layer, normed_rows.at[layer], active_rows.at[layer], kept, sent, sem.at[layer]
            )
            start()
            ready_up(layer)

            def passed_on(store):
                for block in range(BLOCKS):
                    part = hidden[layer, :, span(block)].astype(F32)
                    added = jnp.dot(active, up[layer, block], preferred_element_type=F32)
                    store(span(block), (part + added).astype(BF))

            def store_next(columns, value):
                hidden[layer + 1, :, columns] = value

            def store_last(columns, value):
                h_out[:, columns] = value

            @pl.when(layer < LAYERS - 1)
            def _():
                passed_on(store_next)

            @pl.when(layer == LAYERS - 1)
            def _():
                passed_on(store_last)

            return carry

        lax.fori_loop(0, LAYERS, one_layer, 0)

        def one_wait(layer, carry):
            _, wait = scatter(
                layer, normed_rows.at[layer], active_rows.at[layer], kept, sent, sem.at[layer]
            )
            wait()
            return carry

        lax.fori_loop(0, LAYERS, one_wait, 0)


def backward_kernel(stage, aliased, passes, *refs):
    c_in, hidden, zs, down, up = refs[:5]
    rest = refs[5 + (2 if aliased else 0) + passes :]
    c_out, kept, sent = rest[:3]
    cotangent, dlatent_rows, sem = rest[-3:]
    contract_last = (((1,), (1,)), ((), ()))

    @pl.when(where_am_i()[0] == stage)
    def _():
        cotangent[LAYERS - 1] = c_in[...]

        def one_layer(step, carry):
            layer = LAYERS - 1 - step
            dactive = jnp.zeros((ROWS, RANK), F32)
            for block in range(BLOCKS):
                dactive += lax.dot_general(
                    cotangent[layer, :, span(block)],
                    up[layer, block],
                    contract_last,
                    preferred_element_type=F32,
                )
            latent = zs[layer, :, :RANK]
            scaling = zs[layer, :, RANK:][:, :1]
            dlatent = (dactive * gelu_slope(latent)).astype(BF)
            dlatent_rows[layer] = dlatent
            inner = jnp.sum(dlatent.astype(F32) * latent, axis=-1, keepdims=True) * (1.0 / WIDTH)
            start, _ = scatter(
                layer, cotangent.at[layer], dlatent_rows.at[layer], kept, sent, sem.at[layer]
            )
            start()

            def passed_on(store):
                for block in range(BLOCKS):
                    unit_grad = lax.dot_general(
                        dlatent, down[layer, block], contract_last, preferred_element_type=F32
                    )
                    unit_rows = hidden[layer, :, span(block)].astype(F32) * scaling
                    passed = cotangent[layer, :, span(block)].astype(F32) + scaling * (
                        unit_grad - unit_rows * inner
                    )
                    store(span(block), passed.astype(BF))

            def store_next(columns, value):
                cotangent[layer - 1, :, columns] = value

            def store_last(columns, value):
                c_out[:, columns] = value

            @pl.when(layer > 0)
            def _():
                passed_on(store_next)

            @pl.when(layer == 0)
            def _():
                passed_on(store_last)

            return carry

        lax.fori_loop(0, LAYERS, one_layer, 0)

        def one_wait(layer, carry):
            _, wait = scatter(
                layer, cotangent.at[layer], dlatent_rows.at[layer], kept, sent, sem.at[layer]
            )
            wait()
            return carry

        lax.fori_loop(0, LAYERS, one_wait, 0)


row_shape = jax.ShapeDtypeStruct((ROWS, WIDTH), BF)
side_shape = pltpu.HBM((2, 2, ROWS, PACKED), BF)
cost = pl.CostEstimate(flops=2 * 10**9, bytes_accessed=40 * 2**20, transcendentals=10**5)


saved_shapes = (
    pltpu.VMEM((LAYERS, ROWS, WIDTH), BF),
    pltpu.VMEM((LAYERS, ROWS, RANK + 128), F32),
    side_shape,
    side_shape,
)


def row_scratch():
    return [
        pltpu.VMEM((LAYERS, ROWS, WIDTH), BF),
        pltpu.VMEM((LAYERS, ROWS, RANK), BF),
        pltpu.SemaphoreType.DMA((LAYERS, 4)),
    ]


def run_first(h_in, entries):
    plan = tuple(what for what, *_ in entries)
    operands = [h_in] + [array for _, *pair in entries for array in pair]
    down, up, h_out, *saved = pl.pallas_call(
        functools.partial(first_kernel, plan),
        out_shape=(
            pltpu.VMEM(down_shape, BF),
            pltpu.VMEM(up_shape, BF),
            row_shape,
            *saved_shapes,
        ),
        in_specs=in_vmem(1) + any_specs(len(operands) - 1),
        out_specs=tuple(in_vmem(5) + any_specs(2)),
        scratch_shapes=[
            *row_scratch(),
            pltpu.SemaphoreType.DMA((LAYERS,)),
            pltpu.SemaphoreType.DMA((LAYERS,)),
        ],
        compiler_params=pltpu.CompilerParams(vmem_limit_bytes=FIRST_LIMIT),
        cost_estimate=cost,
    )(*operands)
    return (down, up), h_out, saved


def run_forward(stage, h_in, weights, saved):
    return pl.pallas_call(
        functools.partial(forward_kernel, stage),
        out_shape=(row_shape, *saved_shapes),
        in_specs=in_vmem(5) + any_specs(2),
        out_specs=tuple(in_vmem(3) + any_specs(2)),
        scratch_shapes=row_scratch(),
        input_output_aliases={3 + i: 1 + i for i in range(4)},
        compiler_params=pltpu.CompilerParams(vmem_limit_bytes=VMEM_LIMIT),
        cost_estimate=cost,
    )(h_in, *weights, *saved)


def run_backward(stage, c_in, hidden, zs, weights, saved, passed=()):
    operands = [c_in, hidden, zs, *weights, *(saved or ()), *passed]
    first = 5 + len(saved or ())
    aliases = {5: 1, 6: 2} if saved else {}
    aliases.update({first + i: 3 + i for i in range(len(passed))})
    return pl.pallas_call(
        functools.partial(backward_kernel, stage, saved is not None, len(passed)),
        out_shape=(
            row_shape,
            side_shape,
            side_shape,
            *[jax.ShapeDtypeStruct(p.shape, p.dtype) for p in passed],
        ),
        in_specs=in_vmem(5) + any_specs(first - 5 + len(passed)),
        out_specs=tuple(in_vmem(1) + any_specs(2 + len(passed))),
        scratch_shapes=[
            pltpu.VMEM((LAYERS, ROWS, WIDTH), BF),
            pltpu.VMEM((LAYERS, ROWS, RANK), BF),
            pltpu.SemaphoreType.DMA((LAYERS, 4)),
        ],
        input_output_aliases=aliases,
        compiler_params=pltpu.CompilerParams(vmem_limit_bytes=VMEM_LIMIT),
        cost_estimate=cost,
    )(*operands)


def ring(block):
    held = {0: block}
    for step in range(1, 5):
        held[step] = along_z(held[step - 1], 1)
        if step < 4:
            held[-step] = along_z(held[1 - step], -1)
    return held


def gather_weights(down_shard, up_shard, needed):
    minor = up_shard[MAJOR:]
    packed = jnp.concatenate([down_shard, minor[:, :RANK], minor[:, RANK:]], axis=0)
    major = ring(exchange_pair(up_shard[:MAJOR]))
    small = ring(packed)
    entries = []
    for members in ((0,), (1, -1), (2, -2), (3, -3), (4,)):
        block = jnp.stack([small[k] for k in members])
        if members[0] == 2:
            block = after(block, *needed)
        full = exchange_pair(block)
        entries.append((("both", members), full, to_core(full)))
    for k in (0, 1, -1, 2, -2, 3, -3, 4):
        entries.append((((0, MAJOR), (k,)), major[k], to_core(major[k])))
    return entries


def exchange(kept, sent):
    other = to_core(sent)
    near = to_first(packed_rows((kept, (1,))))
    far = to_first(packed_rows((other, (1,))))
    outgoing = packed_rows((kept, (0, 1)), (other, (0, 1)), (near, (1,)), (far, (1,)))
    arrived = to_second(outgoing)
    return packed_rows(
        (kept, (0, 0)),
        (other, (0, 0)),
        (near, (0,)),
        (far, (0,)),
        (arrived, ()),
    )


def pick(value, index):
    return lax.dynamic_index_in_dim(value, index, 0, keepdims=False)


def body(entering, cotangent, down_proj, up_proj):
    section = lax.axis_index("section")
    y_lo, core = (section // 2) % 2, section % 2

    def own_rows(array, half):
        chosen = pick(array, core).reshape(2, ROWS, 8, 2, BLOCK)
        return pick(chosen, half).swapaxes(1, 2).reshape(ROWS, WIDTH)

    hidden = own_rows(entering, y_lo)
    seeds = own_rows(cotangent, 1 - y_lo)
    entries = gather_weights(down_proj[0], up_proj[0], (hidden, seeds))

    weights, hidden, saved = run_first(hidden, entries)
    incoming = send(
        after(seeds, saved[2]),
        lambda xh, y, c, z, x: (xh, y, c, z, 1 - x),
        lambda xh, y, c, z, x: xh == 1 and y >= 2,
    )
    for stage in range(4):
        if stage > 0:
            hidden, *saved = run_forward(stage, hidden, weights, saved)
        if stage < 3:
            hidden = hop_forward(hidden, stage)
    h_save, zs_save, *sides = saved

    saved = None
    for stage in (3, 2, 1, 0):
        passed = ()
        if stage == 1:
            passed = sides
        if stage == 0:
            passed = (normed,)
        incoming, *saved = run_backward(
            stage, incoming, h_save, zs_save, weights, saved, passed
        )
        saved, passed = saved[:2], saved[2:]
        if stage > 0:
            incoming = hop_backward(incoming, stage)
        if stage == 1:
            normed = exchange(*passed)
    normed = passed[0]
    cotangents = exchange(*saved)

    contract_rows = (((0,), (0,)), ((), ()))

    def partial(wide, narrow):
        return lax.dot_general(
            wide[:, :HALF], narrow[:, HALF:], contract_rows, preferred_element_type=F32
        )

    pieces = jnp.concatenate([partial(normed, cotangents), partial(cotangents, normed)], axis=1)
    groups = [[x + 2 * z for z in range(8)] for x in range(2)]
    totals = lax.psum_scatter(
        pieces.astype(BF), "dp", scatter_dimension=0, axis_index_groups=groups, tiled=True
    ).astype(F32)
    return (totals[:, :RANK][None], totals[:, RANK:].T[None])


def solution(mesh):
    return jax.shard_map(
        body,
        mesh=mesh,
        in_specs=(
            P(None, None, "dp", None),
            P(None, None, "dp", None),
            P("section", "dp", None),
            P("section", None, "dp"),
        ),
        out_specs=(P("section", "dp", None), P("section", None, "dp")),
        check_vma=False,
    )
```

time: 603 us -> 488 us (0.81)
  waiting for transfers between devices: 408 us -> 305 us
  Pallas kernels: 38.2 us -> 30.4 us
    ppermute x58 -> x60, waiting for transfers between devices: 358 us -> 256 us  [send(): return lax.ppermute(value, BOTH, pairs_of(target, keep))]
    unnamed x51 -> x87, local copies, waits for them, and re-layouts: 10.3 us -> 31.7 us
    another operation x1 -> x0, local copies, waits for them, and re-layouts: 11.5 us -> none
    pallas_call x4, Pallas kernels: 23.4 us -> 12.4 us  [run_backward(): pl.pallas_call(functools.partial(backward_kernel, stage, saved is not Non...]
    reshape x2 -> x0, local copies, waits for them, and re-layouts: 7.79 us -> none  [exchange(): wide = rows[:, :WIDTH].reshape(4 * ROWS, 2, WIDTH // 2).swapaxes(0, 1)]
    pallas_call x4 -> x14, Pallas kernels: 14.8 us -> 18 us  [the longest x1 15 us: run_first(): pl.pallas_call(functools.partial(first_kernel, plan), out_shape=(pltpu.VM...]
    ppermute x58 -> x60, starting transfers between devices: 72.6 us -> 72.5 us  [send(): return lax.ppermute(value, BOTH, pairs_of(target, keep))]
  transfers between devices with their start and end apart: 59 -> 61, of which waited for: 25 -> 26; matrix products, arithmetic and copies ran while one was open for 5% -> 3% of each run, Pallas kernels for 4% -> 0%
where the time goes in v2:
time: 488 us; the launch traced here: 479 us
  waiting for transfers between devices  305 us (62%)
  starting transfers between devices  72.6 us (15%)
  local copies, waits for them, and re-layouts  39.4 us (8%)
  Pallas kernels  30.4 us (6%)
  between operations  15.3 us (3%)
  other arithmetic  14.5 us (3%)
    ppermute x60, waiting for transfers between devices, send(): return lax.ppermute(value, BOTH, pairs_of(target, keep))  256 us
    ppermute x60, starting transfers between devices, send(): return lax.ppermute(value, BOTH, pairs_of(target, keep))  72.5 us
    reduce_scatter x1, waiting for transfers between devices, body(): lax.psum_scatter(pieces.astype(BF), 'dp', scatter_dimension=0, axis_index...  49.4 us
    unnamed x87, local copies, waits for them, and re-layouts  31.7 us
    pallas_call x1, Pallas kernels, run_first(): pl.pallas_call(functools.partial(first_kernel, plan), out_shape=(pltpu.VM...  15 us
    pallas_call x4, Pallas kernels, run_backward(): pl.pallas_call(functools.partial(backward_kernel, stage, saved is not Non...  12.4 us
  transfers between devices with their start and end apart: 61, of which 26 were waited for; matrix products, arithmetic and copies ran while one was open for 3% of the time, Pallas kernels for 0%

profile of v2, /device:TPU:1, one launch (start us, length us, event | category | flops | bytes accessed | tf_op | source)
XLA Modules:
  0.0 478.8 jit_solution(6324837277971567248)
XLA Ops:
  8.0 1.7 pad_maximum_fusion.10
  9.7 6.4 %collective-permute-start.5 = (bf16[608,256]{1,0:T(8,128)(2,1)S(1)}, bf16[608,256]{1,0:T(8,128)(2,1)}, u32[]{:S(2)}, u32[]{:S(2)}) collective-permute-start(bf16[608,256]{1,0:T(8,128)(2,1)S(1)} %get-tuple-element.84), channel_id=1, source_target_pairs={{0,14},{1,15},{2,0},{3,1},{4,2},{5,3},{6,4},{7,5},{8,6},{9,7},{10,... | collective-permute-start | bytes 933896 | tf_op jit(solution)/shard_map/ppermute | solution.py:49
  17.1 1.4 collective-permute-start.27
  18.5 1.2 collective-permute-start.1
  19.9 5.4 %collective-permute-done.4 = bf16[608,256]{1,0:T(8,128)(2,1)S(1)} collective-permute-done((bf16[608,256]{1,0:T(8,128)(2,1)S(1)}, bf16[608,256]{1,0:T(8,128)(2,1)S(1)}, u32[]{:S(2)}, u32[]{:S(2)}) %collective-permute-start.4) | collective-permute-done | bytes 311328 | tf_op jit(solution)/shard_map/ppermute | solution.py:49
  25.3 1.2 collective-permute-start.28
  26.8 2.1 fusion.5
  28.8 3.7 collective-permute-done.28
  32.6 1.2 collective-permute-start.7
  33.9 2.7 collective-permute-start.11
  36.7 1.7 constant_dynamic-slice_fusion.1
  39.6 1.2 constant_dynamic-slice_fusion
  41.6 3.0 collective-permute-start.17
  47.4 4.8 %collective-permute-done.2 = bf16[1,608,256]{2,1,0:T(8,128)(2,1)} collective-permute-done((bf16[1,608,256]{2,1,0:T(8,128)(2,1)}, bf16[1,608,256]{2,1,0:T(8,128)(2,1)}, u32[]{:S(2)}, u32[]{:S(2)}) %collective-permute-start.2) | collective-permute-done | bytes 311328 | tf_op jit(solution)/shard_map/ppermute | solution.py:49
  52.3 1.2 collective-permute-start.13
  54.6 2.8 collective-permute-start.33
  58.9 1.2 pad_maximum_fusion.4.refs_1_
  60.1 1.6 collective-permute-done.13
  61.7 2.7 collective-permute-start.3
  64.4 4.8 collective-permute-done.12
  69.2 1.2 collective-permute-start.24
  71.5 3.9 collective-permute-done.33.refs_15_
  75.4 2.0 collective-permute-start.18
  78.5 1.5 collective-permute-start.8
  80.0 2.0 collective-permute-start.23
  82.0 12.0 %collective-permute-done.23 = bf16[1,608,256]{2,1,0:T(8,128)(2,1)S(1)} collective-permute-done((bf16[1,608,256]{2,1,0:T(8,128)(2,1)S(1)}, bf16[1,608,256]{2,1,0:T(8,128)(2,1)S(1)}, u32[]{:S(2)}, u32[]{:S(2)}) %collective-permute-start.23) | collective-permute-done | bytes 311328 | tf_op jit(solution)/shard_map/ppermute | solution.py:49
  94.0 6.3 %collective-permute-start.37 = (bf16[4,208,512]{2,1,0:T(8,128)(2,1)S(1)}, bf16[4,208,512]{2,1,0:T(8,128)(2,1)S(1)}, u32[]{:S(2)}, u32[]{:S(2)}) collective-permute-start(bf16[4,208,512]{2,1,0:T(8,128)(2,1)S(1)} %collective-permute-done.33.refs_15_), channel_id=1, source_target_pairs={{0,14},{1,15},{2,0},{3,1},{4,2},{5,3},{6,4},{7,5},{8,6},{9,7},{10,... | collective-permute-start | bytes 2555912 | tf_op jit(solution)/shard_map/ppermute | solution.py:49
  100.3 2.8 collective-permute-done.8
  103.1 2.3 collective-permute-start.34
  106.8 7.0 %collective-permute-done.37.refs_19_ = bf16[4,208,512]{2,1,0:T(8,128)(2,1)S(1)} collective-permute-done((bf16[4,208,512]{2,1,0:T(8,128)(2,1)S(1)}, bf16[4,208,512]{2,1,0:T(8,128)(2,1)S(1)}, u32[]{:S(2)}, u32[]{:S(2)}) %collective-permute-start.37) | collective-permute-done | bytes 852000 | tf_op jit(solution)/shard_map/ppermute | solution.py:49
  113.8 3.4 collective-permute-start.41
  117.2 7.4 %collective-permute-start.38 = (bf16[4,208,512]{2,1,0:T(8,128)(2,1)S(1)}, bf16[4,208,512]{2,1,0:T(8,128)(2,1)S(1)}, u32[]{:S(2)}, u32[]{:S(2)}) collective-permute-start(bf16[4,208,512]{2,1,0:T(8,128)(2,1)S(1)} %collective-permute-done.37.refs_19_), channel_id=1, source_target_pairs={{0,16},{1,17},{2,18},{3,19},{4,20},{5,21},{6,22},{7,23},{8,24},{9,... | collective-permute-start | bytes 2555912 | tf_op jit(solution)/shard_map/ppermute | solution.py:49
  125.9 1.6 pad_maximum_fusion.1.refs_3_
  127.9 6.2 %collective-permute-done.20 = bf16[2,608,256]{2,1,0:T(8,128)(2,1)S(1)} collective-permute-done((bf16[2,608,256]{2,1,0:T(8,128)(2,1)S(1)}, bf16[2,608,256]{2,1,0:T(8,128)(2,1)S(1)}, u32[]{:S(2)}, u32[]{:S(2)}) %collective-permute-start.20) | collective-permute-done | bytes 622624 | tf_op jit(solution)/shard_map/ppermute | solution.py:49
  135.4 2.3 collective-permute-start.9
  137.8 8.5 %collective-permute-done.39.refs_21_ = bf16[4,208,512]{2,1,0:T(8,128)(2,1)S(1)} collective-permute-done((bf16[4,208,512]{2,1,0:T(8,128)(2,1)S(1)}, bf16[4,208,512]{2,1,0:T(8,128)(2,1)S(1)}, u32[]{:S(2)}, u32[]{:S(2)}) %collective-permute-start.39) | collective-permute-done | bytes 852000 | tf_op jit(solution)/shard_map/ppermute | solution.py:49
  147.3 5.4 %collective-permute-done.42.refs_24_ = bf16[4,208,512]{2,1,0:T(8,128)(2,1)S(1)} collective-permute-done((bf16[4,208,512]{2,1,0:T(8,128)(2,1)S(1)}, bf16[4,208,512]{2,1,0:T(8,128)(2,1)S(1)}, u32[]{:S(2)}, u32[]{:S(2)}) %collective-permute-start.42) | collective-permute-done | bytes 852000 | tf_op jit(solution)/shard_map/ppermute | solution.py:49
  153.1 15.5 %collective-permute-done.43.refs_25_ = bf16[4,208,512]{2,1,0:T(8,128)(2,1)S(1)} collective-permute-done((bf16[4,208,512]{2,1,0:T(8,128)(2,1)S(1)}, bf16[4,208,512]{2,1,0:T(8,128)(2,1)S(1)}, u32[]{:S(2)}, u32[]{:S(2)}) %collective-permute-start.43) | collective-permute-done | bytes 852000 | tf_op jit(solution)/shard_map/ppermute | solution.py:49
  168.6 1.2 collective-permute-start.44
  172.4 1.4 copy-done.18
  173.9 15.0 %shard_map.60 = (bf16[4,16,512,256]{3,2,1,0:T(8,128)(2,1)S(1)}, bf16[4,16,256,512]{3,2,1,0:T(8,128)(2,1)S(1)}, bf16[32,8192]{1,0:T(8,128)(2,1)}, bf16[4,32,8192]...) custom-call(bf16[32,8192]{1,0:T(8,128)(2,1)} %bitcast.64, ...), custom_call_target="tpu_custom_call" | custom-call | flops 2000000000 | bytes 41943040 | tf_op jit(solution)/shard_map/pallas_call | solution.py:480
  188.9 5.8 %copy-done = bf16[4,16,512,256]{3,2,1,0:T(8,128)(2,1)} copy-done((bf16[4,16,512,256]{3,2,1,0:T(8,128)(2,1)}, bf16[4,16,512,256]{3,2,1,0:T(8,128)(2,1)S(1)}, u32[]{:S(2)}) %copy-start) | copy-done | bytes 16777240
  194.8 5.7 %copy-done.2 = bf16[4,16,256,512]{3,2,1,0:T(8,128)(2,1)} copy-done((bf16[4,16,256,512]{3,2,1,0:T(8,128)(2,1)}, bf16[4,16,256,512]{3,2,1,0:T(8,128)(2,1)S(1)}, u32[]{:S(2)}) %copy-start.2) | copy-done | bytes 16777240
  200.5 1.7 collective-permute-start.46
  202.2 1.2 copy-done.4
  203.5 10.1 %collective-permute-done.46.refs_0_ = bf16[32,8192]{1,0:T(8,128)(2,1)S(1)} collective-permute-done((bf16[32,8192]{1,0:T(8,128)(2,1)}, bf16[32,8192]{1,0:T(8,128)(2,1)S(1)}, u32[]{:S(2)}, u32[]{:S(2)}) %collective-permute-start.46) | collective-permute-done | bytes 524320 | tf_op jit(solution)/shard_map/ppermute | solution.py:49
  213.6 5.8 %copy-done.1 = bf16[4,16,512,256]{3,2,1,0:T(8,128)(2,1)S(1)} copy-done((bf16[4,16,512,256]{3,2,1,0:T(8,128)(2,1)S(1)}, bf16[4,16,512,256]{3,2,1,0:T(8,128)(2,1)}, u32[]{:S(2)}) %copy-start.1) | copy-done | bytes 16777240
  219.3 5.8 %copy-done.3 = bf16[4,16,256,512]{3,2,1,0:T(8,128)(2,1)S(1)} copy-done((bf16[4,16,256,512]{3,2,1,0:T(8,128)(2,1)S(1)}, bf16[4,16,256,512]{3,2,1,0:T(8,128)(2,1)}, u32[]{:S(2)}) %copy-start.3) | copy-done | bytes 16777240
  233.0 2.0 collective-permute-done.52.refs_0_.refs_1_
  235.3 6.0 %collective-permute-done.53.refs_2_ = bf16[2,32,4352]{2,1,0:T(8,128)(2,1)S(1)} collective-permute-done((bf16[2,32,4352]{2,1,0:T(8,128)(2,1)S(1)}, bf16[2,32,4352]{2,1,0:T(8,128)(2,1)S(1)}, u32[]{:S(2)}, u32[]{:S(2)}) %collective-permute-start.53) | collective-permute-done | bytes 557088 | tf_op jit(solution)/shard_map/ppermute | solution.py:49
  241.4 6.0 %collective-permute-done.54.refs_3_ = bf16[2,32,4352]{2,1,0:T(8,128)(2,1)S(1)} collective-permute-done((bf16[2,32,4352]{2,1,0:T(8,128)(2,1)S(1)}, bf16[2,32,4352]{2,1,0:T(8,128)(2,1)S(1)}, u32[]{:S(2)}, u32[]{:S(2)}) %collective-permute-start.54) | collective-permute-done | bytes 557088 | tf_op jit(solution)/shard_map/ppermute | solution.py:49
  247.6 1.5 collective-permute-start.55
  249.0 1.3 collective-permute-start.51
  250.3 12.2 %collective-permute-done.55.refs_4_ = bf16[128,4352]{1,0:T(8,128)(2,1)S(1)} collective-permute-done((bf16[128,4352]{1,0:T(8,128)(2,1)S(1)}, bf16[128,4352]{1,0:T(8,128)(2,1)S(1)}, u32[]{:S(2)}, u32[]{:S(2)}) %collective-permute-start.55) | collective-permute-done | bytes 1114144 | tf_op jit(solution)/shard_map/ppermute | solution.py:49
  262.9 107.3 %collective-permute-done.51.refs_0_ = bf16[32,8192]{1,0:T(8,128)(2,1)S(1)} collective-permute-done((bf16[32,8192]{1,0:T(8,128)(2,1)S(1)}, bf16[32,8192]{1,0:T(8,128)(2,1)S(1)}, u32[]{:S(2)}, u32[]{:S(2)}) %collective-permute-start.51) | collective-permute-done | bytes 524320 | tf_op jit(solution)/shard_map/ppermute | solution.py:49
  370.2 11.9 %shard_map.72 = (bf16[32,8192]{1,0:T(8,128)(2,1)}, bf16[2,2,32,4352]{3,2,1,0:T(8,128)(2,1)}, bf16[2,2,32,4352]{3,2,1,0:T(8,128)(2,1)}, bf16[256,4352]{1,0:T(8,128)(2,1)S(1)}) custom-call(bf16[32,8192]{1,0:T(8,128)(2,1)S(1)} %collective-permute-done.51.refs_0_, ...), custom_call_target="tpu_custom_call", output_to_operand_aliasing={{1}: (5, {}), {2}: (6, {}), {3}: (7, {})} | custom-call | flops 2000000000 | bytes 41943040 | tf_op jit(solution)/shard_map/pallas_call | solution.py:519
  382.1 1.5 collective-permute-start.56
  383.7 1.2 copy-done.6
  386.8 7.0 %collective-permute-done.57.refs_2_ = bf16[2,32,4352]{2,1,0:T(8,128)(2,1)S(1)} collective-permute-done((bf16[2,32,4352]{2,1,0:T(8,128)(2,1)S(1)}, bf16[2,32,4352]{2,1,0:T(8,128)(2,1)S(1)}, u32[]{:S(2)}, u32[]{:S(2)}) %collective-permute-start.57) | collective-permute-done | bytes 557088 | tf_op jit(solution)/shard_map/ppermute | solution.py:49
  393.8 6.0 %collective-permute-done.58.refs_3_ = bf16[2,32,4352]{2,1,0:T(8,128)(2,1)S(1)} collective-permute-done((bf16[2,32,4352]{2,1,0:T(8,128)(2,1)S(1)}, bf16[2,32,4352]{2,1,0:T(8,128)(2,1)S(1)}, u32[]{:S(2)}, u32[]{:S(2)}) %collective-permute-start.58) | collective-permute-done | bytes 557088 | tf_op jit(solution)/shard_map/ppermute | solution.py:49
  400.6 14.1 %collective-permute-done.59.refs_4_ = bf16[128,4352]{1,0:T(8,128)(2,1)S(1)} collective-permute-done((bf16[128,4352]{1,0:T(8,128)(2,1)S(1)}, bf16[128,4352]{1,0:T(8,128)(2,1)S(1)}, u32[]{:S(2)}, u32[]{:S(2)}) %collective-permute-start.59) | collective-permute-done | bytes 1114144 | tf_op jit(solution)/shard_map/ppermute | solution.py:49
  416.6 2.5 pad_maximum_fusion
  419.1 49.4 %reduce-scatter.2.cloned.1.call-done = bf16[512,512]{0,1:T(8,128)(2,1)} async-done(((bf16[4096,512]{0,1:T(8,128)(2,1)}), bf16[512,512]{0,1:T(8,128)(2,1)}) %reduce-scatter.2.cloned.1.call-update) | async-done | bytes 524304 | tf_op jit(solution)/shard_map/reduce_scatter | solution.py:637
  468.5 1.2 convert_element_type.4
  (189 shorter events, 35.1 us)
Async XLA Ops:
  7.2 461.3 %reduce-scatter.2.cloned.1.call-start = ((), (), s32[]{:S(2)}) async-start(), calls=%async_computation.1 | async-start | bytes 4718592 | tf_op jit(solution)/shard_map/reduce_scatter | solution.py:637
  9.7 16.7 %collective-permute-start.5 = (bf16[608,256]{1,0:T(8,128)(2,1)S(1)}, bf16[608,256]{1,0:T(8,128)(2,1)}, u32[]{:S(2)}, u32[]{:S(2)}) collective-permute-start(bf16[608,256]{1,0:T(8,128)(2,1)S(1)} %get-tuple-element.84), channel_id=1, source_target_pairs={{0,14},{1,15},{2,0},{3,1},{4,2},{5,3},{6,4},{7,5},{8,6},{9,7},{10,... | collective-permute-start | bytes 933896 | tf_op jit(solution)/shard_map/ppermute | solution.py:49
  16.2 9.1 %collective-permute-start.4 = (bf16[608,256]{1,0:T(8,128)(2,1)S(1)}, bf16[608,256]{1,0:T(8,128)(2,1)S(1)}, u32[]{:S(2)}, u32[]{:S(2)}) collective-permute-start(bf16[608,256]{1,0:T(8,128)(2,1)S(1)} %get-tuple-element.84), channel_id=1, source_target_pairs={{0,2},{1,3},{2,4},{3,5},{4,6},{5,7},{6,8},{7,9},{8,10},{9,11},{10,... | collective-permute-start | bytes 933896 | tf_op jit(solution)/shard_map/ppermute | solution.py:49
  17.1 8.2 %collective-permute-start.27 = (bf16[208,512]{1,0:T(8,128)(2,1)S(1)}, bf16[208,512]{1,0:T(8,128)(2,1)}, u32[]{:S(2)}, u32[]{:S(2)}) collective-permute-start(bf16[208,512]{1,0:T(8,128)(2,1)S(1)} %get-tuple-element.88), channel_id=1, source_target_pairs={{0,1},{1,0},{2,3},{3,2},{4,5},{5,4},{6,7},{7,6},{8,9},{9,8},{10,11... | collective-permute-start | bytes 638984 | tf_op jit(solution)/shard_map/ppermute | solution.py:49
  18.5 14.1 %collective-permute-start.1 = (bf16[1,608,256]{2,1,0:T(8,128)(2,1)S(1)}, bf16[1,608,256]{2,1,0:T(8,128)(2,1)S(1)}, u32[]{:S(2)}, u32[]{:S(2)}) collective-permute-start(bf16[1,608,256]{2,1,0:T(8,128)(2,1)S(1)} %get-tuple-element.86), channel_id=1, source_target_pairs={{0,32},{1,33},{2,34},{3,35},{4,36},{5,37},{6,38},{7,39},{8,40},{9,... | collective-permute-start | bytes 933896 | tf_op jit(solution)/shard_map/ppermute | solution.py:49
  19.7 14.2 %collective-permute-start = (bf16[1,608,256]{2,1,0:T(8,128)(2,1)S(1)}, bf16[1,608,256]{2,1,0:T(8,128)(2,1)}, u32[]{:S(2)}, u32[]{:S(2)}) collective-permute-start(bf16[1,608,256]{2,1,0:T(8,128)(2,1)S(1)} %get-tuple-element.86), channel_id=1, source_target_pairs={{0,1},{1,0},{2,3},{3,2},{4,5},{5,4},{6,7},{7,6},{8,9},{9,8},{10,11... | collective-permute-start | bytes 933896 | tf_op jit(solution)/shard_map/ppermute | solution.py:49
  25.3 11.3 %collective-permute-start.10 = (bf16[608,256]{1,0:T(8,128)(2,1)S(1)}, bf16[608,256]{1,0:T(8,128)(2,1)}, u32[]{:S(2)}, u32[]{:S(2)}) collective-permute-start(bf16[608,256]{1,0:T(8,128)(2,1)S(1)} %collective-permute-done.4), channel_id=1, source_target_pairs={{0,2},{1,3},{2,4},{3,5},{4,6},{5,7},{6,8},{7,9},{8,10},{9,11},{10,... | collective-permute-start | bytes 933896 | tf_op jit(solution)/shard_map/ppermute | solution.py:49
  25.3 7.3 %collective-permute-start.28 = (bf16[208,512]{1,0:T(8,128)(2,1)S(1)}, bf16[208,512]{1,0:T(8,128)(2,1)S(1)}, u32[]{:S(2)}, u32[]{:S(2)}) collective-permute-start(bf16[208,512]{1,0:T(8,128)(2,1)S(1)} %get-tuple-element.88), channel_id=1, source_target_pairs={{0,32},{1,33},{2,34},{3,35},{4,36},{5,37},{6,38},{7,39},{8,40},{9,... | collective-permute-start | bytes 638984 | tf_op jit(solution)/shard_map/ppermute | solution.py:49
  26.5 12.8 %collective-permute-start.29 = (bf16[208,512]{1,0:T(8,128)(2,1)}, bf16[208,512]{1,0:T(8,128)(2,1)}, u32[]{:S(2)}, u32[]{:S(2)}) collective-permute-start(bf16[208,512]{1,0:T(8,128)(2,1)} %collective-permute-done.27), channel_id=1, source_target_pairs={{0,32},{1,33},{2,34},{3,35},{4,36},{5,37},{6,38},{7,39},{8,40},{9,... | collective-permute-start | bytes 638984 | tf_op jit(solution)/shard_map/ppermute | solution.py:49
  32.6 24.9 %collective-permute-start.6 = (bf16[2,608,256]{2,1,0:T(8,128)(2,1)}, bf16[2,608,256]{2,1,0:T(8,128)(2,1)}, u32[]{:S(2)}, u32[]{:S(2)}) collective-permute-start(bf16[2,608,256]{2,1,0:T(8,128)(2,1)} %get-tuple-element.83), channel_id=1, source_target_pairs={{0,1},{1,0},{2,3},{3,2},{4,5},{5,4},{6,7},{7,6},{8,9},{9,8},{10,11... | collective-permute-start | bytes 1867784 | tf_op jit(solution)/shard_map/ppermute | solution.py:49
  32.6 24.8 %collective-permute-start.7 = (bf16[2,608,256]{2,1,0:T(8,128)(2,1)}, bf16[2,608,256]{2,1,0:T(8,128)(2,1)}, u32[]{:S(2)}, u32[]{:S(2)}) collective-permute-start(bf16[2,608,256]{2,1,0:T(8,128)(2,1)} %get-tuple-element.83), channel_id=1, source_target_pairs={{0,32},{1,33},{2,34},{3,35},{4,36},{5,37},{6,38},{7,39},{8,40},{9,... | collective-permute-start | bytes 1867784 | tf_op jit(solution)/shard_map/ppermute | solution.py:49
  33.9 7.8 %collective-permute-start.11 = (bf16[608,256]{1,0:T(8,128)(2,1)}, bf16[608,256]{1,0:T(8,128)(2,1)}, u32[]{:S(2)}, u32[]{:S(2)}) collective-permute-start(bf16[608,256]{1,0:T(8,128)(2,1)} %collective-permute-done.5), channel_id=1, source_target_pairs={{0,14},{1,15},{2,0},{3,1},{4,2},{5,3},{6,4},{7,5},{8,6},{9,7},{10,... | collective-permute-start | bytes 933896 | tf_op jit(solution)/shard_map/ppermute | solution.py:49
  36.6 9.2 %collective-permute-start.16 = (bf16[608,256]{1,0:T(8,128)(2,1)}, bf16[608,256]{1,0:T(8,128)(2,1)}, u32[]{:S(2)}, u32[]{:S(2)}) collective-permute-start(bf16[608,256]{1,0:T(8,128)(2,1)} %collective-permute-done.10), channel_id=1, source_target_pairs={{0,2},{1,3},{2,4},{3,5},{4,6},{5,7},{6,8},{7,9},{8,10},{9,11},{10,... | collective-permute-start | bytes 933896 | tf_op jit(solution)/shard_map/ppermute | solution.py:49
  39.3 13.0 %collective-permute-start.2 = (bf16[1,608,256]{2,1,0:T(8,128)(2,1)}, bf16[1,608,256]{2,1,0:T(8,128)(2,1)}, u32[]{:S(2)}, u32[]{:S(2)}) collective-permute-start(bf16[1,608,256]{2,1,0:T(8,128)(2,1)} %collective-permute-done), channel_id=1, source_target_pairs={{0,32},{1,33},{2,34},{3,35},{4,36},{5,37},{6,38},{7,39},{8,40},{9,... | collective-permute-start | bytes 933896 | tf_op jit(solution)/shard_map/ppermute | solution.py:49
  41.6 13.0 %collective-permute-start.17 = (bf16[608,256]{1,0:T(8,128)(2,1)}, bf16[608,256]{1,0:T(8,128)(2,1)S(1)}, u32[]{:S(2)}, u32[]{:S(2)}) collective-permute-start(bf16[608,256]{1,0:T(8,128)(2,1)} %collective-permute-done.11), channel_id=1, source_target_pairs={{0,14},{1,15},{2,0},{3,1},{4,2},{5,3},{6,4},{7,5},{8,6},{9,7},{10,... | collective-permute-start | bytes 933896 | tf_op jit(solution)/shard_map/ppermute | solution.py:49
  45.8 12.4 %collective-permute-start.22 = (bf16[608,256]{1,0:T(8,128)(2,1)}, bf16[608,256]{1,0:T(8,128)(2,1)S(1)}, u32[]{:S(2)}, u32[]{:S(2)}) collective-permute-start(bf16[608,256]{1,0:T(8,128)(2,1)} %collective-permute-done.16), channel_id=1, source_target_pairs={{0,2},{1,3},{2,4},{3,5},{4,6},{5,7},{6,8},{7,9},{8,10},{9,11},{10,... | collective-permute-start | bytes 933896 | tf_op jit(solution)/shard_map/ppermute | solution.py:49
  52.3 9.5 %collective-permute-start.13 = (bf16[2,608,256]{2,1,0:T(8,128)(2,1)S(1)}, bf16[2,608,256]{2,1,0:T(8,128)(2,1)S(1)}, u32[]{:S(2)}, u32[]{:S(2)}) collective-permute-start(bf16[2,608,256]{2,1,0:T(8,128)(2,1)S(1)} %shard_map.59), channel_id=1, source_target_pairs={{0,32},{1,33},{2,34},{3,35},{4,36},{5,37},{6,38},{7,39},{8,40},{9,... | collective-permute-start | bytes 1867784 | tf_op jit(solution)/shard_map/ppermute | solution.py:49
  54.6 20.8 %collective-permute-start.33 = (bf16[4,208,512]{2,1,0:T(8,128)(2,1)S(1)}, bf16[4,208,512]{2,1,0:T(8,128)(2,1)S(1)}, u32[]{:S(2)}, u32[]{:S(2)}) collective-permute-start(bf16[4,208,512]{2,1,0:T(8,128)(2,1)S(1)} %pad_maximum_fusion.6.refs_11_), channel_id=1, source_target_pairs={{0,14},{1,15},{2,0},{3,1},{4,2},{5,3},{6,4},{7,5},{8,6},{9,7},{10,... | collective-permute-start | bytes 2555912 | tf_op jit(solution)/shard_map/ppermute | solution.py:49
  57.5 21.0 %collective-permute-start.31 = (bf16[4,208,512]{2,1,0:T(8,128)(2,1)S(1)}, bf16[4,208,512]{2,1,0:T(8,128)(2,1)S(1)}, u32[]{:S(2)}, u32[]{:S(2)}) collective-permute-start(bf16[4,208,512]{2,1,0:T(8,128)(2,1)S(1)} %pad_maximum_fusion.6.refs_11_), channel_id=1, source_target_pairs={{0,2},{1,3},{2,4},{3,5},{4,6},{5,7},{6,8},{7,9},{8,10},{9,11},{10,... | collective-permute-start | bytes 2555912 | tf_op jit(solution)/shard_map/ppermute | solution.py:49
  57.5 21.0 %collective-permute-start.30 = (bf16[4,208,512]{2,1,0:T(8,128)(2,1)S(1)}, bf16[4,208,512]{2,1,0:T(8,128)(2,1)S(1)}, u32[]{:S(2)}, u32[]{:S(2)}) collective-permute-start(bf16[4,208,512]{2,1,0:T(8,128)(2,1)S(1)} %pad_maximum_fusion.6.refs_11_), channel_id=1, source_target_pairs={{0,16},{1,17},{2,18},{3,19},{4,20},{5,21},{6,22},{7,23},{8,24},{9,... | collective-permute-start | bytes 2555912 | tf_op jit(solution)/shard_map/ppermute | solution.py:49
  58.2 10.9 %collective-permute-start.12 = (bf16[2,608,256]{2,1,0:T(8,128)(2,1)S(1)}, bf16[2,608,256]{2,1,0:T(8,128)(2,1)S(1)}, u32[]{:S(2)}, u32[]{:S(2)}) collective-permute-start(bf16[2,608,256]{2,1,0:T(8,128)(2,1)S(1)} %shard_map.59), channel_id=1, source_target_pairs={{0,1},{1,0},{2,3},{3,2},{4,5},{5,4},{6,7},{7,6},{8,9},{9,8},{10,11... | collective-permute-start | bytes 1867784 | tf_op jit(solution)/shard_map/ppermute | solution.py:49
  60.1 65.1 %copy-start.13 = (bf16[4,1,608,256]{3,2,1,0:T(8,128)(2,1)}, bf16[4,1,608,256]{3,2,1,0:T(8,128)(2,1)S(1)}, u32[]{:S(2)}) copy-start(bf16[4,1,608,256]{3,2,1,0:T(8,128)(2,1)S(1)} %pad_maximum_fusion.4.refs_1_) | copy-start | bytes 3735556
  61.7 44.8 %collective-permute-start.3 = (bf16[4,1,608,256]{3,2,1,0:T(8,128)(2,1)S(1)}, bf16[4,1,608,256]{3,2,1,0:T(8,128)(2,1)S(1)}, u32[]{:S(2)}, u32[]{:S(2)}) collective-permute-start(bf16[4,1,608,256]{3,2,1,0:T(8,128)(2,1)S(1)} %pad_maximum_fusion.4.refs_1_), channel_id=1, source_target_pairs={{0,16},{1,17},{2,18},{3,19},{4,20},{5,21},{6,22},{7,23},{8,24},{9,... | collective-permute-start | bytes 3735560 | tf_op jit(solution)/shard_map/ppermute | solution.py:49
  69.2 10.8 %collective-permute-start.24 = (bf16[1,608,256]{2,1,0:T(8,128)(2,1)S(1)}, bf16[1,608,256]{2,1,0:T(8,128)(2,1)S(1)}, u32[]{:S(2)}, u32[]{:S(2)}) collective-permute-start(bf16[1,608,256]{2,1,0:T(8,128)(2,1)S(1)} %bitcast.79), channel_id=1, source_target_pairs={{0,32},{1,33},{2,34},{3,35},{4,36},{5,37},{6,38},{7,39},{8,40},{9,... | collective-permute-start | bytes 933896 | tf_op jit(solution)/shard_map/ppermute | solution.py:49
  70.4 55.5 %copy-start.19 = (bf16[1,2,608,256]{3,2,1,0:T(8,128)(2,1)S(1)}, bf16[1,2,608,256]{3,2,1,0:T(8,128)(2,1)}, u32[]{:S(2)}) copy-start(bf16[1,2,608,256]{3,2,1,0:T(8,128)(2,1)} %get-tuple-element.82) | copy-start | bytes 1867780
  75.4 52.0 %copy-start.24 = (bf16[4,208,512]{2,1,0:T(8,128)(2,1)}, bf16[4,208,512]{2,1,0:T(8,128)(2,1)S(1)}, u32[]{:S(2)}) copy-start(bf16[4,208,512]{2,1,0:T(8,128)(2,1)S(1)} %collective-permute-done.33.refs_15_) | copy-start | bytes 2555908
  75.4 18.6 %collective-permute-start.18 = (bf16[2,608,256]{2,1,0:T(8,128)(2,1)S(1)}, bf16[2,608,256]{2,1,0:T(8,128)(2,1)S(1)}, u32[]{:S(2)}, u32[]{:S(2)}) collective-permute-start(bf16[2,608,256]{2,1,0:T(8,128)(2,1)S(1)} %get-tuple-element.81), channel_id=1, source_target_pairs={{0,1},{1,0},{2,3},{3,2},{4,5},{5,4},{6,7},{7,6},{8,9},{9,8},{10,11... | collective-permute-start | bytes 1867784 | tf_op jit(solution)/shard_map/ppermute | solution.py:49
  78.5 21.8 %collective-permute-start.19 = (bf16[2,608,256]{2,1,0:T(8,128)(2,1)S(1)}, bf16[2,608,256]{2,1,0:T(8,128)(2,1)S(1)}, u32[]{:S(2)}, u32[]{:S(2)}) collective-permute-start(bf16[2,608,256]{2,1,0:T(8,128)(2,1)S(1)} %get-tuple-element.81), channel_id=1, source_target_pairs={{0,32},{1,33},{2,34},{3,35},{4,36},{5,37},{6,38},{7,39},{8,40},{9,... | collective-permute-start | bytes 1867784 | tf_op jit(solution)/shard_map/ppermute | solution.py:49
  78.5 24.6 %collective-permute-start.8 = (bf16[2,608,256]{2,1,0:T(8,128)(2,1)}, bf16[2,608,256]{2,1,0:T(8,128)(2,1)S(1)}, u32[]{:S(2)}, u32[]{:S(2)}) collective-permute-start(bf16[2,608,256]{2,1,0:T(8,128)(2,1)} %collective-permute-done.6), channel_id=1, source_target_pairs={{0,32},{1,33},{2,34},{3,35},{4,36},{5,37},{6,38},{7,39},{8,40},{9,... | collective-permute-start | bytes 1867784 | tf_op jit(solution)/shard_map/ppermute | solution.py:49
  80.0 14.0 %collective-permute-start.23 = (bf16[1,608,256]{2,1,0:T(8,128)(2,1)S(1)}, bf16[1,608,256]{2,1,0:T(8,128)(2,1)S(1)}, u32[]{:S(2)}, u32[]{:S(2)}) collective-permute-start(bf16[1,608,256]{2,1,0:T(8,128)(2,1)S(1)} %bitcast.80), channel_id=1, source_target_pairs={{0,1},{1,0},{2,3},{3,2},{4,5},{5,4},{6,7},{7,6},{8,9},{9,8},{10,11... | collective-permute-start | bytes 933896 | tf_op jit(solution)/shard_map/ppermute | solution.py:49
  94.0 12.5 %collective-permute-start.25 = (bf16[1,608,256]{2,1,0:T(8,128)(2,1)S(1)}, bf16[1,608,256]{2,1,0:T(8,128)(2,1)S(1)}, u32[]{:S(2)}, u32[]{:S(2)}) collective-permute-start(bf16[1,608,256]{2,1,0:T(8,128)(2,1)S(1)} %collective-permute-done.23), channel_id=1, source_target_pairs={{0,32},{1,33},{2,34},{3,35},{4,36},{5,37},{6,38},{7,39},{8,40},{9,... | collective-permute-start | bytes 933896 | tf_op jit(solution)/shard_map/ppermute | solution.py:49
  94.0 19.8 %collective-permute-start.37 = (bf16[4,208,512]{2,1,0:T(8,128)(2,1)S(1)}, bf16[4,208,512]{2,1,0:T(8,128)(2,1)S(1)}, u32[]{:S(2)}, u32[]{:S(2)}) collective-permute-start(bf16[4,208,512]{2,1,0:T(8,128)(2,1)S(1)} %collective-permute-done.33.refs_15_), channel_id=1, source_target_pairs={{0,14},{1,15},{2,0},{3,1},{4,2},{5,3},{6,4},{7,5},{8,6},{9,7},{10,... | collective-permute-start | bytes 2555912 | tf_op jit(solution)/shard_map/ppermute | solution.py:49
  100.3 24.3 %collective-permute-start.35 = (bf16[4,208,512]{2,1,0:T(8,128)(2,1)S(1)}, bf16[4,208,512]{2,1,0:T(8,128)(2,1)S(1)}, u32[]{:S(2)}, u32[]{:S(2)}) collective-permute-start(bf16[4,208,512]{2,1,0:T(8,128)(2,1)S(1)} %collective-permute-done.31.refs_13_), channel_id=1, source_target_pairs={{0,2},{1,3},{2,4},{3,5},{4,6},{5,7},{6,8},{7,9},{8,10},{9,11},{10,... | collective-permute-start | bytes 2555912 | tf_op jit(solution)/shard_map/ppermute | solution.py:49
  103.1 21.5 %collective-permute-start.34 = (bf16[4,208,512]{2,1,0:T(8,128)(2,1)S(1)}, bf16[4,208,512]{2,1,0:T(8,128)(2,1)S(1)}, u32[]{:S(2)}, u32[]{:S(2)}) collective-permute-start(bf16[4,208,512]{2,1,0:T(8,128)(2,1)S(1)} %collective-permute-done.33.refs_15_), channel_id=1, source_target_pairs={{0,16},{1,17},{2,18},{3,19},{4,20},{5,21},{6,22},{7,23},{8,24},{9,... | collective-permute-start | bytes 2555912 | tf_op jit(solution)/shard_map/ppermute | solution.py:49
  106.5 18.7 %collective-permute-start.32 = (bf16[4,208,512]{2,1,0:T(8,128)(2,1)S(1)}, bf16[4,208,512]{2,1,0:T(8,128)(2,1)S(1)}, u32[]{:S(2)}, u32[]{:S(2)}) collective-permute-start(bf16[4,208,512]{2,1,0:T(8,128)(2,1)S(1)} %collective-permute-done.31.refs_13_), channel_id=1, source_target_pairs={{0,16},{1,17},{2,18},{3,19},{4,20},{5,21},{6,22},{7,23},{8,24},{9,... | collective-permute-start | bytes 2555912 | tf_op jit(solution)/shard_map/ppermute | solution.py:49
  106.5 10.7 %collective-permute-start.14 = (bf16[2,608,256]{2,1,0:T(8,128)(2,1)S(1)}, bf16[2,608,256]{2,1,0:T(8,128)(2,1)S(1)}, u32[]{:S(2)}, u32[]{:S(2)}) collective-permute-start(bf16[2,608,256]{2,1,0:T(8,128)(2,1)S(1)} %collective-permute-done.12), channel_id=1, source_target_pairs={{0,32},{1,33},{2,34},{3,35},{4,36},{5,37},{6,38},{7,39},{8,40},{9,... | collective-permute-start | bytes 1867784 | tf_op jit(solution)/shard_map/ppermute | solution.py:49
  113.8 21.6 %collective-permute-start.41 = (bf16[4,208,512]{2,1,0:T(8,128)(2,1)S(1)}, bf16[4,208,512]{2,1,0:T(8,128)(2,1)S(1)}, u32[]{:S(2)}, u32[]{:S(2)}) collective-permute-start(bf16[4,208,512]{2,1,0:T(8,128)(2,1)S(1)} %collective-permute-done.37.refs_19_), channel_id=1, source_target_pairs={{0,14},{1,15},{2,0},{3,1},{4,2},{5,3},{6,4},{7,5},{8,6},{9,7},{10,... | collective-permute-start | bytes 2555912 | tf_op jit(solution)/shard_map/ppermute | solution.py:49
  117.2 20.5 %collective-permute-start.38 = (bf16[4,208,512]{2,1,0:T(8,128)(2,1)S(1)}, bf16[4,208,512]{2,1,0:T(8,128)(2,1)S(1)}, u32[]{:S(2)}, u32[]{:S(2)}) collective-permute-start(bf16[4,208,512]{2,1,0:T(8,128)(2,1)S(1)} %collective-permute-done.37.refs_19_), channel_id=1, source_target_pairs={{0,16},{1,17},{2,18},{3,19},{4,20},{5,21},{6,22},{7,23},{8,24},{9,... | collective-permute-start | bytes 2555912 | tf_op jit(solution)/shard_map/ppermute | solution.py:49
  124.6 21.7 %collective-permute-start.39 = (bf16[4,208,512]{2,1,0:T(8,128)(2,1)S(1)}, bf16[4,208,512]{2,1,0:T(8,128)(2,1)S(1)}, u32[]{:S(2)}, u32[]{:S(2)}) collective-permute-start(bf16[4,208,512]{2,1,0:T(8,128)(2,1)S(1)} %collective-permute-done.35.refs_17_), channel_id=1, source_target_pairs={{0,2},{1,3},{2,4},{3,5},{4,6},{5,7},{6,8},{7,9},{8,10},{9,11},{10,... | collective-permute-start | bytes 2555912 | tf_op jit(solution)/shard_map/ppermute | solution.py:49
  124.6 9.5 %collective-permute-start.20 = (bf16[2,608,256]{2,1,0:T(8,128)(2,1)S(1)}, bf16[2,608,256]{2,1,0:T(8,128)(2,1)S(1)}, u32[]{:S(2)}, u32[]{:S(2)}) collective-permute-start(bf16[2,608,256]{2,1,0:T(8,128)(2,1)S(1)} %collective-permute-done.18), channel_id=1, source_target_pairs={{0,32},{1,33},{2,34},{3,35},{4,36},{5,37},{6,38},{7,39},{8,40},{9,... | collective-permute-start | bytes 1867784 | tf_op jit(solution)/shard_map/ppermute | solution.py:49
  125.2 22.1 %collective-permute-start.26 = (bf16[4,1,608,256]{3,2,1,0:T(8,128)(2,1)S(1)}, bf16[4,1,608,256]{3,2,1,0:T(8,128)(2,1)S(1)}, u32[]{:S(2)}, u32[]{:S(2)}) collective-permute-start(bf16[4,1,608,256]{3,2,1,0:T(8,128)(2,1)S(1)} %pad_maximum_fusion.5.refs_9_), channel_id=1, source_target_pairs={{0,16},{1,17},{2,18},{3,19},{4,20},{5,21},{6,22},{7,23},{8,24},{9,... | collective-permute-start | bytes 3735560 | tf_op jit(solution)/shard_map/ppermute | solution.py:49
  134.1 13.1 %collective-permute-start.36 = (bf16[4,208,512]{2,1,0:T(8,128)(2,1)S(1)}, bf16[4,208,512]{2,1,0:T(8,128)(2,1)S(1)}, u32[]{:S(2)}, u32[]{:S(2)}) collective-permute-start(bf16[4,208,512]{2,1,0:T(8,128)(2,1)S(1)} %collective-permute-done.35.refs_17_), channel_id=1, source_target_pairs={{0,16},{1,17},{2,18},{3,19},{4,20},{5,21},{6,22},{7,23},{8,24},{9,... | collective-permute-start | bytes 2555912 | tf_op jit(solution)/shard_map/ppermute | solution.py:49
  135.4 34.5 %collective-permute-start.9 = (bf16[4,2,608,256]{3,2,1,0:T(8,128)(2,1)S(1)}, bf16[4,2,608,256]{3,2,1,0:T(8,128)(2,1)S(1)}, u32[]{:S(2)}, u32[]{:S(2)}) collective-permute-start(bf16[4,2,608,256]{3,2,1,0:T(8,128)(2,1)S(1)} %pad_maximum_fusion.1.refs_3_), channel_id=1, source_target_pairs={{0,16},{1,17},{2,18},{3,19},{4,20},{5,21},{6,22},{7,23},{8,24},{9,... | collective-permute-start | bytes 7471112 | tf_op jit(solution)/shard_map/ppermute | solution.py:49
  137.7 32.2 %collective-permute-start.15 = (bf16[4,2,608,256]{3,2,1,0:T(8,128)(2,1)S(1)}, bf16[4,2,608,256]{3,2,1,0:T(8,128)(2,1)S(1)}, u32[]{:S(2)}, u32[]{:S(2)}) collective-permute-start(bf16[4,2,608,256]{3,2,1,0:T(8,128)(2,1)S(1)} %pad_maximum_fusion.2.refs_5_), channel_id=1, source_target_pairs={{0,16},{1,17},{2,18},{3,19},{4,20},{5,21},{6,22},{7,23},{8,24},{9,... | collective-permute-start | bytes 7471112 | tf_op jit(solution)/shard_map/ppermute | solution.py:49
  146.3 23.6 %collective-permute-start.21 = (bf16[4,2,608,256]{3,2,1,0:T(8,128)(2,1)S(1)}, bf16[4,2,608,256]{3,2,1,0:T(8,128)(2,1)S(1)}, u32[]{:S(2)}, u32[]{:S(2)}) collective-permute-start(bf16[4,2,608,256]{3,2,1,0:T(8,128)(2,1)S(1)} %pad_maximum_fusion.3.refs_7_), channel_id=1, source_target_pairs={{0,16},{1,17},{2,18},{3,19},{4,20},{5,21},{6,22},{7,23},{8,24},{9,... | collective-permute-start | bytes 7471112 | tf_op jit(solution)/shard_map/ppermute | solution.py:49
  147.2 5.6 %collective-permute-start.42 = (bf16[4,208,512]{2,1,0:T(8,128)(2,1)S(1)}, bf16[4,208,512]{2,1,0:T(8,128)(2,1)S(1)}, u32[]{:S(2)}, u32[]{:S(2)}) collective-permute-start(bf16[4,208,512]{2,1,0:T(8,128)(2,1)S(1)} %collective-permute-done.41.refs_23_), channel_id=1, source_target_pairs={{0,16},{1,17},{2,18},{3,19},{4,20},{5,21},{6,22},{7,23},{8,24},{9,... | collective-permute-start | bytes 2555912 | tf_op jit(solution)/shard_map/ppermute | solution.py:49
  147.3 21.3 %collective-permute-start.43 = (bf16[4,208,512]{2,1,0:T(8,128)(2,1)S(1)}, bf16[4,208,512]{2,1,0:T(8,128)(2,1)S(1)}, u32[]{:S(2)}, u32[]{:S(2)}) collective-permute-start(bf16[4,208,512]{2,1,0:T(8,128)(2,1)S(1)} %collective-permute-done.39.refs_21_), channel_id=1, source_target_pairs={{0,2},{1,3},{2,4},{3,5},{4,6},{5,7},{6,8},{7,9},{8,10},{9,11},{10,... | collective-permute-start | bytes 2555912 | tf_op jit(solution)/shard_map/ppermute | solution.py:49
  152.8 17.1 %collective-permute-start.40 = (bf16[4,208,512]{2,1,0:T(8,128)(2,1)S(1)}, bf16[4,208,512]{2,1,0:T(8,128)(2,1)S(1)}, u32[]{:S(2)}, u32[]{:S(2)}) collective-permute-start(bf16[4,208,512]{2,1,0:T(8,128)(2,1)S(1)} %collective-permute-done.39.refs_21_), channel_id=1, source_target_pairs={{0,16},{1,17},{2,18},{3,19},{4,20},{5,21},{6,22},{7,23},{8,24},{9,... | collective-permute-start | bytes 2555912 | tf_op jit(solution)/shard_map/ppermute | solution.py:49
  168.6 5.2 %collective-permute-start.44 = (bf16[4,208,512]{2,1,0:T(8,128)(2,1)S(1)}, bf16[4,208,512]{2,1,0:T(8,128)(2,1)}, u32[]{:S(2)}, u32[]{:S(2)}) collective-permute-start(bf16[4,208,512]{2,1,0:T(8,128)(2,1)S(1)} %collective-permute-done.43.refs_25_), channel_id=1, source_target_pairs={{0,16},{1,17},{2,18},{3,19},{4,20},{5,21},{6,22},{7,23},{8,24},{9,... | collective-permute-start | bytes 2555912 | tf_op jit(solution)/shard_map/ppermute | solution.py:49
  200.5 13.0 %collective-permute-start.46 = (bf16[32,8192]{1,0:T(8,128)(2,1)}, bf16[32,8192]{1,0:T(8,128)(2,1)S(1)}, u32[]{:S(2)}, u32[]{:S(2)}) collective-permute-start(bf16[32,8192]{1,0:T(8,128)(2,1)} %get-tuple-element.38), channel_id=1, source_target_pairs={{0,96},{1,97},{2,98},{3,99},{4,100},{5,101},{6,102},{7,103},{8,104... | collective-permute-start | bytes 1572872 | tf_op jit(solution)/shard_map/ppermute | solution.py:49
  225.3 0.7 collective-permute-start.47
  226.4 1.4 collective-permute-start.48
  227.1 1.7 collective-permute-start.45
  228.9 0.7 collective-permute-start.49
  229.8 0.8 collective-permute-start.50
  231.4 3.5 collective-permute-start.52
  232.6 8.8 %collective-permute-start.53 = (bf16[2,32,4352]{2,1,0:T(8,128)(2,1)S(1)}, bf16[2,32,4352]{2,1,0:T(8,128)(2,1)S(1)}, u32[]{:S(2)}, u32[]{:S(2)}) collective-permute-start(bf16[2,32,4352]{2,1,0:T(8,128)(2,1)S(1)} %shard_map.68), channel_id=1, source_target_pairs={{0,1},{1,0},{2,3},{3,2},{4,5},{5,4},{6,7},{7,6},{8,9},{9,8},{10,11... | collective-permute-start | bytes 1671176 | tf_op jit(solution)/shard_map/ppermute | solution.py:49
  235.0 12.4 %collective-permute-start.54 = (bf16[2,32,4352]{2,1,0:T(8,128)(2,1)S(1)}, bf16[2,32,4352]{2,1,0:T(8,128)(2,1)S(1)}, u32[]{:S(2)}, u32[]{:S(2)}) collective-permute-start(bf16[2,32,4352]{2,1,0:T(8,128)(2,1)S(1)} %shard_map.69), channel_id=1, source_target_pairs={{0,1},{1,0},{2,3},{3,2},{4,5},{5,4},{6,7},{7,6},{8,9},{9,8},{10,11... | collective-permute-start | bytes 1671176 | tf_op jit(solution)/shard_map/ppermute | solution.py:49
  247.6 15.0 %collective-permute-start.55 = (bf16[128,4352]{1,0:T(8,128)(2,1)S(1)}, bf16[128,4352]{1,0:T(8,128)(2,1)S(1)}, u32[]{:S(2)}, u32[]{:S(2)}) collective-permute-start(bf16[128,4352]{1,0:T(8,128)(2,1)S(1)} %shard_map.70), channel_id=1, source_target_pairs={{0,32},{1,33},{2,34},{3,35},{4,36},{5,37},{6,38},{7,39},{8,40},{9,... | collective-permute-start | bytes 3342344 | tf_op jit(solution)/shard_map/ppermute | solution.py:49
  249.0 121.2 %collective-permute-start.51 = (bf16[32,8192]{1,0:T(8,128)(2,1)S(1)}, bf16[32,8192]{1,0:T(8,128)(2,1)S(1)}, u32[]{:S(2)}, u32[]{:S(2)}) collective-permute-start(bf16[32,8192]{1,0:T(8,128)(2,1)S(1)} %get-tuple-element.64), channel_id=1, source_target_pairs={{64,32},{65,33},{66,34},{67,35},{68,36},{69,37},{70,38},{71,39},{7... | collective-permute-start | bytes 1572872 | tf_op jit(solution)/shard_map/ppermute | solution.py:49
  382.1 4.1 collective-permute-start.56
  385.0 8.8 %collective-permute-start.57 = (bf16[2,32,4352]{2,1,0:T(8,128)(2,1)S(1)}, bf16[2,32,4352]{2,1,0:T(8,128)(2,1)S(1)}, u32[]{:S(2)}, u32[]{:S(2)}) collective-permute-start(bf16[2,32,4352]{2,1,0:T(8,128)(2,1)S(1)} %shard_map.73), channel_id=1, source_target_pairs={{0,1},{1,0},{2,3},{3,2},{4,5},{5,4},{6,7},{7,6},{8,9},{9,8},{10,11... | collective-permute-start | bytes 1671176 | tf_op jit(solution)/shard_map/ppermute | solution.py:49
  386.4 13.4 %collective-permute-start.58 = (bf16[2,32,4352]{2,1,0:T(8,128)(2,1)S(1)}, bf16[2,32,4352]{2,1,0:T(8,128)(2,1)S(1)}, u32[]{:S(2)}, u32[]{:S(2)}) collective-permute-start(bf16[2,32,4352]{2,1,0:T(8,128)(2,1)S(1)} %shard_map.74), channel_id=1, source_target_pairs={{0,1},{1,0},{2,3},{3,2},{4,5},{5,4},{6,7},{7,6},{8,9},{9,8},{10,11... | collective-permute-start | bytes 1671176 | tf_op jit(solution)/shard_map/ppermute | solution.py:49
  400.0 14.7 %collective-permute-start.59 = (bf16[128,4352]{1,0:T(8,128)(2,1)S(1)}, bf16[128,4352]{1,0:T(8,128)(2,1)S(1)}, u32[]{:S(2)}, u32[]{:S(2)}) collective-permute-start(bf16[128,4352]{1,0:T(8,128)(2,1)S(1)} %shard_map.75), channel_id=1, source_target_pairs={{0,32},{1,33},{2,34},{3,35},{4,36},{5,37},{6,38},{7,39},{8,40},{9,... | collective-permute-start | bytes 3342344 | tf_op jit(solution)/shard_map/ppermute | solution.py:49
  (39 other events, 469.1 us)
Sparse Core Ops, SparseCore 0:
  419.3 49.1 reduce-scatter.1

commit v3 on v2

--- a/solution.py
+++ b/solution.py
@@ -567,14 +567,15 @@
     other = to_core(sent)
     near = to_first(packed_rows((kept, (1,))))
     far = to_first(packed_rows((other, (1,))))
-    outgoing = packed_rows((kept, (0, 1)), (other, (0, 1)), (near, (1,)), (far, (1,)))
-    arrived = to_second(outgoing)
+    early = to_second(packed_rows((kept, (0, 1)), (other, (0, 1))))
+    late = to_second(packed_rows((near, (1,)), (far, (1,))))
     return packed_rows(
         (kept, (0, 0)),
         (other, (0, 0)),
         (near, (0,)),
         (far, (0,)),
-        (arrived, ()),
+        (early, ()),
+        (late, ()),
     )
 
 

time: 488 us -> 494 us (1.012)
    ppermute x60 -> x62, waiting for transfers between devices: 256 us -> 259 us  [send(): return lax.ppermute(value, BOTH, pairs_of(target, keep))]
    ppermute x60 -> x62, starting transfers between devices: 72.5 us -> 74.7 us  [send(): return lax.ppermute(value, BOTH, pairs_of(target, keep))]
  transfers between devices with their start and end apart: 61 -> 63, of which waited for: 26 -> 26; matrix products, arithmetic and copies ran while one was open for 3% -> 3% of each run, Pallas kernels for 0% -> 0%
where the time goes in v3:
time: 494 us; the launch traced here: 484 us
  waiting for transfers between devices  309 us (63%)
  starting transfers between devices  74.7 us (15%)
  local copies, waits for them, and re-layouts  39.4 us (8%)
  Pallas kernels  30.4 us (6%)
  between operations  15.4 us (3%)
  other arithmetic  14.5 us (3%)
    ppermute x62, waiting for transfers between devices, send(): return lax.ppermute(value, BOTH, pairs_of(target, keep))  259 us
    ppermute x62, starting transfers between devices, send(): return lax.ppermute(value, BOTH, pairs_of(target, keep))  74.7 us
    reduce_scatter x1, waiting for transfers between devices, body(): lax.psum_scatter(pieces.astype(BF), 'dp', scatter_dimension=0, axis_index...  49.4 us
    unnamed x87, local copies, waits for them, and re-layouts  31.7 us
    pallas_call x1, Pallas kernels, run_first(): pl.pallas_call(functools.partial(first_kernel, plan), out_shape=(pltpu.VM...  15 us
    pallas_call x4, Pallas kernels, run_backward(): pl.pallas_call(functools.partial(backward_kernel, stage, saved is not Non...  12.4 us
  transfers between devices with their start and end apart: 63, of which 26 were waited for; matrix products, arithmetic and copies ran while one was open for 3% of the time, Pallas kernels for 0%

profile of v3, /device:TPU:1, one launch (start us, length us, event | category | flops | bytes accessed | tf_op | source)
XLA Modules:
  0.0 484.3 jit_solution(4140518174490436652)
XLA Ops:
  8.0 1.7 pad_maximum_fusion.10
  9.7 6.4 %collective-permute-start.5 = (bf16[608,256]{1,0:T(8,128)(2,1)S(1)}, bf16[608,256]{1,0:T(8,128)(2,1)}, u32[]{:S(2)}, u32[]{:S(2)}) collective-permute-start(bf16[608,256]{1,0:T(8,128)(2,1)S(1)} %get-tuple-element.84), channel_id=1, source_target_pairs={{0,14},{1,15},{2,0},{3,1},{4,2},{5,3},{6,4},{7,5},{8,6},{9,7},{10,... | collective-permute-start | bytes 933896 | tf_op jit(solution)/shard_map/ppermute | solution.py:49
  17.1 1.4 collective-permute-start.27
  18.5 1.2 collective-permute-start.1
  19.9 5.4 %collective-permute-done.4 = bf16[608,256]{1,0:T(8,128)(2,1)S(1)} collective-permute-done((bf16[608,256]{1,0:T(8,128)(2,1)S(1)}, bf16[608,256]{1,0:T(8,128)(2,1)S(1)}, u32[]{:S(2)}, u32[]{:S(2)}) %collective-permute-start.4) | collective-permute-done | bytes 311328 | tf_op jit(solution)/shard_map/ppermute | solution.py:49
  25.3 1.2 collective-permute-start.28
  26.8 2.1 fusion.5
  28.8 3.7 collective-permute-done.28
  32.6 1.2 collective-permute-start.7
  33.9 2.7 collective-permute-start.11
  36.7 1.7 constant_dynamic-slice_fusion.1
  39.6 1.2 constant_dynamic-slice_fusion
  41.6 3.0 collective-permute-start.17
  47.4 4.8 collective-permute-done.2
  52.3 1.2 collective-permute-start.13
  54.6 2.8 collective-permute-start.33
  58.9 1.2 pad_maximum_fusion.4.refs_1_
  60.1 1.6 collective-permute-done.13
  61.7 2.7 collective-permute-start.3
  64.4 4.8 collective-permute-done.12
  69.2 1.2 collective-permute-start.24
  71.5 3.9 collective-permute-done.33.refs_15_
  75.4 2.0 collective-permute-start.18
  78.5 1.5 collective-permute-start.8
  80.0 2.0 collective-permute-start.23
  82.0 12.0 %collective-permute-done.23 = bf16[1,608,256]{2,1,0:T(8,128)(2,1)S(1)} collective-permute-done((bf16[1,608,256]{2,1,0:T(8,128)(2,1)S(1)}, bf16[1,608,256]{2,1,0:T(8,128)(2,1)S(1)}, u32[]{:S(2)}, u32[]{:S(2)}) %collective-permute-start.23) | collective-permute-done | bytes 311328 | tf_op jit(solution)/shard_map/ppermute | solution.py:49
  94.0 6.3 %collective-permute-start.37 = (bf16[4,208,512]{2,1,0:T(8,128)(2,1)S(1)}, bf16[4,208,512]{2,1,0:T(8,128)(2,1)S(1)}, u32[]{:S(2)}, u32[]{:S(2)}) collective-permute-start(bf16[4,208,512]{2,1,0:T(8,128)(2,1)S(1)} %collective-permute-done.33.refs_15_), channel_id=1, source_target_pairs={{0,14},{1,15},{2,0},{3,1},{4,2},{5,3},{6,4},{7,5},{8,6},{9,7},{10,... | collective-permute-start | bytes 2555912 | tf_op jit(solution)/shard_map/ppermute | solution.py:49
  100.3 2.8 collective-permute-done.8
  103.1 2.3 collective-permute-start.34
  106.8 7.0 %collective-permute-done.37.refs_19_ = bf16[4,208,512]{2,1,0:T(8,128)(2,1)S(1)} collective-permute-done((bf16[4,208,512]{2,1,0:T(8,128)(2,1)S(1)}, bf16[4,208,512]{2,1,0:T(8,128)(2,1)S(1)}, u32[]{:S(2)}, u32[]{:S(2)}) %collective-permute-start.37) | collective-permute-done | bytes 852000 | tf_op jit(solution)/shard_map/ppermute | solution.py:49
  113.8 3.4 collective-permute-start.41
  117.2 7.4 %collective-permute-start.38 = (bf16[4,208,512]{2,1,0:T(8,128)(2,1)S(1)}, bf16[4,208,512]{2,1,0:T(8,128)(2,1)S(1)}, u32[]{:S(2)}, u32[]{:S(2)}) collective-permute-start(bf16[4,208,512]{2,1,0:T(8,128)(2,1)S(1)} %collective-permute-done.37.refs_19_), channel_id=1, source_target_pairs={{0,16},{1,17},{2,18},{3,19},{4,20},{5,21},{6,22},{7,23},{8,24},{9,... | collective-permute-start | bytes 2555912 | tf_op jit(solution)/shard_map/ppermute | solution.py:49
  125.9 1.6 pad_maximum_fusion.1.refs_3_
  127.9 6.2 %collective-permute-done.20 = bf16[2,608,256]{2,1,0:T(8,128)(2,1)S(1)} collective-permute-done((bf16[2,608,256]{2,1,0:T(8,128)(2,1)S(1)}, bf16[2,608,256]{2,1,0:T(8,128)(2,1)S(1)}, u32[]{:S(2)}, u32[]{:S(2)}) %collective-permute-start.20) | collective-permute-done | bytes 622624 | tf_op jit(solution)/shard_map/ppermute | solution.py:49
  135.4 2.3 collective-permute-start.9
  137.8 8.5 %collective-permute-done.39.refs_21_ = bf16[4,208,512]{2,1,0:T(8,128)(2,1)S(1)} collective-permute-done((bf16[4,208,512]{2,1,0:T(8,128)(2,1)S(1)}, bf16[4,208,512]{2,1,0:T(8,128)(2,1)S(1)}, u32[]{:S(2)}, u32[]{:S(2)}) %collective-permute-start.39) | collective-permute-done | bytes 852000 | tf_op jit(solution)/shard_map/ppermute | solution.py:49
  147.3 5.4 %collective-permute-done.42.refs_24_ = bf16[4,208,512]{2,1,0:T(8,128)(2,1)S(1)} collective-permute-done((bf16[4,208,512]{2,1,0:T(8,128)(2,1)S(1)}, bf16[4,208,512]{2,1,0:T(8,128)(2,1)S(1)}, u32[]{:S(2)}, u32[]{:S(2)}) %collective-permute-start.42) | collective-permute-done | bytes 852000 | tf_op jit(solution)/shard_map/ppermute | solution.py:49
  153.1 15.5 %collective-permute-done.43.refs_25_ = bf16[4,208,512]{2,1,0:T(8,128)(2,1)S(1)} collective-permute-done((bf16[4,208,512]{2,1,0:T(8,128)(2,1)S(1)}, bf16[4,208,512]{2,1,0:T(8,128)(2,1)S(1)}, u32[]{:S(2)}, u32[]{:S(2)}) %collective-permute-start.43) | collective-permute-done | bytes 852000 | tf_op jit(solution)/shard_map/ppermute | solution.py:49
  168.6 1.2 collective-permute-start.44
  172.4 1.4 copy-done.18
  173.9 15.0 %shard_map.60 = (bf16[4,16,512,256]{3,2,1,0:T(8,128)(2,1)S(1)}, bf16[4,16,256,512]{3,2,1,0:T(8,128)(2,1)S(1)}, bf16[32,8192]{1,0:T(8,128)(2,1)}, bf16[4,32,8192]...) custom-call(bf16[32,8192]{1,0:T(8,128)(2,1)} %bitcast.64, ...), custom_call_target="tpu_custom_call" | custom-call | flops 2000000000 | bytes 41943040 | tf_op jit(solution)/shard_map/pallas_call | solution.py:480
  188.9 5.8 %copy-done = bf16[4,16,512,256]{3,2,1,0:T(8,128)(2,1)} copy-done((bf16[4,16,512,256]{3,2,1,0:T(8,128)(2,1)}, bf16[4,16,512,256]{3,2,1,0:T(8,128)(2,1)S(1)}, u32[]{:S(2)}) %copy-start) | copy-done | bytes 16777240
  194.8 5.7 %copy-done.2 = bf16[4,16,256,512]{3,2,1,0:T(8,128)(2,1)} copy-done((bf16[4,16,256,512]{3,2,1,0:T(8,128)(2,1)}, bf16[4,16,256,512]{3,2,1,0:T(8,128)(2,1)S(1)}, u32[]{:S(2)}) %copy-start.2) | copy-done | bytes 16777240
  200.5 1.7 collective-permute-start.46
  202.2 1.2 copy-done.4
  203.5 10.1 %collective-permute-done.46.refs_0_ = bf16[32,8192]{1,0:T(8,128)(2,1)S(1)} collective-permute-done((bf16[32,8192]{1,0:T(8,128)(2,1)}, bf16[32,8192]{1,0:T(8,128)(2,1)S(1)}, u32[]{:S(2)}, u32[]{:S(2)}) %collective-permute-start.46) | collective-permute-done | bytes 524320 | tf_op jit(solution)/shard_map/ppermute | solution.py:49
  213.6 5.8 %copy-done.1 = bf16[4,16,512,256]{3,2,1,0:T(8,128)(2,1)S(1)} copy-done((bf16[4,16,512,256]{3,2,1,0:T(8,128)(2,1)S(1)}, bf16[4,16,512,256]{3,2,1,0:T(8,128)(2,1)}, u32[]{:S(2)}) %copy-start.1) | copy-done | bytes 16777240
  219.3 5.8 %copy-done.3 = bf16[4,16,256,512]{3,2,1,0:T(8,128)(2,1)S(1)} copy-done((bf16[4,16,256,512]{3,2,1,0:T(8,128)(2,1)S(1)}, bf16[4,16,256,512]{3,2,1,0:T(8,128)(2,1)}, u32[]{:S(2)}) %copy-start.3) | copy-done | bytes 16777240
  232.9 2.0 collective-permute-done.52.refs_0_.refs_1_
  235.4 1.6 collective-permute-start.55
  237.0 5.1 %collective-permute-done.53.refs_0_.refs_2_ = bf16[2,32,4352]{2,1,0:T(8,128)(2,1)S(1)} collective-permute-done((bf16[2,32,4352]{2,1,0:T(8,128)(2,1)S(1)}, bf16[2,32,4352]{2,1,0:T(8,128)(2,1)S(1)}, u32[]{:S(2)}, u32[]{:S(2)}) %collective-permute-start.53) | collective-permute-done | bytes 557088 | tf_op jit(solution)/shard_map/ppermute | solution.py:49
  242.2 11.1 %collective-permute-done.54.refs_1_.refs_3_ = bf16[2,32,4352]{2,1,0:T(8,128)(2,1)S(1)} collective-permute-done((bf16[2,32,4352]{2,1,0:T(8,128)(2,1)S(1)}, bf16[2,32,4352]{2,1,0:T(8,128)(2,1)S(1)}, u32[]{:S(2)}, u32[]{:S(2)}) %collective-permute-start.54) | collective-permute-done | bytes 557088 | tf_op jit(solution)/shard_map/ppermute | solution.py:49
  253.4 1.2 collective-permute-start.56
  254.6 1.3 collective-permute-start.51
  255.9 6.2 %collective-permute-done.56.refs_5_ = bf16[64,4352]{1,0:T(8,128)(2,1)S(1)} collective-permute-done((bf16[64,4352]{1,0:T(8,128)(2,1)S(1)}, bf16[64,4352]{1,0:T(8,128)(2,1)S(1)}, u32[]{:S(2)}, u32[]{:S(2)}) %collective-permute-start.56) | collective-permute-done | bytes 557088 | tf_op jit(solution)/shard_map/ppermute | solution.py:49
  262.5 113.2 %collective-permute-done.51.refs_0_ = bf16[32,8192]{1,0:T(8,128)(2,1)S(1)} collective-permute-done((bf16[32,8192]{1,0:T(8,128)(2,1)S(1)}, bf16[32,8192]{1,0:T(8,128)(2,1)S(1)}, u32[]{:S(2)}, u32[]{:S(2)}) %collective-permute-start.51) | collective-permute-done | bytes 524320 | tf_op jit(solution)/shard_map/ppermute | solution.py:49
  375.8 11.9 %shard_map.73 = (bf16[32,8192]{1,0:T(8,128)(2,1)}, bf16[2,2,32,4352]{3,2,1,0:T(8,128)(2,1)}, bf16[2,2,32,4352]{3,2,1,0:T(8,128)(2,1)}, bf16[256,4352]{1,0:T(8,128)(2,1)S(1)}) custom-call(bf16[32,8192]{1,0:T(8,128)(2,1)S(1)} %collective-permute-done.51.refs_0_, ...), custom_call_target="tpu_custom_call", output_to_operand_aliasing={{1}: (5, {}), {2}: (6, {}), {3}: (7, {})} | custom-call | flops 2000000000 | bytes 41943040 | tf_op jit(solution)/shard_map/pallas_call | solution.py:519
  387.7 1.6 collective-permute-start.57
  389.3 1.2 copy-done.6
  393.1 8.9 %collective-permute-done.58.refs_0_.refs_2_ = bf16[2,32,4352]{2,1,0:T(8,128)(2,1)S(1)} collective-permute-done((bf16[2,32,4352]{2,1,0:T(8,128)(2,1)S(1)}, bf16[2,32,4352]{2,1,0:T(8,128)(2,1)S(1)}, u32[]{:S(2)}, u32[]{:S(2)}) %collective-permute-start.58) | collective-permute-done | bytes 557088 | tf_op jit(solution)/shard_map/ppermute | solution.py:49
  402.0 9.3 %collective-permute-done.59.refs_1_.refs_3_ = bf16[2,32,4352]{2,1,0:T(8,128)(2,1)S(1)} collective-permute-done((bf16[2,32,4352]{2,1,0:T(8,128)(2,1)S(1)}, bf16[2,32,4352]{2,1,0:T(8,128)(2,1)S(1)}, u32[]{:S(2)}, u32[]{:S(2)}) %collective-permute-start.59) | collective-permute-done | bytes 557088 | tf_op jit(solution)/shard_map/ppermute | solution.py:49
  412.1 8.1 %collective-permute-done.61.refs_5_ = bf16[64,4352]{1,0:T(8,128)(2,1)S(1)} collective-permute-done((bf16[64,4352]{1,0:T(8,128)(2,1)S(1)}, bf16[64,4352]{1,0:T(8,128)(2,1)S(1)}, u32[]{:S(2)}, u32[]{:S(2)}) %collective-permute-start.61) | collective-permute-done | bytes 557088 | tf_op jit(solution)/shard_map/ppermute | solution.py:49
  422.1 2.5 pad_maximum_fusion
  424.6 49.4 %reduce-scatter.2.cloned.1.call-done = bf16[512,512]{0,1:T(8,128)(2,1)} async-done(((bf16[4096,512]{0,1:T(8,128)(2,1)}), bf16[512,512]{0,1:T(8,128)(2,1)}) %reduce-scatter.2.cloned.1.call-update) | async-done | bytes 524304 | tf_op jit(solution)/shard_map/reduce_scatter | solution.py:638
  (195 shorter events, 37.1 us)
Async XLA Ops:
  7.2 466.8 %reduce-scatter.2.cloned.1.call-start = ((), (), s32[]{:S(2)}) async-start(), calls=%async_computation.1 | async-start | bytes 4718592 | tf_op jit(solution)/shard_map/reduce_scatter | solution.py:638
  9.7 16.7 %collective-permute-start.5 = (bf16[608,256]{1,0:T(8,128)(2,1)S(1)}, bf16[608,256]{1,0:T(8,128)(2,1)}, u32[]{:S(2)}, u32[]{:S(2)}) collective-permute-start(bf16[608,256]{1,0:T(8,128)(2,1)S(1)} %get-tuple-element.84), channel_id=1, source_target_pairs={{0,14},{1,15},{2,0},{3,1},{4,2},{5,3},{6,4},{7,5},{8,6},{9,7},{10,... | collective-permute-start | bytes 933896 | tf_op jit(solution)/shard_map/ppermute | solution.py:49
  16.2 9.1 %collective-permute-start.4 = (bf16[608,256]{1,0:T(8,128)(2,1)S(1)}, bf16[608,256]{1,0:T(8,128)(2,1)S(1)}, u32[]{:S(2)}, u32[]{:S(2)}) collective-permute-start(bf16[608,256]{1,0:T(8,128)(2,1)S(1)} %get-tuple-element.84), channel_id=1, source_target_pairs={{0,2},{1,3},{2,4},{3,5},{4,6},{5,7},{6,8},{7,9},{8,10},{9,11},{10,... | collective-permute-start | bytes 933896 | tf_op jit(solution)/shard_map/ppermute | solution.py:49
  17.1 8.2 %collective-permute-start.27 = (bf16[208,512]{1,0:T(8,128)(2,1)S(1)}, bf16[208,512]{1,0:T(8,128)(2,1)}, u32[]{:S(2)}, u32[]{:S(2)}) collective-permute-start(bf16[208,512]{1,0:T(8,128)(2,1)S(1)} %get-tuple-element.88), channel_id=1, source_target_pairs={{0,1},{1,0},{2,3},{3,2},{4,5},{5,4},{6,7},{7,6},{8,9},{9,8},{10,11... | collective-permute-start | bytes 638984 | tf_op jit(solution)/shard_map/ppermute | solution.py:49
  18.5 14.1 %collective-permute-start.1 = (bf16[1,608,256]{2,1,0:T(8,128)(2,1)S(1)}, bf16[1,608,256]{2,1,0:T(8,128)(2,1)S(1)}, u32[]{:S(2)}, u32[]{:S(2)}) collective-permute-start(bf16[1,608,256]{2,1,0:T(8,128)(2,1)S(1)} %get-tuple-element.86), channel_id=1, source_target_pairs={{0,32},{1,33},{2,34},{3,35},{4,36},{5,37},{6,38},{7,39},{8,40},{9,... | collective-permute-start | bytes 933896 | tf_op jit(solution)/shard_map/ppermute | solution.py:49
  19.7 14.2 %collective-permute-start = (bf16[1,608,256]{2,1,0:T(8,128)(2,1)S(1)}, bf16[1,608,256]{2,1,0:T(8,128)(2,1)}, u32[]{:S(2)}, u32[]{:S(2)}) collective-permute-start(bf16[1,608,256]{2,1,0:T(8,128)(2,1)S(1)} %get-tuple-element.86), channel_id=1, source_target_pairs={{0,1},{1,0},{2,3},{3,2},{4,5},{5,4},{6,7},{7,6},{8,9},{9,8},{10,11... | collective-permute-start | bytes 933896 | tf_op jit(solution)/shard_map/ppermute | solution.py:49
  25.3 11.3 %collective-permute-start.10 = (bf16[608,256]{1,0:T(8,128)(2,1)S(1)}, bf16[608,256]{1,0:T(8,128)(2,1)}, u32[]{:S(2)}, u32[]{:S(2)}) collective-permute-start(bf16[608,256]{1,0:T(8,128)(2,1)S(1)} %collective-permute-done.4), channel_id=1, source_target_pairs={{0,2},{1,3},{2,4},{3,5},{4,6},{5,7},{6,8},{7,9},{8,10},{9,11},{10,... | collective-permute-start | bytes 933896 | tf_op jit(solution)/shard_map/ppermute | solution.py:49
  25.3 7.3 %collective-permute-start.28 = (bf16[208,512]{1,0:T(8,128)(2,1)S(1)}, bf16[208,512]{1,0:T(8,128)(2,1)S(1)}, u32[]{:S(2)}, u32[]{:S(2)}) collective-permute-start(bf16[208,512]{1,0:T(8,128)(2,1)S(1)} %get-tuple-element.88), channel_id=1, source_target_pairs={{0,32},{1,33},{2,34},{3,35},{4,36},{5,37},{6,38},{7,39},{8,40},{9,... | collective-permute-start | bytes 638984 | tf_op jit(solution)/shard_map/ppermute | solution.py:49
  26.5 12.8 %collective-permute-start.29 = (bf16[208,512]{1,0:T(8,128)(2,1)}, bf16[208,512]{1,0:T(8,128)(2,1)}, u32[]{:S(2)}, u32[]{:S(2)}) collective-permute-start(bf16[208,512]{1,0:T(8,128)(2,1)} %collective-permute-done.27), channel_id=1, source_target_pairs={{0,32},{1,33},{2,34},{3,35},{4,36},{5,37},{6,38},{7,39},{8,40},{9,... | collective-permute-start | bytes 638984 | tf_op jit(solution)/shard_map/ppermute | solution.py:49
  32.6 24.9 %collective-permute-start.6 = (bf16[2,608,256]{2,1,0:T(8,128)(2,1)}, bf16[2,608,256]{2,1,0:T(8,128)(2,1)}, u32[]{:S(2)}, u32[]{:S(2)}) collective-permute-start(bf16[2,608,256]{2,1,0:T(8,128)(2,1)} %get-tuple-element.83), channel_id=1, source_target_pairs={{0,1},{1,0},{2,3},{3,2},{4,5},{5,4},{6,7},{7,6},{8,9},{9,8},{10,11... | collective-permute-start | bytes 1867784 | tf_op jit(solution)/shard_map/ppermute | solution.py:49
  32.6 24.8 %collective-permute-start.7 = (bf16[2,608,256]{2,1,0:T(8,128)(2,1)}, bf16[2,608,256]{2,1,0:T(8,128)(2,1)}, u32[]{:S(2)}, u32[]{:S(2)}) collective-permute-start(bf16[2,608,256]{2,1,0:T(8,128)(2,1)} %get-tuple-element.83), channel_id=1, source_target_pairs={{0,32},{1,33},{2,34},{3,35},{4,36},{5,37},{6,38},{7,39},{8,40},{9,... | collective-permute-start | bytes 1867784 | tf_op jit(solution)/shard_map/ppermute | solution.py:49
  33.9 7.8 %collective-permute-start.11 = (bf16[608,256]{1,0:T(8,128)(2,1)}, bf16[608,256]{1,0:T(8,128)(2,1)}, u32[]{:S(2)}, u32[]{:S(2)}) collective-permute-start(bf16[608,256]{1,0:T(8,128)(2,1)} %collective-permute-done.5), channel_id=1, source_target_pairs={{0,14},{1,15},{2,0},{3,1},{4,2},{5,3},{6,4},{7,5},{8,6},{9,7},{10,... | collective-permute-start | bytes 933896 | tf_op jit(solution)/shard_map/ppermute | solution.py:49
  36.6 9.2 %collective-permute-start.16 = (bf16[608,256]{1,0:T(8,128)(2,1)}, bf16[608,256]{1,0:T(8,128)(2,1)}, u32[]{:S(2)}, u32[]{:S(2)}) collective-permute-start(bf16[608,256]{1,0:T(8,128)(2,1)} %collective-permute-done.10), channel_id=1, source_target_pairs={{0,2},{1,3},{2,4},{3,5},{4,6},{5,7},{6,8},{7,9},{8,10},{9,11},{10,... | collective-permute-start | bytes 933896 | tf_op jit(solution)/shard_map/ppermute | solution.py:49
  39.3 13.0 %collective-permute-start.2 = (bf16[1,608,256]{2,1,0:T(8,128)(2,1)}, bf16[1,608,256]{2,1,0:T(8,128)(2,1)}, u32[]{:S(2)}, u32[]{:S(2)}) collective-permute-start(bf16[1,608,256]{2,1,0:T(8,128)(2,1)} %collective-permute-done), channel_id=1, source_target_pairs={{0,32},{1,33},{2,34},{3,35},{4,36},{5,37},{6,38},{7,39},{8,40},{9,... | collective-permute-start | bytes 933896 | tf_op jit(solution)/shard_map/ppermute | solution.py:49
  41.6 13.0 %collective-permute-start.17 = (bf16[608,256]{1,0:T(8,128)(2,1)}, bf16[608,256]{1,0:T(8,128)(2,1)S(1)}, u32[]{:S(2)}, u32[]{:S(2)}) collective-permute-start(bf16[608,256]{1,0:T(8,128)(2,1)} %collective-permute-done.11), channel_id=1, source_target_pairs={{0,14},{1,15},{2,0},{3,1},{4,2},{5,3},{6,4},{7,5},{8,6},{9,7},{10,... | collective-permute-start | bytes 933896 | tf_op jit(solution)/shard_map/ppermute | solution.py:49
  45.8 12.4 %collective-permute-start.22 = (bf16[608,256]{1,0:T(8,128)(2,1)}, bf16[608,256]{1,0:T(8,128)(2,1)S(1)}, u32[]{:S(2)}, u32[]{:S(2)}) collective-permute-start(bf16[608,256]{1,0:T(8,128)(2,1)} %collective-permute-done.16), channel_id=1, source_target_pairs={{0,2},{1,3},{2,4},{3,5},{4,6},{5,7},{6,8},{7,9},{8,10},{9,11},{10,... | collective-permute-start | bytes 933896 | tf_op jit(solution)/shard_map/ppermute | solution.py:49
  52.3 9.5 %collective-permute-start.13 = (bf16[2,608,256]{2,1,0:T(8,128)(2,1)S(1)}, bf16[2,608,256]{2,1,0:T(8,128)(2,1)S(1)}, u32[]{:S(2)}, u32[]{:S(2)}) collective-permute-start(bf16[2,608,256]{2,1,0:T(8,128)(2,1)S(1)} %shard_map.59), channel_id=1, source_target_pairs={{0,32},{1,33},{2,34},{3,35},{4,36},{5,37},{6,38},{7,39},{8,40},{9,... | collective-permute-start | bytes 1867784 | tf_op jit(solution)/shard_map/ppermute | solution.py:49
  54.6 20.8 %collective-permute-start.33 = (bf16[4,208,512]{2,1,0:T(8,128)(2,1)S(1)}, bf16[4,208,512]{2,1,0:T(8,128)(2,1)S(1)}, u32[]{:S(2)}, u32[]{:S(2)}) collective-permute-start(bf16[4,208,512]{2,1,0:T(8,128)(2,1)S(1)} %pad_maximum_fusion.6.refs_11_), channel_id=1, source_target_pairs={{0,14},{1,15},{2,0},{3,1},{4,2},{5,3},{6,4},{7,5},{8,6},{9,7},{10,... | collective-permute-start | bytes 2555912 | tf_op jit(solution)/shard_map/ppermute | solution.py:49
  57.5 21.0 %collective-permute-start.31 = (bf16[4,208,512]{2,1,0:T(8,128)(2,1)S(1)}, bf16[4,208,512]{2,1,0:T(8,128)(2,1)S(1)}, u32[]{:S(2)}, u32[]{:S(2)}) collective-permute-start(bf16[4,208,512]{2,1,0:T(8,128)(2,1)S(1)} %pad_maximum_fusion.6.refs_11_), channel_id=1, source_target_pairs={{0,2},{1,3},{2,4},{3,5},{4,6},{5,7},{6,8},{7,9},{8,10},{9,11},{10,... | collective-permute-start | bytes 2555912 | tf_op jit(solution)/shard_map/ppermute | solution.py:49
  57.5 21.0 %collective-permute-start.30 = (bf16[4,208,512]{2,1,0:T(8,128)(2,1)S(1)}, bf16[4,208,512]{2,1,0:T(8,128)(2,1)S(1)}, u32[]{:S(2)}, u32[]{:S(2)}) collective-permute-start(bf16[4,208,512]{2,1,0:T(8,128)(2,1)S(1)} %pad_maximum_fusion.6.refs_11_), channel_id=1, source_target_pairs={{0,16},{1,17},{2,18},{3,19},{4,20},{5,21},{6,22},{7,23},{8,24},{9,... | collective-permute-start | bytes 2555912 | tf_op jit(solution)/shard_map/ppermute | solution.py:49
  58.2 10.9 %collective-permute-start.12 = (bf16[2,608,256]{2,1,0:T(8,128)(2,1)S(1)}, bf16[2,608,256]{2,1,0:T(8,128)(2,1)S(1)}, u32[]{:S(2)}, u32[]{:S(2)}) collective-permute-start(bf16[2,608,256]{2,1,0:T(8,128)(2,1)S(1)} %shard_map.59), channel_id=1, source_target_pairs={{0,1},{1,0},{2,3},{3,2},{4,5},{5,4},{6,7},{7,6},{8,9},{9,8},{10,11... | collective-permute-start | bytes 1867784 | tf_op jit(solution)/shard_map/ppermute | solution.py:49
  60.1 65.1 %copy-start.13 = (bf16[4,1,608,256]{3,2,1,0:T(8,128)(2,1)}, bf16[4,1,608,256]{3,2,1,0:T(8,128)(2,1)S(1)}, u32[]{:S(2)}) copy-start(bf16[4,1,608,256]{3,2,1,0:T(8,128)(2,1)S(1)} %pad_maximum_fusion.4.refs_1_) | copy-start | bytes 3735556
  61.7 44.8 %collective-permute-start.3 = (bf16[4,1,608,256]{3,2,1,0:T(8,128)(2,1)S(1)}, bf16[4,1,608,256]{3,2,1,0:T(8,128)(2,1)S(1)}, u32[]{:S(2)}, u32[]{:S(2)}) collective-permute-start(bf16[4,1,608,256]{3,2,1,0:T(8,128)(2,1)S(1)} %pad_maximum_fusion.4.refs_1_), channel_id=1, source_target_pairs={{0,16},{1,17},{2,18},{3,19},{4,20},{5,21},{6,22},{7,23},{8,24},{9,... | collective-permute-start | bytes 3735560 | tf_op jit(solution)/shard_map/ppermute | solution.py:49
  69.2 10.8 %collective-permute-start.24 = (bf16[1,608,256]{2,1,0:T(8,128)(2,1)S(1)}, bf16[1,608,256]{2,1,0:T(8,128)(2,1)S(1)}, u32[]{:S(2)}, u32[]{:S(2)}) collective-permute-start(bf16[1,608,256]{2,1,0:T(8,128)(2,1)S(1)} %bitcast.79), channel_id=1, source_target_pairs={{0,32},{1,33},{2,34},{3,35},{4,36},{5,37},{6,38},{7,39},{8,40},{9,... | collective-permute-start | bytes 933896 | tf_op jit(solution)/shard_map/ppermute | solution.py:49
  75.4 18.6 %collective-permute-start.18 = (bf16[2,608,256]{2,1,0:T(8,128)(2,1)S(1)}, bf16[2,608,256]{2,1,0:T(8,128)(2,1)S(1)}, u32[]{:S(2)}, u32[]{:S(2)}) collective-permute-start(bf16[2,608,256]{2,1,0:T(8,128)(2,1)S(1)} %get-tuple-element.81), channel_id=1, source_target_pairs={{0,1},{1,0},{2,3},{3,2},{4,5},{5,4},{6,7},{7,6},{8,9},{9,8},{10,11... | collective-permute-start | bytes 1867784 | tf_op jit(solution)/shard_map/ppermute | solution.py:49
  78.5 21.8 %collective-permute-start.19 = (bf16[2,608,256]{2,1,0:T(8,128)(2,1)S(1)}, bf16[2,608,256]{2,1,0:T(8,128)(2,1)S(1)}, u32[]{:S(2)}, u32[]{:S(2)}) collective-permute-start(bf16[2,608,256]{2,1,0:T(8,128)(2,1)S(1)} %get-tuple-element.81), channel_id=1, source_target_pairs={{0,32},{1,33},{2,34},{3,35},{4,36},{5,37},{6,38},{7,39},{8,40},{9,... | collective-permute-start | bytes 1867784 | tf_op jit(solution)/shard_map/ppermute | solution.py:49
  78.5 24.6 %collective-permute-start.8 = (bf16[2,608,256]{2,1,0:T(8,128)(2,1)}, bf16[2,608,256]{2,1,0:T(8,128)(2,1)S(1)}, u32[]{:S(2)}, u32[]{:S(2)}) collective-permute-start(bf16[2,608,256]{2,1,0:T(8,128)(2,1)} %collective-permute-done.6), channel_id=1, source_target_pairs={{0,32},{1,33},{2,34},{3,35},{4,36},{5,37},{6,38},{7,39},{8,40},{9,... | collective-permute-start | bytes 1867784 | tf_op jit(solution)/shard_map/ppermute | solution.py:49
  80.0 14.0 %collective-permute-start.23 = (bf16[1,608,256]{2,1,0:T(8,128)(2,1)S(1)}, bf16[1,608,256]{2,1,0:T(8,128)(2,1)S(1)}, u32[]{:S(2)}, u32[]{:S(2)}) collective-permute-start(bf16[1,608,256]{2,1,0:T(8,128)(2,1)S(1)} %bitcast.80), channel_id=1, source_target_pairs={{0,1},{1,0},{2,3},{3,2},{4,5},{5,4},{6,7},{7,6},{8,9},{9,8},{10,11... | collective-permute-start | bytes 933896 | tf_op jit(solution)/shard_map/ppermute | solution.py:49
  94.0 12.5 %collective-permute-start.25 = (bf16[1,608,256]{2,1,0:T(8,128)(2,1)S(1)}, bf16[1,608,256]{2,1,0:T(8,128)(2,1)S(1)}, u32[]{:S(2)}, u32[]{:S(2)}) collective-permute-start(bf16[1,608,256]{2,1,0:T(8,128)(2,1)S(1)} %collective-permute-done.23), channel_id=1, source_target_pairs={{0,32},{1,33},{2,34},{3,35},{4,36},{5,37},{6,38},{7,39},{8,40},{9,... | collective-permute-start | bytes 933896 | tf_op jit(solution)/shard_map/ppermute | solution.py:49
  94.0 19.8 %collective-permute-start.37 = (bf16[4,208,512]{2,1,0:T(8,128)(2,1)S(1)}, bf16[4,208,512]{2,1,0:T(8,128)(2,1)S(1)}, u32[]{:S(2)}, u32[]{:S(2)}) collective-permute-start(bf16[4,208,512]{2,1,0:T(8,128)(2,1)S(1)} %collective-permute-done.33.refs_15_), channel_id=1, source_target_pairs={{0,14},{1,15},{2,0},{3,1},{4,2},{5,3},{6,4},{7,5},{8,6},{9,7},{10,... | collective-permute-start | bytes 2555912 | tf_op jit(solution)/shard_map/ppermute | solution.py:49
  100.3 24.3 %collective-permute-start.35 = (bf16[4,208,512]{2,1,0:T(8,128)(2,1)S(1)}, bf16[4,208,512]{2,1,0:T(8,128)(2,1)S(1)}, u32[]{:S(2)}, u32[]{:S(2)}) collective-permute-start(bf16[4,208,512]{2,1,0:T(8,128)(2,1)S(1)} %collective-permute-done.31.refs_13_), channel_id=1, source_target_pairs={{0,2},{1,3},{2,4},{3,5},{4,6},{5,7},{6,8},{7,9},{8,10},{9,11},{10,... | collective-permute-start | bytes 2555912 | tf_op jit(solution)/shard_map/ppermute | solution.py:49
  103.1 21.5 %collective-permute-start.34 = (bf16[4,208,512]{2,1,0:T(8,128)(2,1)S(1)}, bf16[4,208,512]{2,1,0:T(8,128)(2,1)S(1)}, u32[]{:S(2)}, u32[]{:S(2)}) collective-permute-start(bf16[4,208,512]{2,1,0:T(8,128)(2,1)S(1)} %collective-permute-done.33.refs_15_), channel_id=1, source_target_pairs={{0,16},{1,17},{2,18},{3,19},{4,20},{5,21},{6,22},{7,23},{8,24},{9,... | collective-permute-start | bytes 2555912 | tf_op jit(solution)/shard_map/ppermute | solution.py:49
  106.5 18.7 %collective-permute-start.32 = (bf16[4,208,512]{2,1,0:T(8,128)(2,1)S(1)}, bf16[4,208,512]{2,1,0:T(8,128)(2,1)S(1)}, u32[]{:S(2)}, u32[]{:S(2)}) collective-permute-start(bf16[4,208,512]{2,1,0:T(8,128)(2,1)S(1)} %collective-permute-done.31.refs_13_), channel_id=1, source_target_pairs={{0,16},{1,17},{2,18},{3,19},{4,20},{5,21},{6,22},{7,23},{8,24},{9,... | collective-permute-start | bytes 2555912 | tf_op jit(solution)/shard_map/ppermute | solution.py:49
  106.5 10.7 %collective-permute-start.14 = (bf16[2,608,256]{2,1,0:T(8,128)(2,1)S(1)}, bf16[2,608,256]{2,1,0:T(8,128)(2,1)S(1)}, u32[]{:S(2)}, u32[]{:S(2)}) collective-permute-start(bf16[2,608,256]{2,1,0:T(8,128)(2,1)S(1)} %collective-permute-done.12), channel_id=1, source_target_pairs={{0,32},{1,33},{2,34},{3,35},{4,36},{5,37},{6,38},{7,39},{8,40},{9,... | collective-permute-start | bytes 1867784 | tf_op jit(solution)/shard_map/ppermute | solution.py:49
  113.8 21.6 %collective-permute-start.41 = (bf16[4,208,512]{2,1,0:T(8,128)(2,1)S(1)}, bf16[4,208,512]{2,1,0:T(8,128)(2,1)S(1)}, u32[]{:S(2)}, u32[]{:S(2)}) collective-permute-start(bf16[4,208,512]{2,1,0:T(8,128)(2,1)S(1)} %collective-permute-done.37.refs_19_), channel_id=1, source_target_pairs={{0,14},{1,15},{2,0},{3,1},{4,2},{5,3},{6,4},{7,5},{8,6},{9,7},{10,... | collective-permute-start | bytes 2555912 | tf_op jit(solution)/shard_map/ppermute | solution.py:49
  117.2 20.5 %collective-permute-start.38 = (bf16[4,208,512]{2,1,0:T(8,128)(2,1)S(1)}, bf16[4,208,512]{2,1,0:T(8,128)(2,1)S(1)}, u32[]{:S(2)}, u32[]{:S(2)}) collective-permute-start(bf16[4,208,512]{2,1,0:T(8,128)(2,1)S(1)} %collective-permute-done.37.refs_19_), channel_id=1, source_target_pairs={{0,16},{1,17},{2,18},{3,19},{4,20},{5,21},{6,22},{7,23},{8,24},{9,... | collective-permute-start | bytes 2555912 | tf_op jit(solution)/shard_map/ppermute | solution.py:49
  124.6 21.7 %collective-permute-start.39 = (bf16[4,208,512]{2,1,0:T(8,128)(2,1)S(1)}, bf16[4,208,512]{2,1,0:T(8,128)(2,1)S(1)}, u32[]{:S(2)}, u32[]{:S(2)}) collective-permute-start(bf16[4,208,512]{2,1,0:T(8,128)(2,1)S(1)} %collective-permute-done.35.refs_17_), channel_id=1, source_target_pairs={{0,2},{1,3},{2,4},{3,5},{4,6},{5,7},{6,8},{7,9},{8,10},{9,11},{10,... | collective-permute-start | bytes 2555912 | tf_op jit(solution)/shard_map/ppermute | solution.py:49
  124.6 9.5 %collective-permute-start.20 = (bf16[2,608,256]{2,1,0:T(8,128)(2,1)S(1)}, bf16[2,608,256]{2,1,0:T(8,128)(2,1)S(1)}, u32[]{:S(2)}, u32[]{:S(2)}) collective-permute-start(bf16[2,608,256]{2,1,0:T(8,128)(2,1)S(1)} %collective-permute-done.18), channel_id=1, source_target_pairs={{0,32},{1,33},{2,34},{3,35},{4,36},{5,37},{6,38},{7,39},{8,40},{9,... | collective-permute-start | bytes 1867784 | tf_op jit(solution)/shard_map/ppermute | solution.py:49
  125.2 22.1 %collective-permute-start.26 = (bf16[4,1,608,256]{3,2,1,0:T(8,128)(2,1)S(1)}, bf16[4,1,608,256]{3,2,1,0:T(8,128)(2,1)S(1)}, u32[]{:S(2)}, u32[]{:S(2)}) collective-permute-start(bf16[4,1,608,256]{3,2,1,0:T(8,128)(2,1)S(1)} %pad_maximum_fusion.5.refs_9_), channel_id=1, source_target_pairs={{0,16},{1,17},{2,18},{3,19},{4,20},{5,21},{6,22},{7,23},{8,24},{9,... | collective-permute-start | bytes 3735560 | tf_op jit(solution)/shard_map/ppermute | solution.py:49
  134.1 13.1 %collective-permute-start.36 = (bf16[4,208,512]{2,1,0:T(8,128)(2,1)S(1)}, bf16[4,208,512]{2,1,0:T(8,128)(2,1)S(1)}, u32[]{:S(2)}, u32[]{:S(2)}) collective-permute-start(bf16[4,208,512]{2,1,0:T(8,128)(2,1)S(1)} %collective-permute-done.35.refs_17_), channel_id=1, source_target_pairs={{0,16},{1,17},{2,18},{3,19},{4,20},{5,21},{6,22},{7,23},{8,24},{9,... | collective-permute-start | bytes 2555912 | tf_op jit(solution)/shard_map/ppermute | solution.py:49
  135.4 34.5 %collective-permute-start.9 = (bf16[4,2,608,256]{3,2,1,0:T(8,128)(2,1)S(1)}, bf16[4,2,608,256]{3,2,1,0:T(8,128)(2,1)S(1)}, u32[]{:S(2)}, u32[]{:S(2)}) collective-permute-start(bf16[4,2,608,256]{3,2,1,0:T(8,128)(2,1)S(1)} %pad_maximum_fusion.1.refs_3_), channel_id=1, source_target_pairs={{0,16},{1,17},{2,18},{3,19},{4,20},{5,21},{6,22},{7,23},{8,24},{9,... | collective-permute-start | bytes 7471112 | tf_op jit(solution)/shard_map/ppermute | solution.py:49
  137.7 32.2 %collective-permute-start.15 = (bf16[4,2,608,256]{3,2,1,0:T(8,128)(2,1)S(1)}, bf16[4,2,608,256]{3,2,1,0:T(8,128)(2,1)S(1)}, u32[]{:S(2)}, u32[]{:S(2)}) collective-permute-start(bf16[4,2,608,256]{3,2,1,0:T(8,128)(2,1)S(1)} %pad_maximum_fusion.2.refs_5_), channel_id=1, source_target_pairs={{0,16},{1,17},{2,18},{3,19},{4,20},{5,21},{6,22},{7,23},{8,24},{9,... | collective-permute-start | bytes 7471112 | tf_op jit(solution)/shard_map/ppermute | solution.py:49
  146.3 23.6 %collective-permute-start.21 = (bf16[4,2,608,256]{3,2,1,0:T(8,128)(2,1)S(1)}, bf16[4,2,608,256]{3,2,1,0:T(8,128)(2,1)S(1)}, u32[]{:S(2)}, u32[]{:S(2)}) collective-permute-start(bf16[4,2,608,256]{3,2,1,0:T(8,128)(2,1)S(1)} %pad_maximum_fusion.3.refs_7_), channel_id=1, source_target_pairs={{0,16},{1,17},{2,18},{3,19},{4,20},{5,21},{6,22},{7,23},{8,24},{9,... | collective-permute-start | bytes 7471112 | tf_op jit(solution)/shard_map/ppermute | solution.py:49
  147.2 5.6 %collective-permute-start.42 = (bf16[4,208,512]{2,1,0:T(8,128)(2,1)S(1)}, bf16[4,208,512]{2,1,0:T(8,128)(2,1)S(1)}, u32[]{:S(2)}, u32[]{:S(2)}) collective-permute-start(bf16[4,208,512]{2,1,0:T(8,128)(2,1)S(1)} %collective-permute-done.41.refs_23_), channel_id=1, source_target_pairs={{0,16},{1,17},{2,18},{3,19},{4,20},{5,21},{6,22},{7,23},{8,24},{9,... | collective-permute-start | bytes 2555912 | tf_op jit(solution)/shard_map/ppermute | solution.py:49
  147.3 21.3 %collective-permute-start.43 = (bf16[4,208,512]{2,1,0:T(8,128)(2,1)S(1)}, bf16[4,208,512]{2,1,0:T(8,128)(2,1)S(1)}, u32[]{:S(2)}, u32[]{:S(2)}) collective-permute-start(bf16[4,208,512]{2,1,0:T(8,128)(2,1)S(1)} %collective-permute-done.39.refs_21_), channel_id=1, source_target_pairs={{0,2},{1,3},{2,4},{3,5},{4,6},{5,7},{6,8},{7,9},{8,10},{9,11},{10,... | collective-permute-start | bytes 2555912 | tf_op jit(solution)/shard_map/ppermute | solution.py:49
  152.8 17.1 %collective-permute-start.40 = (bf16[4,208,512]{2,1,0:T(8,128)(2,1)S(1)}, bf16[4,208,512]{2,1,0:T(8,128)(2,1)S(1)}, u32[]{:S(2)}, u32[]{:S(2)}) collective-permute-start(bf16[4,208,512]{2,1,0:T(8,128)(2,1)S(1)} %collective-permute-done.39.refs_21_), channel_id=1, source_target_pairs={{0,16},{1,17},{2,18},{3,19},{4,20},{5,21},{6,22},{7,23},{8,24},{9,... | collective-permute-start | bytes 2555912 | tf_op jit(solution)/shard_map/ppermute | solution.py:49
  168.6 5.2 %collective-permute-start.44 = (bf16[4,208,512]{2,1,0:T(8,128)(2,1)S(1)}, bf16[4,208,512]{2,1,0:T(8,128)(2,1)}, u32[]{:S(2)}, u32[]{:S(2)}) collective-permute-start(bf16[4,208,512]{2,1,0:T(8,128)(2,1)S(1)} %collective-permute-done.43.refs_25_), channel_id=1, source_target_pairs={{0,16},{1,17},{2,18},{3,19},{4,20},{5,21},{6,22},{7,23},{8,24},{9,... | collective-permute-start | bytes 2555912 | tf_op jit(solution)/shard_map/ppermute | solution.py:49
  200.5 13.1 %collective-permute-start.46 = (bf16[32,8192]{1,0:T(8,128)(2,1)}, bf16[32,8192]{1,0:T(8,128)(2,1)S(1)}, u32[]{:S(2)}, u32[]{:S(2)}) collective-permute-start(bf16[32,8192]{1,0:T(8,128)(2,1)} %get-tuple-element.38), channel_id=1, source_target_pairs={{0,96},{1,97},{2,98},{3,99},{4,100},{5,101},{6,102},{7,103},{8,104... | collective-permute-start | bytes 1572872 | tf_op jit(solution)/shard_map/ppermute | solution.py:49
  225.2 0.7 collective-permute-start.47
  226.3 1.4 collective-permute-start.48
  227.0 1.7 collective-permute-start.45
  228.9 0.7 collective-permute-start.49
  229.8 0.8 collective-permute-start.50
  231.4 3.5 collective-permute-start.52
  232.6 9.6 %collective-permute-start.53 = (bf16[2,32,4352]{2,1,0:T(8,128)(2,1)S(1)}, bf16[2,32,4352]{2,1,0:T(8,128)(2,1)S(1)}, u32[]{:S(2)}, u32[]{:S(2)}) collective-permute-start(bf16[2,32,4352]{2,1,0:T(8,128)(2,1)S(1)} %shard_map.68), channel_id=1, source_target_pairs={{0,1},{1,0},{2,3},{3,2},{4,5},{5,4},{6,7},{7,6},{8,9},{9,8},{10,11... | collective-permute-start | bytes 1671176 | tf_op jit(solution)/shard_map/ppermute | solution.py:49
  235.0 18.3 %collective-permute-start.54 = (bf16[2,32,4352]{2,1,0:T(8,128)(2,1)S(1)}, bf16[2,32,4352]{2,1,0:T(8,128)(2,1)S(1)}, u32[]{:S(2)}, u32[]{:S(2)}) collective-permute-start(bf16[2,32,4352]{2,1,0:T(8,128)(2,1)S(1)} %shard_map.69), channel_id=1, source_target_pairs={{0,1},{1,0},{2,3},{3,2},{4,5},{5,4},{6,7},{7,6},{8,9},{9,8},{10,11... | collective-permute-start | bytes 1671176 | tf_op jit(solution)/shard_map/ppermute | solution.py:49
  235.4 20.5 %collective-permute-start.55 = (bf16[64,4352]{1,0:T(8,128)(2,1)S(1)}, bf16[64,4352]{1,0:T(8,128)(2,1)S(1)}, u32[]{:S(2)}, u32[]{:S(2)}) collective-permute-start(bf16[64,4352]{1,0:T(8,128)(2,1)S(1)} %shard_map.70), channel_id=1, source_target_pairs={{0,32},{1,33},{2,34},{3,35},{4,36},{5,37},{6,38},{7,39},{8,40},{9,... | collective-permute-start | bytes 1671176 | tf_op jit(solution)/shard_map/ppermute | solution.py:49
  253.4 8.8 %collective-permute-start.56 = (bf16[64,4352]{1,0:T(8,128)(2,1)S(1)}, bf16[64,4352]{1,0:T(8,128)(2,1)S(1)}, u32[]{:S(2)}, u32[]{:S(2)}) collective-permute-start(bf16[64,4352]{1,0:T(8,128)(2,1)S(1)} %shard_map.71), channel_id=1, source_target_pairs={{0,32},{1,33},{2,34},{3,35},{4,36},{5,37},{6,38},{7,39},{8,40},{9,... | collective-permute-start | bytes 1671176 | tf_op jit(solution)/shard_map/ppermute | solution.py:49
  254.6 121.2 %collective-permute-start.51 = (bf16[32,8192]{1,0:T(8,128)(2,1)S(1)}, bf16[32,8192]{1,0:T(8,128)(2,1)S(1)}, u32[]{:S(2)}, u32[]{:S(2)}) collective-permute-start(bf16[32,8192]{1,0:T(8,128)(2,1)S(1)} %get-tuple-element.64), channel_id=1, source_target_pairs={{64,32},{65,33},{66,34},{67,35},{68,36},{69,37},{70,38},{71,39},{7... | collective-permute-start | bytes 1572872 | tf_op jit(solution)/shard_map/ppermute | solution.py:49
  387.7 4.1 collective-permute-start.57
  390.6 11.4 %collective-permute-start.58 = (bf16[2,32,4352]{2,1,0:T(8,128)(2,1)S(1)}, bf16[2,32,4352]{2,1,0:T(8,128)(2,1)S(1)}, u32[]{:S(2)}, u32[]{:S(2)}) collective-permute-start(bf16[2,32,4352]{2,1,0:T(8,128)(2,1)S(1)} %shard_map.74), channel_id=1, source_target_pairs={{0,1},{1,0},{2,3},{3,2},{4,5},{5,4},{6,7},{7,6},{8,9},{9,8},{10,11... | collective-permute-start | bytes 1671176 | tf_op jit(solution)/shard_map/ppermute | solution.py:49
  391.9 19.4 %collective-permute-start.59 = (bf16[2,32,4352]{2,1,0:T(8,128)(2,1)S(1)}, bf16[2,32,4352]{2,1,0:T(8,128)(2,1)S(1)}, u32[]{:S(2)}, u32[]{:S(2)}) collective-permute-start(bf16[2,32,4352]{2,1,0:T(8,128)(2,1)S(1)} %shard_map.75), channel_id=1, source_target_pairs={{0,1},{1,0},{2,3},{3,2},{4,5},{5,4},{6,7},{7,6},{8,9},{9,8},{10,11... | collective-permute-start | bytes 1671176 | tf_op jit(solution)/shard_map/ppermute | solution.py:49
  392.4 19.7 %collective-permute-start.60 = (bf16[64,4352]{1,0:T(8,128)(2,1)S(1)}, bf16[64,4352]{1,0:T(8,128)(2,1)S(1)}, u32[]{:S(2)}, u32[]{:S(2)}) collective-permute-start(bf16[64,4352]{1,0:T(8,128)(2,1)S(1)} %shard_map.76), channel_id=1, source_target_pairs={{0,32},{1,33},{2,34},{3,35},{4,36},{5,37},{6,38},{7,39},{8,40},{9,... | collective-permute-start | bytes 1671176 | tf_op jit(solution)/shard_map/ppermute | solution.py:49
  411.4 8.8 %collective-permute-start.61 = (bf16[64,4352]{1,0:T(8,128)(2,1)S(1)}, bf16[64,4352]{1,0:T(8,128)(2,1)S(1)}, u32[]{:S(2)}, u32[]{:S(2)}) collective-permute-start(bf16[64,4352]{1,0:T(8,128)(2,1)S(1)} %shard_map.77), channel_id=1, source_target_pairs={{0,32},{1,33},{2,34},{3,35},{4,36},{5,37},{6,38},{7,39},{8,40},{9,... | collective-permute-start | bytes 1671176 | tf_op jit(solution)/shard_map/ppermute | solution.py:49
  (41 other events, 563.6 us)
Sparse Core Ops, SparseCore 0:
  424.7 49.2 reduce-scatter.1
